TPU v7x, 32 devices: a whole 2x2x4 slice. The times are simulated.
32 devices in a mesh: dp: 8 (over y, x, core), mp: 4 (over z).
Axes of the slice: x: 2, y: 2, z: 4, core: 2. Of those that a mesh axis runs over, the one named last changes fastest.
Arguments:
- word_inputs: bfloat16 [8, 1024, 512], P('dp'), may hold values from -6 to 6
- character_embeddings: bfloat16 [160, 128, 16, 256], P('dp', 'mp'), may hold values from -6 to 6
- cotangent: bfloat16 [8, 1024, 512], P('dp'), may hold values from -6 to 6
- char_count: int32 [160, 128], P('dp', 'mp'), may hold values from 1 to 16, as said below
- word_place: int32 [160, 128], P('dp'), may hold values from -1 to 1023, as said below
- block_home: int32 [160], P('dp'), may hold values from -1 to 7, as said below
- documents: int32 [8, 1024], P('dp'), may hold values from 0 to 5, never falling along the last dimension, each value on 1 to 512 neighbouring positions
- char_gain: float32 [256], replicated, may hold values from 0.5 to 1.5
- word_gains: float32 [2, 512], replicated, may hold values from 0.5 to 1.5
- char_mixer: float32 [4, 256, 256], P(None, 'dp'), may hold values from -0.375 to 0.375
- char_mixer_left: float32 [4, 256, 256], P(None, 'dp'), as said below
- char_mixer_right: float32 [4, 256, 256], P(None, 'dp'), as said below
- char_mixer_left_root: float32 [4, 256, 256], P(None, 'dp'), as said below
- char_mixer_right_root: float32 [4, 256, 256], P(None, 'dp'), as said below
- char_lift: float32 [1, 256, 512], P(None, 'dp'), may hold values from -0.375 to 0.375
- char_lift_left: float32 [1, 256, 256], P(None, 'dp'), as said below
- char_lift_right: float32 [1, 512, 512], P(None, 'dp'), as said below
- char_lift_left_root: float32 [1, 256, 256], P(None, 'dp'), as said below
- char_lift_right_root: float32 [1, 512, 512], P(None, 'dp'), as said below
- word_project: float32 [3, 4, 512, 128], P(None, 'mp', 'dp'), may hold values from -0.25 to 0.25
- word_project_left: float32 [3, 4, 512, 512], P(None, 'mp', 'dp'), as said below
- word_project_right: float32 [3, 4, 128, 128], P(None, 'mp', 'dp'), as said below
- word_project_left_root: float32 [3, 4, 512, 512], P(None, 'mp', 'dp'), as said below
- word_project_right_root: float32 [3, 4, 128, 128], P(None, 'mp', 'dp'), as said below
- word_output: float32 [4, 128, 512], P('mp', 'dp'), may hold values from -1 to 1
- word_output_left: float32 [4, 128, 128], P('mp', 'dp'), as said below
- word_output_right: float32 [4, 512, 512], P('mp', 'dp'), as said below
- word_output_left_root: float32 [4, 128, 128], P('mp', 'dp'), as said below
- word_output_right_root: float32 [4, 512, 512], P('mp', 'dp'), as said below
- feed_upper: float32 [4, 512, 512], P('mp', 'dp'), may hold values from -0.25 to 0.25
- feed_upper_left: float32 [4, 512, 512], P('mp', 'dp'), as said below
- feed_upper_right: float32 [4, 512, 512], P('mp', 'dp'), as said below
- feed_upper_left_root: float32 [4, 512, 512], P('mp', 'dp'), as said below
- feed_upper_right_root: float32 [4, 512, 512], P('mp', 'dp'), as said below
- feed_lower: float32 [4, 512, 512], P('mp', 'dp'), may hold values from -0.125 to 0.125
- feed_lower_left: float32 [4, 512, 512], P('mp', 'dp'), as said below
- feed_lower_right: float32 [4, 512, 512], P('mp', 'dp'), as said below
- feed_lower_left_root: float32 [4, 512, 512], P('mp', 'dp'), as said below
- feed_lower_right_root: float32 [4, 512, 512], P('mp', 'dp'), as said below
Outputs:
- block_out: bfloat16 [8, 1024, 512], P('dp')
- word_inputs_gradient: bfloat16 [8, 1024, 512], P('dp')
- char_embeds_gradient: bfloat16 [160, 128, 16, 256], P('dp', 'mp')
- char_gain_gradient: float32 [256], replicated
- word_gains_gradient: float32 [2, 512], replicated
- char_gain_new: float32 [256], replicated
- word_gains_new: float32 [2, 512], replicated
- global_norm: float32 [], replicated
- char_mixer_gradient: float32 [4, 256, 256], P(None, 'dp')
- char_mixer_left_new: float32 [4, 256, 256], P(None, 'dp')
- char_mixer_right_new: float32 [4, 256, 256], P(None, 'dp')
- char_mixer_new: float32 [4, 256, 256], P(None, 'dp')
- char_mixer_copy: bfloat16 [4, 256, 256], P(None, 'dp')
- char_lift_gradient: float32 [1, 256, 512], P(None, 'dp')
- char_lift_left_new: float32 [1, 256, 256], P(None, 'dp')
- char_lift_right_new: float32 [1, 512, 512], P(None, 'dp')
- char_lift_new: float32 [1, 256, 512], P(None, 'dp')
- char_lift_copy: bfloat16 [1, 256, 512], P(None, 'dp')
- word_project_gradient: float32 [3, 4, 512, 128], P(None, 'mp', 'dp')
- word_project_left_new: float32 [3, 4, 512, 512], P(None, 'mp', 'dp')
- word_project_right_new: float32 [3, 4, 128, 128], P(None, 'mp', 'dp')
- word_project_new: float32 [3, 4, 512, 128], P(None, 'mp', 'dp')
- word_project_copy: bfloat16 [3, 4, 512, 128], P(None, 'mp', 'dp')
- word_output_gradient: float32 [4, 128, 512], P('mp', 'dp')
- word_output_left_new: float32 [4, 128, 128], P('mp', 'dp')
- word_output_right_new: float32 [4, 512, 512], P('mp', 'dp')
- word_output_new: float32 [4, 128, 512], P('mp', 'dp')
- word_output_copy: bfloat16 [4, 128, 512], P('mp', 'dp')
- feed_upper_gradient: float32 [4, 512, 512], P('mp', 'dp')
- feed_upper_left_new: float32 [4, 512, 512], P('mp', 'dp')
- feed_upper_right_new: float32 [4, 512, 512], P('mp', 'dp')
- feed_upper_new: float32 [4, 512, 512], P('mp', 'dp')
- feed_upper_copy: bfloat16 [4, 512, 512], P('mp', 'dp')
- feed_lower_gradient: float32 [4, 512, 512], P('mp', 'dp')
- feed_lower_left_new: float32 [4, 512, 512], P('mp', 'dp')
- feed_lower_right_new: float32 [4, 512, 512], P('mp', 'dp')
- feed_lower_new: float32 [4, 512, 512], P('mp', 'dp')
- feed_lower_copy: bfloat16 [4, 512, 512], P('mp', 'dp')
Inputs may be any that keep to these rules, and one draw needn't show every extreme that they name: Slots s of index i of dp are i * 20 to (i + 1) * 20 - 1; block_home names the owner of the block in a slot, -1 an empty slot; the live slots of an index come first. Each owner has exactly 10 blocks in all; no index holds more than 3 blocks of one owner, and some index does; some index has all 20 slots live. word_place is -1 on empty places and empty slots; over the slots of one owner each of its 1024 places appears exactly once. `char_count`: within one block all counts lie in one range (k - 1) * 4 + 1 to k * 4 for some k of 1 to 4. `char_mixer_left`: statistics of the previous step. `char_mixer_right`: statistics of the previous step. `char_mixer_left_root`: inverse roots of earlier statistics. `char_mixer_right_root`: inverse roots of earlier statistics. `char_lift_left`: statistics of the previous step. `char_lift_right`: statistics of the previous step. `char_lift_left_root`: inverse roots of earlier statistics. `char_lift_right_root`: inverse roots of earlier statistics. `word_project_left`: statistics of the previous step. `word_project_right`: statistics of the previous step. `word_project_left_root`: inverse roots of earlier statistics. `word_project_right_root`: inverse roots of earlier statistics. `word_output_left`: statistics of the previous step. `word_output_right`: statistics of the previous step. `word_output_left_root`: inverse roots of earlier statistics. `word_output_right_root`: inverse roots of earlier statistics. `feed_upper_left`: statistics of the previous step. `feed_upper_right`: statistics of the previous step. `feed_upper_left_root`: inverse roots of earlier statistics. `feed_upper_right_root`: inverse roots of earlier statistics. `feed_lower_left`: statistics of the previous step. `feed_lower_right`: statistics of the previous step. `feed_lower_left_root`: inverse roots of earlier statistics. `feed_lower_right_root`: inverse roots of earlier statistics.
All inputs are finite; a program needn't handle non-finite values.
Results may differ from a plain program's by a relative error of at most 0.024.
Values may be sent and summed in bfloat16 or wider, within the bound.
A program may use at most 256 MiB of HBM per device.

v0:
```python
import functools
import math

import jax
import jax.numpy as jnp
from jax import lax
from jax.experimental import pallas as pl
from jax.experimental.pallas import tpu as pltpu
from jax.sharding import PartitionSpec as P

D = 512
HD = 64
FF = 2048
CHAR_BLOCK_WIDTH = 256
OWNER_BLOCKS = 10
decay_rate = 0.5
learn_rate = 1.0
gain_rate = 0.4
negative_big = -1e30

CW = 256
CHEADS = 4
CHD = 64
SPOTS = 16
KEPT = 3 * CW + CHEADS * 128 + CW
epsilon = 1e-05
BF = jnp.bfloat16
F32 = jnp.float32


def nn(a, b):
    return lax.dot_general(a, b, (((1,), (0,)), ((), ())), preferred_element_type=F32)


def nt(a, b):
    return lax.dot_general(a, b, (((1,), (1,)), ((), ())), preferred_element_type=F32)


def tn(a, b):
    return lax.dot_general(a, b, (((0,), (0,)), ((), ())), preferred_element_type=F32)


def char_classes(share):
    listed = [(1, 4, 32), (2, 8, 16), (4, 16, 8)]
    return [c for c in listed if c[2] <= share]


def order_matrix(places, words):
    row = lax.broadcasted_iota(jnp.int32, (128, SPOTS * words), 0)
    col = lax.broadcasted_iota(jnp.int32, (128, SPOTS * words), 1)
    return ((row % words) * SPOTS + row // words == col).astype(BF)


def head_stack(rows, scale):
    lane = lax.broadcasted_iota(jnp.int32, (1, CW), 1) // CHD
    return jnp.concatenate(
        [rows * jnp.where(lane == h, scale, 0.0).astype(BF) for h in range(CHEADS)], axis=0
    )


def char_forward_kernel(
    classes, kind, x_ref, count_ref, gain_ref, mats_ref, *refs
):
    orders = refs[: len(classes)]
    vec_ref, kept_ref, pooled_ref, msum_ref, sumx, counts = refs[len(classes) :]
    step = pl.program_id(0)
    share = count_ref.shape[1]
    own = pl.ds(pl.multiple_of(step * share, share), share)
    counts[own, :] = count_ref[0]

    @pl.when(kind[step] == 0)
    def _():
        sumx[own, :] = jnp.zeros((share, CW), F32)
        msum_ref[own, :] = jnp.zeros((share, CW), F32)

    def block(places, words, order_ref):
        groups = share // words
        kept_x = []
        normed = []
        for g in range(groups):
            x = nn(order_ref[...], x_ref[0, pl.ds(g * words * SPOTS, words * SPOTS), :])
            scale = lax.rsqrt(jnp.mean(x * x, axis=-1, keepdims=True) + epsilon)
            normed.append((x * scale * gain_ref[...]).astype(BF))
            cnt = count_ref[0, pl.ds(g * words, words), :]
            cnt2 = jnp.concatenate([cnt, cnt], axis=1)
            place = lax.broadcasted_iota(jnp.int32, (places, words, CW), 0).astype(F32)
            x3 = x.reshape(places, words, CW)
            sumx[pl.ds(pl.multiple_of(step * share + g * words, words), words), :] = jnp.sum(
                jnp.where(place < cnt2[None], x3, 0.0), axis=0
            )
        rows = groups * 128
        normed = jnp.concatenate(normed, axis=0) if groups > 1 else normed[0]
        for t in range(3):
            kept_ref[0, :rows, t * CW : (t + 1) * CW] = nn(
                normed, mats_ref[:, t * CW : (t + 1) * CW]
            ).astype(BF)
        lane = lax.broadcasted_iota(jnp.int32, (words, CHEADS * 128), 1) % 128
        word = lax.broadcasted_iota(jnp.int32, (words, CHEADS * 128), 0)
        mine = lane % words == word
        spot = (lane // words).astype(F32)
        head_row = lax.broadcasted_iota(jnp.int32, (CHEADS * 128, CW), 0) // 128
        head_col = lax.broadcasted_iota(jnp.int32, (CHEADS * 128, CW), 1) // CHD
        same_head = (head_row == head_col).astype(BF)
        for g in range(groups):
            at = g * 128
            q = kept_ref[0, at : at + 128, :CW]
            k = kept_ref[0, at : at + 128, CW : 2 * CW]
            v = kept_ref[0, at : at + 128, 2 * CW : 3 * CW]
            s = nt(k, head_stack(q, 1.0 / math.sqrt(CHD))).reshape(places, words, CHEADS * 128)
            cnt = count_ref[0, pl.ds(g * words, words), :]
            cnt4 = jnp.concatenate([cnt] * CHEADS, axis=1)
            place = lax.broadcasted_iota(jnp.int32, (places, words, CHEADS * 128), 0).astype(F32)
            s = jnp.where(place < cnt4[None], s, -1e30)
            e = jnp.exp(s - jnp.max(s, axis=0)[None])
            r = jnp.where(mine & (spot < cnt4), 1.0 / jnp.sum(e, axis=0), 0.0)
            p = (e * r[None]).astype(BF).reshape(128, CHEADS * 128)
            kept_ref[0, at : at + 128, 3 * CW : 3 * CW + CHEADS * 128] = p
            c = nn(p, same_head)
            kept_ref[0, at : at + 128, 3 * CW + CHEADS * 128 :] = c.astype(BF)
            msum_ref[pl.ds(pl.multiple_of(step * share + g * words, words), words), :] = jnp.sum(
                (c * v.astype(F32)).reshape(places, words, CW), axis=0
            )

    for (number, places, words), order_ref in zip(classes, orders):
        pl.when(kind[step] == number)(functools.partial(block, places, words, order_ref))

    @pl.when(step == pl.num_programs(0) - 1)
    def _():
        cnt2 = jnp.concatenate([counts[...]] * 2, axis=1)
        summed = sumx[...] + nn(msum_ref[...].astype(BF), mats_ref[:, 3 * CW : 4 * CW])
        pooled = (summed / cnt2).astype(BF)
        pooled_ref[...] = pooled
        vec_ref[...] = nn(pooled, mats_ref[:, 4 * CW :]).astype(BF)


def char_kind(block_home, char_count, share):
    places = jnp.max(char_count, axis=1)
    kind = jnp.where(places <= 8, 2, 4)
    if share >= 32:
        kind = jnp.where(places <= 4, 1, kind)
    return jnp.where(block_home >= 0, kind, 0).astype(jnp.int32)


def whole(shape):
    return pl.BlockSpec(shape, lambda i, *_: (0,) * len(shape))


def char_forward(x, kind, counts, gain, mats):
    slots, share = x.shape[:2]
    classes = char_classes(share)
    rows = share * SPOTS
    orders = [order_matrix(p, w) for _, p, w in classes]
    words_all = slots * share
    per_slot = lambda shape: pl.BlockSpec((1,) + shape, lambda i, *_: (i,) + (0,) * len(shape))
    return pl.pallas_call(
        functools.partial(char_forward_kernel, classes),
        grid_spec=pltpu.PrefetchScalarGridSpec(
            num_scalar_prefetch=1,
            grid=(slots,),
            in_specs=[
                per_slot((rows, CW)),
                per_slot((share, 128)),
                whole((1, CW)),
                whole(mats.shape),
            ]
            + [whole(o.shape) for o in orders],
            out_specs=[
                whole((words_all, D)),
                per_slot((rows, KEPT)),
                whole((words_all, CW)),
                whole((words_all, CW)),
            ],
            scratch_shapes=[
                pltpu.VMEM((words_all, CW), F32),
                pltpu.VMEM((words_all, 128), F32),
            ],
        ),
        out_shape=[
            jax.ShapeDtypeStruct((words_all, D), BF),
            jax.ShapeDtypeStruct((slots, rows, KEPT), BF),
            jax.ShapeDtypeStruct((words_all, CW), BF),
            jax.ShapeDtypeStruct((words_all, CW), F32),
        ],
        compiler_params=pltpu.CompilerParams(vmem_limit_bytes=60 << 20),
        cost_estimate=pl.CostEstimate(
            flops=slots * rows * CW * CW * 16, bytes_accessed=slots * rows * KEPT * 3, transcendentals=0
        ),
        name="char_forward",
    )(kind, x.reshape(slots, rows, CW), counts, gain.reshape(1, CW), mats, *orders)


def char_backward_kernel(
    classes, kind, x_ref, count_ref, kept_ref, all_counts_ref, gv_ref, pooled_ref, msum_ref,
    gain_ref, mats_ref, *refs
):
    orders = refs[: len(classes)]
    dx_ref, grads_ref, dgain_ref, gp_all, gm_all, dh, normed_all, dqkv_sum = refs[len(classes) :]
    step = pl.program_id(0)
    share = count_ref.shape[1]
    base = step * share

    @pl.when(step == 0)
    def _():
        gv = gv_ref[...]
        cnt2 = jnp.concatenate([all_counts_ref[...]] * 2, axis=1)
        gp = nt(gv, mats_ref[:, 4 * CW :]) / cnt2
        gp_all[...] = gp
        gpb = gp.astype(BF)
        gm_all[...] = nt(gpb, mats_ref[:, 3 * CW : 4 * CW]).astype(BF).astype(F32)
        grads_ref[:, 4 * CW :] = tn(pooled_ref[...], gv).astype(BF)
        grads_ref[:, 3 * CW : 4 * CW] = tn(msum_ref[...].astype(BF), gpb).astype(BF)
        dqkv_sum[...] = jnp.zeros_like(dqkv_sum)
        dgain_ref[...] = jnp.zeros_like(dgain_ref)

    @pl.when(kind[step] == 0)
    def _():
        dx_ref[...] = jnp.zeros_like(dx_ref)

    def block(places, words, order_ref):
        groups = share // words
        rows = groups * 128
        gain = gain_ref[...]
        xs = []
        scales = []
        gps = []
        for g in range(groups):
            at = g * 128
            x = nn(order_ref[...], x_ref[0, pl.ds(g * words * SPOTS, words * SPOTS), :])
            scale = lax.rsqrt(jnp.mean(x * x, axis=-1, keepdims=True) + epsilon)
            normed_all[at : at + 128, :] = (x * scale * gain).astype(BF)
            xs.append(x)
            scales.append(scale)
            mine = pl.ds(pl.multiple_of(base + g * words, words), words)
            cnt = count_ref[0, pl.ds(g * words, words), :]
            cnt2 = jnp.concatenate([cnt, cnt], axis=1)
            place = lax.broadcasted_iota(jnp.int32, (places, words, CW), 0).astype(F32)
            shown = place < cnt2[None]
            gps.append(jnp.where(shown, gp_all[mine, :][None], 0.0).reshape(128, CW))
            gm_word = gm_all[mine, :]
            gm = jnp.where(shown, gm_word[None], 0.0).reshape(128, CW).astype(BF)
            q = kept_ref[0, at : at + 128, :CW]
            k = kept_ref[0, at : at + 128, CW : 2 * CW]
            v = kept_ref[0, at : at + 128, 2 * CW : 3 * CW]
            p = kept_ref[0, at : at + 128, 3 * CW : 3 * CW + CHEADS * 128].astype(F32)
            c = kept_ref[0, at : at + 128, 3 * CW + CHEADS * 128 :].astype(F32)
            dp = nt(v, head_stack(gm, 1.0))
            p3 = p.reshape(places, words, CHEADS * 128)
            t = p3 * dp.reshape(places, words, CHEADS * 128)
            ds = (t - p3 * jnp.sum(t, axis=0)[None]).astype(BF).reshape(128, CHEADS * 128)
            eighth = 1.0 / math.sqrt(CHD)
            dk = nn(ds, head_stack(q, eighth))
            ds_rows = jnp.concatenate([ds[:, h * 128 : (h + 1) * 128] for h in range(CHEADS)], axis=0)
            dq = tn(ds_rows, head_stack(k, eighth))
            dv = (c.reshape(places, words, CW) * gm_word[None]).reshape(128, CW)
            dh[at : at + 128, :CW] = dq.astype(BF)
            dh[at : at + 128, CW : 2 * CW] = dk.astype(BF)
            dh[at : at + 128, 2 * CW :] = dv.astype(BF)
        grads = dh[:rows, :]
        dqkv_sum[...] += tn(normed_all[:rows, :], grads)
        dn_all = nt(grads, mats_ref[:, : 3 * CW])
        dgain = jnp.zeros((1, CW), F32)
        for g in range(groups):
            x, scale = xs[g], scales[g]
            dn = dn_all[g * 128 : (g + 1) * 128]
            xr = x * scale
            dgain = dgain + jnp.sum(xr * dn, axis=0, keepdims=True)
            w = dn * gain
            inner = jnp.mean(xr * w, axis=-1, keepdims=True)
            dx = gps[g] + scale * (w - xr * inner)
            dx_ref[0, pl.ds(g * words * SPOTS, words * SPOTS), :] = tn(
                order_ref[...], dx.astype(BF)
            ).astype(BF)
        dgain_ref[...] += dgain

    for (number, places, words), order_ref in zip(classes, orders):
        pl.when(kind[step] == number)(functools.partial(block, places, words, order_ref))

    @pl.when(step == pl.num_programs(0) - 1)
    def _():
        grads_ref[:, : 3 * CW] = dqkv_sum[...].astype(BF)


def char_backward(x, kind, counts, gain, mats, kept, pooled, msum, grad_vectors):
    slots, share = x.shape[:2]
    classes = char_classes(share)
    rows = share * SPOTS
    orders = [order_matrix(p, w) for _, p, w in classes]
    words_all = slots * share
    per_slot = lambda shape: pl.BlockSpec((1,) + shape, lambda i, *_: (i,) + (0,) * len(shape))
    dx, grads, dgain = pl.pallas_call(
        functools.partial(char_backward_kernel, classes),
        grid_spec=pltpu.PrefetchScalarGridSpec(
            num_scalar_prefetch=1,
            grid=(slots,),
            in_specs=[
                per_slot((rows, CW)),
                per_slot((share, 128)),
                per_slot((rows, KEPT)),
                whole((words_all, 128)),
                whole((words_all, D)),
                whole((words_all, CW)),
                whole((words_all, CW)),
                whole((1, CW)),
                whole(mats.shape),
            ]
            + [whole(o.shape) for o in orders],
            out_specs=[
                per_slot((rows, CW)),
                whole(mats.shape),
                whole((1, CW)),
            ],
            scratch_shapes=[
                pltpu.VMEM((words_all, CW), F32),
                pltpu.VMEM((words_all, CW), F32),
                pltpu.VMEM((rows, 3 * CW), BF),
                pltpu.VMEM((rows, CW), BF),
                pltpu.VMEM((CW, 3 * CW), F32),
            ],
        ),
        out_shape=[
            jax.ShapeDtypeStruct((slots, rows, CW), BF),
            jax.ShapeDtypeStruct(mats.shape, BF),
            jax.ShapeDtypeStruct((1, CW), F32),
        ],
        compiler_params=pltpu.CompilerParams(vmem_limit_bytes=60 << 20),
        cost_estimate=pl.CostEstimate(
            flops=slots * rows * CW * CW * 28, bytes_accessed=slots * rows * KEPT * 3, transcendentals=0
        ),
        name="char_backward",
    )(
        kind, x.reshape(slots, rows, CW), counts, kept, counts.reshape(words_all, 128), grad_vectors,
        pooled, msum, gain.reshape(1, CW), mats, *orders,
    )
    return dx.reshape(x.shape), grads, dgain


MESH_ID = pl.DeviceIdType.MESH


def greet(sizes, me):
    barrier = pltpu.get_barrier_semaphore()
    for axis, n in sizes.items():
        for d in range(1, n):
            pl.semaphore_signal(
                barrier, inc=1, device_id={axis: lax.rem(me[axis] + d, n)}, device_id_type=MESH_ID
            )
    pl.semaphore_wait(barrier, sum(n - 1 for n in sizes.values()))


def remote(source, target, sems, at, axis, peer):
    return pltpu.make_async_remote_copy(
        src_ref=source,
        dst_ref=target,
        send_sem=sems[0].at[at],
        recv_sem=sems[1].at[at],
        device_id={axis: peer},
        device_id_type=MESH_ID,
    )


def pair_gather_stages(own_of, sems, axis, n, mine, begin, late):
    chips = n // 2
    core = lax.rem(mine, 2)
    chip = mine // 2
    sibling = chip * 2 + 1 - core

    def start():
        for d in range(1, chips):
            there = lax.rem(chip + d, chips) * 2 + core
            remote(own_of(mine), own_of(mine), sems, d, axis, there).start()
        remote(own_of(mine), own_of(mine), sems, chips, axis, sibling).start()

    def hand_on():
        for d in range(1, chips):
            came = lax.rem(chip + chips - d, chips) * 2 + core
            remote(own_of(mine), own_of(came), sems, d, axis, sibling).wait_recv()
            remote(own_of(came), own_of(came), sems, chips + d, axis, sibling).start()

    def finish():
        for d in range(1, 2 * chips):
            remote(own_of(mine), own_of(mine), sems, d, axis, sibling).wait_send()
            if d >= chips:
                remote(own_of(mine), own_of(mine), sems, d, axis, sibling).wait_recv()

    return [(begin, start), (late, hand_on), (90.0, finish)]


def pair_part_stages(x, held, came, out, sems, axis, n, mine, begin, late):
    chips = n // 2
    core = lax.rem(mine, 2)
    chip = mine // 2
    sibling = chip * 2 + 1 - core

    def start():
        remote(x.at[:, 1 - core], came, sems, 0, axis, sibling).start()

    def onward():
        remote(x.at[:, 1 - core], came, sems, 0, axis, sibling).wait()
        for d in range(chips):
            there = lax.rem(chip + 1 + d, chips)
            came[there] = (came[there].astype(F32) + x[there, core].astype(F32)).astype(came.dtype)
            if d < chips - 1:
                remote(
                    came.at[there], held.at[chip], sems, 1 + d, axis, there * 2 + core
                ).start()

    def finish():
        held[chip] = came[chip]
        for d in range(chips - 1):
            remote(came.at[chip], held.at[chip], sems, 1 + d, axis, sibling).wait()
        total = held[0].astype(F32)
        for p in range(1, chips):
            total = total + held[p].astype(F32)
        out[...] = total.astype(out.dtype)

    return [(begin, start), (late, onward), (80.0, finish)]


def line_gather_stages(out, sems, axis, n, mine, begin, each):
    def step(k):
        for way in range(2):
            block = mine - k if way == 0 else mine + k
            here = (block >= 0) & (block < n)
            block = jnp.clip(block, 0, n - 1)
            onward = mine + 1 if way == 0 else mine - 1
            room = (onward >= 0) & (onward < n)
            peer = jnp.clip(onward, 0, n - 1)
            if k > 0:

                @pl.when(here)
                def _(way=way, block=block):
                    remote(out.at[block], out.at[block], sems, way * n + k - 1, axis, mine).wait_recv()

            if k < n - 1:

                @pl.when(here & room)
                def _(way=way, block=block, peer=peer):
                    remote(out.at[block], out.at[block], sems, way * n + k, axis, peer).start()

    def finish():
        for way in range(2):
            for k in range(n - 1):
                block = mine - k if way == 0 else mine + k
                sent = (mine < n - 1) & (block >= 0) if way == 0 else (mine > 0) & (block < n)

                @pl.when(sent)
                def _(way=way, k=k):
                    remote(out.at[mine], out.at[mine], sems, way * n + k, axis, mine).wait_send()

    stages = [(begin + each * k, functools.partial(step, k)) for k in range(n)]
    return stages + [(95.0, finish)]


def line_part_stages(x, held, out, sems, axis, n, mine, begin, each):
    def step(t):
        for way in range(2):
            distance = mine if way == 0 else n - 1 - mine
            turn = t - distance
            here = (turn >= 0) & (turn < n - 1 - distance)
            turn = jnp.clip(turn, 0, n - 1)
            block = n - 1 - turn if way == 0 else turn
            peer = jnp.clip(mine + 1 if way == 0 else mine - 1, 0, n - 1)
            at = way * n + block

            @pl.when(here & (distance == 0))
            def _(way=way, block=block, peer=peer, at=at):
                remote(x.at[block], held.at[way, block], sems, at, axis, peer).start()

            @pl.when(here & (distance > 0))
            def _(way=way, block=block, peer=peer, at=at):
                place = held.at[way, block]
                remote(place, place, sems, at, axis, mine).wait_recv()
                held[way, block] = (held[way, block].astype(F32) + x[block].astype(F32)).astype(x.dtype)
                remote(place, place, sems, at, axis, peer).start()

    def finish():
        out[...] = x[mine].astype(F32)
        for way, there in ((0, mine > 0), (1, mine < n - 1)):

            @pl.when(there)
            def _(way=way):
                here = held.at[way, mine]
                remote(here, here, sems, way * n + mine, axis, mine).wait_recv()
                out[...] += held[way, mine].astype(F32)

        for way in range(2):
            for block in range(n):
                further = block > mine if way == 0 else block < mine

                @pl.when(further)
                def _(way=way, block=block):
                    here = held.at[way, block]
                    remote(here, here, sems, way * n + block, axis, mine).wait_send()

    stages = [(begin + each * k, functools.partial(step, k)) for k in range(n - 1)]
    return stages + [(70.0, finish)]


def direct_stages(source_of, target, sems, axis, n, mine, begin, done, end):
    def start():
        for d in range(1, n):
            peer = lax.rem(mine + d, n)
            remote(source_of(peer), target.at[mine], sems, d, axis, peer).start()

    def finish():
        for d in range(1, n):
            remote(source_of(mine), target.at[mine], sems, d, axis, mine).wait()
        done()

    return [(begin, start), (end, finish)]


def exchange(name, number, tasks):
    sizes = {axis: lax.axis_size(axis) for _, axis, _ in tasks}
    outs, scratch, counts, shapers = [], [], [], []
    for kind, axis, arrays in tasks:
        n = sizes[axis]
        array = arrays[0]
        shaper = lambda a: a
        if kind == "gather":
            rows = array.shape[1]
            cols = sum(a.shape[0] * a.shape[2] for a in arrays)
            made = jax.ShapeDtypeStruct((n * rows, cols) if rows % 16 == 0 else (n, rows, cols), BF)
            shaper = lambda a, rows=rows, cols=cols, n=n: a.reshape(n * rows, cols)
        elif kind == "gather_mid":
            lead, rows, cols = array.shape
            made = jax.ShapeDtypeStruct(
                (lead, n * rows, cols) if rows % 16 == 0 else (n, lead, rows, cols), array.dtype
            )
            if rows % 16:
                shaper = lambda a, lead=lead, rows=rows, cols=cols, n=n: a.transpose(1, 0, 2, 3).reshape(
                    lead, n * rows, cols
                )
        else:
            block = array.shape if kind in ("line_gather", "total") else array.shape[1:]
            if kind == "part":
                block = array.shape[2:]
            summed = kind in ("part", "line_part", "total")
            made = jax.ShapeDtypeStruct(block if summed else (n,) + block, F32 if summed else array.dtype)
        outs.append(made)
        shapers.append(shaper)
        counts.append(len(arrays))
        scratch += [pltpu.SemaphoreType.DMA((2 * n,)), pltpu.SemaphoreType.DMA((2 * n,))]
        if kind == "part":
            scratch += [pltpu.VMEM((n // 2,) + block, array.dtype)] * 2
        if kind == "total":
            scratch.append(pltpu.VMEM((n,) + block, array.dtype))
        if kind == "line_part":
            scratch.append(pltpu.VMEM((2, n) + block, array.dtype))
    total_ins = sum(counts)

    def kernel(*refs):
        ins, at = [], 0
        for count in counts:
            ins.append(refs[at : at + count])
            at += count
        results = refs[at : at + len(tasks)]
        rest = list(refs[at + len(tasks) :])
        me = {axis: lax.axis_index(axis) for axis in sizes}
        greet(sizes, me)
        stages = []
        for (kind, axis, _), xs, out in zip(tasks, ins, results):
            sems = (rest.pop(0), rest.pop(0))
            n, mine, x = sizes[axis], me[axis], xs[0]
            if kind == "line_gather":
                out[mine] = x[...]
                stages += line_gather_stages(out, sems, axis, n, mine, 0.0, 6.0)
            elif kind == "line_part":
                stages += line_part_stages(x, rest.pop(0), out, sems, axis, n, mine, 0.0, 6.0)
            elif kind == "part":
                held, came = rest.pop(0), rest.pop(0)
                stages += pair_part_stages(x, held, came, out, sems, axis, n, mine, 0.1, 1.0)
            elif kind in ("gather", "gather_mid"):
                if kind == "gather":
                    rows = x.shape[1]
                    if rows % 16 == 0:
                        own_of = lambda i, out=out, rows=rows: out.at[
                            pl.ds(pl.multiple_of(i * rows, 16), rows), :
                        ]
                    else:
                        own_of = lambda i, out=out: out.at[i]
                    own, col = own_of(mine), 0
                    for piece in xs:
                        for t in range(piece.shape[0]):
                            own[:, col : col + piece.shape[2]] = piece[t].astype(BF)
                            col += piece.shape[2]
                else:
                    rows = x.shape[1]
                    if rows % 16 == 0:
                        own_of = lambda i, out=out, rows=rows: out.at[
                            :, pl.ds(pl.multiple_of(i * rows, 16), rows), :
                        ]
                    else:
                        own_of = lambda i, out=out: out.at[i]
                    own_of(mine)[...] = x[...]
                if axis == "dp":
                    stages += pair_gather_stages(own_of, sems, axis, n, mine, 0.2, 7.0)
                else:

                    def start(own_of=own_of, sems=sems, axis=axis, n=n, mine=mine):
                        for d in range(1, n):
                            peer = lax.rem(mine + d, n)
                            remote(own_of(mine), own_of(mine), sems, d, axis, peer).start()

                    def finish(own_of=own_of, sems=sems, axis=axis, n=n, mine=mine):
                        for d in range(1, n):
                            remote(own_of(mine), own_of(mine), sems, d, axis, mine).wait()

                    stages += [(0.15, start), (90.0, finish)]
            elif kind == "total":
                held = rest.pop(0)
                held[mine] = x[...]

                def done(held=held, out=out, n=n):
                    total = held[0].astype(F32)
                    for p in range(1, n):
                        total = total + held[p].astype(F32)
                    out[...] = total

                stages += direct_stages(
                    lambda p, held=held, mine=mine: held.at[mine], held, sems, axis, n, mine, 0.3, done, 60.0
                )
            else:
                out[mine] = x[mine]
                stages += direct_stages(
                    lambda p, x=x: x.at[p], out, sems, axis, n, mine, 0.0, lambda: None, 60.0
                )
        for _, run in sorted(stages, key=lambda stage: stage[0]):
            run()

    vmem = pl.BlockSpec(memory_space=pltpu.VMEM)
    results = pl.pallas_call(
        kernel,
        out_shape=outs,
        in_specs=[vmem] * total_ins,
        out_specs=[vmem] * len(tasks),
        scratch_shapes=scratch,
        compiler_params=pltpu.CompilerParams(
            collective_id=number, has_side_effects=True, vmem_limit_bytes=48 << 20
        ),
        name=name,
    )(*[array for _, _, arrays in tasks for array in arrays])
    return [shaper(a) for shaper, a in zip(shapers, results)]


def by_chip(array):
    return array.reshape(lax.axis_size("dp") // 2, 2, -1, array.shape[-1])


def sum_char_grads(grads, small, word_sums):
    n, m = lax.axis_size("dp"), lax.axis_size("mp")
    grads = by_chip(grads)
    rows, cols = grads.shape[2:]
    slim = cols // m

    def kernel(x, s, *refs):
        words = refs[: len(word_sums)]
        (out, small_out, held, came, total_dp, cut, cut_held, merged, small_dp, small_mp, *sems) = refs[len(word_sums) :]
        pairs = [tuple(sems[2 * t : 2 * t + 2]) for t in range(6)]
        i, j = lax.axis_index("dp"), lax.axis_index("mp")
        greet({"dp": n, "mp": m}, {"dp": i, "mp": j})
        part = [
            run for _, run in pair_part_stages(x, held, came, total_dp, pairs[0], "dp", n, i, 0.0, 0.0)
        ]
        part[0]()
        squares = jnp.zeros((1, 1), F32)
        for word in words:
            wide = word[...].astype(F32)
            squares = squares + jnp.sum(jnp.sum(wide * wide, axis=0, keepdims=True), axis=1, keepdims=True)
        row = lax.broadcasted_iota(jnp.int32, s.shape, 0)
        small_dp[i] = s[...] + jnp.where(row == 3, squares * (1.0 / n), 0.0)
        part[1]()

        def small_done():
            total = small_dp[0]
            for p in range(1, n):
                total = total + small_dp[p]
            small_mp[j] = total

        def small_end():
            total = small_mp[0]
            for p in range(1, m):
                total = total + small_mp[p]
            small_out[...] = total

        def cut_done():
            total = cut_held[0].astype(F32)
            for p in range(1, m):
                total = total + cut_held[p].astype(F32)
            merged[j] = total.astype(BF)

        one = direct_stages(lambda p: small_dp.at[i], small_dp, pairs[1], "dp", n, i, 0, small_done, 0)
        two = direct_stages(lambda p: small_mp.at[j], small_mp, pairs[2], "mp", m, j, 0, small_end, 0)
        three = direct_stages(lambda p: cut.at[p], cut_held, pairs[3], "mp", m, j, 0, cut_done, 0)
        four = direct_stages(lambda p: merged.at[j], merged, pairs[4], "mp", m, j, 0, lambda: None, 0)
        one[0][1]()
        part[2]()
        for p in range(m):
            cut[p] = total_dp[:, p * slim : (p + 1) * slim]
        cut_held[j] = cut[j]
        three[0][1]()
        one[1][1]()
        two[0][1]()
        three[1][1]()
        four[0][1]()
        two[1][1]()
        four[1][1]()
        if rows % 16 == 0:
            own_of = lambda d: out.at[pl.ds(pl.multiple_of(d * rows, 16), rows), :]
        else:
            own_of = lambda d: out.at[d]
        own = own_of(i)
        for p in range(m):
            own[:, p * slim : (p + 1) * slim] = merged[p]
        for _, run in pair_gather_stages(own_of, pairs[5], "dp", n, i, 0, 0):
            run()

    vmem = pl.BlockSpec(memory_space=pltpu.VMEM)
    sums, smalls = pl.pallas_call(
        kernel,
        out_shape=[
            jax.ShapeDtypeStruct((n * rows, cols) if rows % 16 == 0 else (n, rows, cols), BF),
            jax.ShapeDtypeStruct(small.shape, F32),
        ],
        in_specs=[vmem] * (2 + len(word_sums)),
        out_specs=[vmem] * 2,
        scratch_shapes=[
            pltpu.VMEM((n // 2, rows, cols), BF),
            pltpu.VMEM((n // 2, rows, cols), BF),
            pltpu.VMEM((rows, cols), BF),
            pltpu.VMEM((m, rows, slim), BF),
            pltpu.VMEM((m, rows, slim), BF),
            pltpu.VMEM((m, rows, slim), BF),
            pltpu.VMEM((n,) + small.shape, F32),
            pltpu.VMEM((m,) + small.shape, F32),
        ]
        + [pltpu.SemaphoreType.DMA((2 * max(n, m),))] * 12,
        compiler_params=pltpu.CompilerParams(
            collective_id=20, has_side_effects=True, vmem_limit_bytes=48 << 20
        ),
        name="sum_char_grads",
    )(grads, small, *word_sums)
    return sums.reshape(n * rows, cols), smalls


ROWS = 256


def rms_scale(values):
    return lax.rsqrt(jnp.mean(values * values, axis=-1, keepdims=True) + epsilon)


def norm_back(values, scale, gain_row, grad):
    weighted = grad * gain_row
    inner = jnp.mean(values * weighted, axis=-1, keepdims=True)
    return scale * weighted - values * (scale * scale * scale) * inner


def word_forward_kernel(
    width, vec_ref, place_ref, words_ref, doc_ref, doc_row_ref, gain_ref, project_ref,
    stream_ref, normed_ref, qkv_ref, probs_ref, mixed_ref, keys, values
):
    step = pl.program_id(0)
    numbers = lax.broadcasted_iota(jnp.int32, (ROWS, place_ref.shape[1]), 0) + step * ROWS
    placed = nn((numbers == place_ref[...]).astype(BF), vec_ref[...])
    stream = words_ref[...].astype(F32) + placed
    stream_ref[...] = stream
    normed = (stream * rms_scale(stream) * gain_ref[...]).astype(BF)
    normed_ref[...] = normed
    qkv = nn(normed, project_ref[...]).astype(BF)
    qkv_ref[...] = qkv
    first = pl.ds(pl.multiple_of(step * ROWS, ROWS), ROWS)
    keys[first, :] = qkv[:, width : 2 * width]
    values[first, :] = qkv[:, 2 * width :]
    queries = (qkv[:, :width].astype(F32) * (1.0 / math.sqrt(HD))).astype(BF)

    def attend(number):
        count = (number + 1) * ROWS
        same = doc_ref[:count, :] == doc_row_ref[...]
        key_at = lax.broadcasted_iota(jnp.int32, (count, ROWS), 0)
        query_at = lax.broadcasted_iota(jnp.int32, (count, ROWS), 1) + number * ROWS
        allowed = same & (key_at <= query_at)
        parts = []
        for head in range(width // HD):
            at = slice(head * HD, (head + 1) * HD)
            scores = jnp.where(allowed, nt(keys[:count, at], queries[:, at]), negative_big)
            raised = jnp.exp(scores - jnp.max(scores, axis=0, keepdims=True))
            probs = (raised * (1.0 / jnp.sum(raised, axis=0, keepdims=True))).astype(BF)
            probs_ref[head, :count, :] = probs
            parts.append(tn(values[:count, at], probs).T)
        mixed_ref[...] = jnp.concatenate(parts, axis=1).astype(BF)

    for number in range(doc_ref.shape[0] // ROWS):
        pl.when(step == number)(functools.partial(attend, number))


def word_forward(vectors, places, words, documents, gain, project):
    length = words.shape[0]
    width = project.shape[1] // 3
    heads = width // HD
    rows = lambda cols: pl.BlockSpec((ROWS, cols), lambda i: (i, 0))
    full = lambda shape: pl.BlockSpec(shape, lambda i: (0,) * len(shape))
    return pl.pallas_call(
        functools.partial(word_forward_kernel, width),
        grid=(length // ROWS,),
        in_specs=[
            full(vectors.shape),
            full((1, places.shape[0])),
            rows(D),
            full((length, 1)),
            pl.BlockSpec((1, ROWS), lambda i: (0, i)),
            full((1, D)),
            full(project.shape),
        ],
        out_specs=[
            rows(D),
            rows(D),
            rows(3 * width),
            pl.BlockSpec((heads, length, ROWS), lambda i: (0, 0, i)),
            rows(width),
        ],
        out_shape=[
            jax.ShapeDtypeStruct((length, D), F32),
            jax.ShapeDtypeStruct((length, D), BF),
            jax.ShapeDtypeStruct((length, 3 * width), BF),
            jax.ShapeDtypeStruct((heads, length, length), BF),
            jax.ShapeDtypeStruct((length, width), BF),
        ],
        scratch_shapes=[pltpu.VMEM((length, width), BF), pltpu.VMEM((length, width), BF)],
        compiler_params=pltpu.CompilerParams(vmem_limit_bytes=48 << 20),
        name="word_forward",
    )(
        vectors,
        places.reshape(1, -1),
        words,
        documents.reshape(length, 1),
        documents.reshape(1, length),
        gain.reshape(1, D),
        project,
    )


def feed_kernel(
    mixed_ref, output_ref, stream_ref, cot_ref, gain_ref, upper_ref, lower_ref,
    hidden_ref, feed_ref, part_ref, grad_upper_ref, grad_lower_ref, upper_sum, lower_sum
):
    step = pl.program_id(0)

    @pl.when(step == 0)
    def _():
        upper_sum[...] = jnp.zeros_like(upper_sum)
        lower_sum[...] = jnp.zeros_like(lower_sum)

    parts, _, width = mixed_ref.shape
    hidden = stream_ref[...]
    for j in range(parts):
        hidden = hidden + nn(mixed_ref[j], output_ref[j * width : (j + 1) * width, :])
    hidden_ref[...] = hidden
    normed = (hidden * rms_scale(hidden) * gain_ref[...]).astype(BF)
    raised = nn(normed, upper_ref[...])
    constant = math.sqrt(2.0 / math.pi)
    square = raised * raised
    curve = jnp.tanh(constant * raised * (1.0 + 0.044715 * square))
    half = 0.5 * (1.0 + curve)
    active = (raised * half).astype(BF)
    slope = half + 0.5 * raised * (1.0 - curve * curve) * constant * (1.0 + 3.0 * 0.044715 * square)
    feed_ref[...] = nn(active, lower_ref[...]).astype(BF)
    grad_feed = cot_ref[...]
    grad_raised = (nt(grad_feed, lower_ref[...]) * slope).astype(BF)
    part_ref[...] = nt(grad_raised, upper_ref[...]).astype(BF)
    lower_sum[...] += tn(active, grad_feed)
    upper_sum[...] += tn(normed, grad_raised)

    @pl.when(step == pl.num_programs(0) - 1)
    def _():
        grad_upper_ref[...] = upper_sum[...].astype(BF)
        grad_lower_ref[...] = lower_sum[...].astype(BF)


def feed(mixed, output, stream, cotangent, gain, upper, lower):
    length = stream.shape[0]
    rows = pl.BlockSpec((ROWS, D), lambda i: (i, 0))
    full = lambda shape: pl.BlockSpec(shape, lambda i: (0,) * len(shape))
    return pl.pallas_call(
        feed_kernel,
        grid=(length // ROWS,),
        in_specs=[
            pl.BlockSpec((mixed.shape[0], ROWS, mixed.shape[2]), lambda i: (0, i, 0)),
            full(output.shape),
            rows,
            rows,
            full((1, D)),
            full(upper.shape),
            full(lower.shape),
        ],
        out_specs=[rows, rows, rows, full(upper.shape), full(lower.shape)],
        out_shape=[
            jax.ShapeDtypeStruct((length, D), F32),
            jax.ShapeDtypeStruct((length, D), BF),
            jax.ShapeDtypeStruct((length, D), BF),
            jax.ShapeDtypeStruct(upper.shape, BF),
            jax.ShapeDtypeStruct(lower.shape, BF),
        ],
        scratch_shapes=[pltpu.VMEM(upper.shape, F32), pltpu.VMEM(lower.shape, F32)],
        compiler_params=pltpu.CompilerParams(vmem_limit_bytes=48 << 20),
        name="feed",
    )(mixed, output, stream, cotangent, gain.reshape(1, D), upper, lower)


def hidden_back_kernel(
    own, grad_ref, hidden_ref, cot_ref, mixed_ref, output_ref, gain_ref,
    grad_hidden_ref, grad_mixed_ref, grad_output_ref, gain_grad_ref
):
    hidden = hidden_ref[...]
    scale = rms_scale(hidden)
    grad = grad_ref[...]
    grad_hidden = cot_ref[...].astype(F32) + norm_back(hidden, scale, gain_ref[...], grad)
    grad_hidden_ref[...] = grad_hidden
    gain_grad_ref[...] = jnp.sum(hidden * scale * grad, axis=0, keepdims=True)
    attend = grad_hidden.astype(BF)
    parts, _, width = mixed_ref.shape
    for j in range(parts):
        at = slice(j * width, (j + 1) * width)
        grad_mixed_ref[j] = nt(attend, output_ref[at, :]).astype(BF)
        grad_output_ref[at, :] = tn(mixed_ref[j], attend).astype(BF)


def hidden_back(own, grad, hidden, cotangent, mixed, output, gain):
    share = grad.shape[0]
    parts, _, width = mixed.shape
    mine = pl.BlockSpec((share, D), lambda i, own: (own[0], 0))
    full = lambda shape: pl.BlockSpec(shape, lambda i, own: (0,) * len(shape))
    return pl.pallas_call(
        hidden_back_kernel,
        grid_spec=pltpu.PrefetchScalarGridSpec(
            num_scalar_prefetch=1,
            grid=(1,),
            in_specs=[
                full((share, D)),
                mine,
                mine,
                pl.BlockSpec((parts, share, width), lambda i, own: (0, own[0], 0)),
                full(output.shape),
                full((1, D)),
            ],
            out_specs=[
                full((share, D)),
                full((parts, share, width)),
                full(output.shape),
                full((1, D)),
            ],
        ),
        out_shape=[
            jax.ShapeDtypeStruct((share, D), F32),
            jax.ShapeDtypeStruct((parts, share, width), BF),
            jax.ShapeDtypeStruct(output.shape, BF),
            jax.ShapeDtypeStruct((1, D), F32),
        ],
        compiler_params=pltpu.CompilerParams(vmem_limit_bytes=48 << 20),
        name="hidden_back",
    )(own, grad, hidden, cotangent, mixed, output, gain.reshape(1, D))


def word_backward_kernel(
    width, probs_ref, qkv_ref, all_ref, grad_ref, normed_ref, project_ref,
    part_ref, grad_project_ref, grads, key_sum, value_sum
):
    step = pl.program_id(0)
    steps = all_ref.shape[0] // ROWS
    first = pl.ds(pl.multiple_of(step * ROWS, ROWS), ROWS)
    eighth = 1.0 / math.sqrt(HD)
    queries = (qkv_ref[:, :width].astype(F32) * eighth).astype(BF)

    @pl.when(step == 0)
    def _():
        key_sum[...] = jnp.zeros_like(key_sum)
        value_sum[...] = jnp.zeros_like(value_sum)

    def attend(number):
        count = (number + 1) * ROWS
        parts = []
        for head in range(width // HD):
            at = slice(head * HD, (head + 1) * HD)
            keys = all_ref[:count, width + head * HD : width + (head + 1) * HD]
            values = all_ref[:count, 2 * width + head * HD : 2 * width + (head + 1) * HD]
            grad = grad_ref[:, at]
            probs = probs_ref[head, :count, :]
            wide = probs.astype(F32)
            product = wide * nt(values, grad)
            scores = (product - wide * jnp.sum(product, axis=0, keepdims=True)).astype(BF)
            key_sum[head, :count, :] += nn(scores, queries[:, at])
            value_sum[head, :count, :] += nn(probs, grad)
            parts.append(tn(keys, scores).T * eighth)
        grads[first, :width] = jnp.concatenate(parts, axis=1).astype(BF)

    for number in range(steps):
        pl.when(step == number)(functools.partial(attend, number))

    @pl.when(step == steps - 1)
    def _():
        for head in range(width // HD):
            grads[:, width + head * HD : width + (head + 1) * HD] = key_sum[head].astype(BF)
            grads[:, 2 * width + head * HD : 2 * width + (head + 1) * HD] = value_sum[head].astype(BF)
        grad_project_ref[...] = tn(normed_ref[...], grads[...]).astype(BF)
        part_ref[...] = nt(grads[...], project_ref[...]).astype(BF)


def word_backward(probs, qkv, grad_mixed, normed, project):
    length = qkv.shape[0]
    width = project.shape[1] // 3
    heads = width // HD
    rows = lambda cols: pl.BlockSpec((ROWS, cols), lambda i: (i, 0))
    full = lambda shape: pl.BlockSpec(shape, lambda i: (0,) * len(shape))
    return pl.pallas_call(
        functools.partial(word_backward_kernel, width),
        grid=(length // ROWS,),
        in_specs=[
            pl.BlockSpec((heads, length, ROWS), lambda i: (0, 0, i)),
            rows(3 * width),
            full(qkv.shape),
            rows(width),
            full(normed.shape),
            full(project.shape),
        ],
        out_specs=[full((length, D)), full(project.shape)],
        out_shape=[
            jax.ShapeDtypeStruct((length, D), BF),
            jax.ShapeDtypeStruct(project.shape, BF),
        ],
        scratch_shapes=[
            pltpu.VMEM(qkv.shape, BF),
            pltpu.VMEM((heads, length, HD), F32),
            pltpu.VMEM((heads, length, HD), F32),
        ],
        compiler_params=pltpu.CompilerParams(vmem_limit_bytes=48 << 20),
        name="word_backward",
    )(probs, qkv, qkv, grad_mixed, normed, project)


def stream_back_kernel(own, grad_ref, stream_ref, hidden_grad_ref, gain_ref, out_ref, gain_grad_ref):
    stream = stream_ref[...]
    scale = rms_scale(stream)
    grad = grad_ref[...]
    total = hidden_grad_ref[...] + norm_back(stream, scale, gain_ref[...], grad)
    out_ref[...] = total.astype(BF)
    gain_grad_ref[...] = jnp.sum(stream * scale * grad, axis=0, keepdims=True)


def stream_back(own, grad, stream, hidden_grad, gain):
    share = grad.shape[0]
    full = lambda shape: pl.BlockSpec(shape, lambda i, own: (0,) * len(shape))
    return pl.pallas_call(
        stream_back_kernel,
        grid_spec=pltpu.PrefetchScalarGridSpec(
            num_scalar_prefetch=1,
            grid=(1,),
            in_specs=[
                full((share, D)),
                pl.BlockSpec((share, D), lambda i, own: (own[0], 0)),
                full((share, D)),
                full((1, D)),
            ],
            out_specs=[full((share, D)), full((1, D))],
        ),
        out_shape=[
            jax.ShapeDtypeStruct((share, D), BF),
            jax.ShapeDtypeStruct((1, D), F32),
        ],
        name="stream_back",
    )(own, grad, stream, hidden_grad, gain.reshape(1, D))


def shampoo_kernel(threshold, position, char_ref, small_ref, gain_ref, gains_ref, *refs):
    sums, refs = refs[:4], refs[4:]
    given, refs = [refs[5 * t : 5 * t + 5] for t in range(6)], refs[30:]
    norm_ref, gain_grad_ref, gains_grad_ref, gain_new_ref, gains_new_ref = refs[:5]
    made = [refs[5 + 5 * t : 10 + 5 * t] for t in range(6)]
    me = position[0]
    char = char_ref[...].astype(F32)
    small = small_ref[...]
    lanes = lax.broadcasted_iota(jnp.int32, small.shape, 0)
    squares = (
        jnp.sum(jnp.sum(char * char, axis=0, keepdims=True), axis=1, keepdims=True)
        + jnp.sum(
            jnp.sum(jnp.where(lanes < 3, small * small, 0.0), axis=0, keepdims=True),
            axis=1,
            keepdims=True,
        )
        + small[3:4, :1]
    )
    norm = jnp.sqrt(squares)
    factor = jnp.minimum(1.0, threshold / norm)
    norm_ref[...] = norm
    gain_grad = small[0:1, :CW] * factor
    gain_grad_ref[...] = gain_grad
    gain_new_ref[...] = gain_ref[...] - gain_rate * gain_grad
    gains_grad = small[1:3, :] * factor
    gains_grad_ref[...] = gains_grad
    gains_new_ref[...] = gains_ref[...] - gain_rate * gains_grad
    width = sums[0].shape[1] // 3

    def whole_of(number, t):
        if number == 0:
            return char_ref[:, t * CW : (t + 1) * CW]
        if number == 1:
            return char_ref[:, 4 * CW :]
        if number == 2:
            return sums[0][:, t * width : (t + 1) * width]
        return sums[number - 2][...]

    def chosen(rows, cols):
        row = lax.broadcasted_iota(jnp.int32, (rows, cols), 0) + me * rows
        return (row == lax.broadcasted_iota(jnp.int32, (rows, cols), 1)).astype(BF)

    half = (1.0 - decay_rate) * factor * factor
    for number in range(6):
        master, left, right, left_root, right_root = given[number]
        grad_out, left_out, right_out, new_out, copy_out = made[number]
        for t in range(master.shape[0]):
            grad = whole_of(number, t)
            own = nn(chosen(master.shape[1], grad.shape[0]), grad)
            grad_out[t] = own * factor
            left_out[t] = decay_rate * left[t] + half * nt(own.astype(BF), grad)
            cols = nt(grad, chosen(right.shape[1], grad.shape[1])).astype(BF)
            right_out[t] = decay_rate * right[t] + half * tn(cols, grad)
            turned = (nn(left_root[t].astype(BF), grad) * factor).astype(BF)
            new = master[t] - learn_rate * nn(turned, right_root[:, t * grad.shape[1] : (t + 1) * grad.shape[1]])
            new_out[t] = new
            copy_out[t] = new.astype(BF)


def shampoo(threshold, position, char_sums, small, gain, gains, word_sums, given):
    flat = []
    shapes = [
        jax.ShapeDtypeStruct((1, 1), F32),
        jax.ShapeDtypeStruct((1, CW), F32),
        jax.ShapeDtypeStruct((2, D), F32),
        jax.ShapeDtypeStruct((1, CW), F32),
        jax.ShapeDtypeStruct((2, D), F32),
    ]
    for master, left, right, left_root, right_root in given:
        flat += [master, left, right, left_root, right_root]
        shapes += [
            jax.ShapeDtypeStruct(a.shape, F32) for a in (master, left, right, master)
        ] + [jax.ShapeDtypeStruct(master.shape, BF)]
    vmem = pl.BlockSpec(memory_space=pltpu.VMEM)
    smem = pl.BlockSpec(memory_space=pltpu.SMEM)
    return pl.pallas_call(
        functools.partial(shampoo_kernel, threshold),
        in_specs=[smem] + [vmem] * (4 + len(word_sums) + len(flat)),
        out_specs=[vmem] * len(shapes),
        out_shape=shapes,
        compiler_params=pltpu.CompilerParams(vmem_limit_bytes=56 << 20),
        name="shampoo",
    )(position, char_sums, small, gain.reshape(1, CW), gains, *word_sums, *flat)


def run_stages(stages):
    for _, run in sorted(stages, key=lambda stage: stage[0]):
        run()


def spread_blocks(chosen, rows, cols, share):
    up = lax.broadcasted_iota(jnp.int32, (rows, chosen.shape[0]), 0) // share
    up = (up == lax.broadcasted_iota(jnp.int32, (rows, chosen.shape[0]), 1)).astype(BF)
    down = lax.broadcasted_iota(jnp.int32, (chosen.shape[1], cols), 1) // share
    down = (down == lax.broadcasted_iota(jnp.int32, (chosen.shape[1], cols), 0)).astype(BF)
    wide = nn(nn(up, chosen).astype(BF), down)
    row = lax.broadcasted_iota(jnp.int32, (rows, cols), 0) % share
    col = lax.broadcasted_iota(jnp.int32, (rows, cols), 1) % share
    return jnp.where(row == col, wide, 0.0).astype(BF)


def gather_setup(xs, out):
    rows = xs[0].shape[1]

    def own_of(i):
        if rows % 16 == 0:
            return out.at[pl.ds(pl.multiple_of(i * rows, 16), rows), :]
        return out.at[i]

    def put(mine):
        own, col = own_of(mine), 0
        for piece in xs:
            for t in range(piece.shape[0]):
                own[:, col : col + piece.shape[2]] = piece[t].astype(BF)
                col += piece.shape[2]

    return own_of, put


def gather_shape(arrays, n):
    rows = arrays[0].shape[1]
    cols = sum(a.shape[0] * a.shape[2] for a in arrays)
    shape = (n * rows, cols) if rows % 16 == 0 else (n, rows, cols)
    return jax.ShapeDtypeStruct(shape, BF), lambda a: a.reshape(n * rows, cols)


def dma_sems(count):
    return [pltpu.SemaphoreType.DMA((count,))] * 2


def call_remote(kernel, name, number, outs, scratch, inputs):
    vmem = pl.BlockSpec(memory_space=pltpu.VMEM)
    return pl.pallas_call(
        kernel,
        out_shape=outs,
        in_specs=[vmem] * len(inputs),
        out_specs=[vmem] * len(outs),
        scratch_shapes=scratch,
        compiler_params=pltpu.CompilerParams(
            collective_id=number, has_side_effects=True, vmem_limit_bytes=56 << 20
        ),
        name=name,
    )(*inputs)


def send_vectors(vectors, to_slot, to_live, share, project, upper, lower, output_line):
    n, m = lax.axis_size("dp"), lax.axis_size("mp")
    total = to_slot.shape[0] * share
    block = total // n
    kept = OWNER_BLOCKS * share
    made = [gather_shape([a], n) for a in (project, upper, lower)]
    made[0] = gather_shape([project], n)
    lead, line_rows, line_cols = output_line.shape
    aligned = line_rows % 16 == 0
    output_shape = (lead, n * line_rows, line_cols) if aligned else (n, lead, line_rows, line_cols)

    def kernel(vec, slots, live, *refs):
        weights, line = refs[:3], refs[3]
        out, wides, output = refs[4], refs[5:8], refs[8]
        sent, came, *sems = refs[9:]
        pairs = [tuple(sems[2 * t : 2 * t + 2]) for t in range(6)]
        i, j = lax.axis_index("dp"), lax.axis_index("mp")
        sent[...] = (
            nn(spread_blocks(slots[...], total, vec.shape[0], share), vec[...])
            .astype(BF)
            .reshape(sent.shape)
        )
        greet({"dp": n, "mp": m}, {"dp": i, "mp": j})
        came[i] = sent[i]
        stages = []

        def compact():
            out[j] = nn(
                spread_blocks(live[...], kept, total, share), came[...].reshape(total, D)
            ).astype(BF)

        stages += direct_stages(lambda p: sent.at[p], came, pairs[0], "dp", n, i, 0.0, compact, 1.0)
        stages += line_gather_stages(out, pairs[1], "mp", m, j, 2.0, 6.0)
        for t, (x, wide) in enumerate(zip(weights, wides)):
            own_of, put = gather_setup([x], wide)
            put(i)
            stages += pair_gather_stages(own_of, pairs[2 + t], "dp", n, i, 2.1, 9.0)
        if aligned:
            output_of = lambda d: output.at[:, pl.ds(pl.multiple_of(d * line_rows, 16), line_rows), :]
        else:
            output_of = lambda d: output.at[d]
        output_of(i)[...] = line[...]
        stages += pair_gather_stages(output_of, pairs[5], "dp", n, i, 2.1, 9.0)
        run_stages(stages)

    results = call_remote(
        kernel,
        "send_vectors",
        1,
        [jax.ShapeDtypeStruct((m, kept, D), BF)]
        + [shape for shape, _ in made]
        + [jax.ShapeDtypeStruct(output_shape, BF)],
        [pltpu.VMEM((n, block, D), BF)] * 2 + dma_sems(2 * max(n, m)) * 6,
        [vectors, to_slot, to_live, project, upper, lower, output_line],
    )
    output = results[4]
    if not aligned:
        output = output.transpose(1, 0, 2, 3)
    return (
        [results[0]]
        + [shaper(a) for (_, shaper), a in zip(made, results[1:4])]
        + [output.reshape(-1, line_cols)]
    )


def hidden_grads(part_two, hidden, cotangent, mixed, output, gain, grad_upper, grad_lower, roots):
    n, m = lax.axis_size("dp"), lax.axis_size("mp")
    share = part_two.shape[1]
    width = mixed.shape[2]
    made = [gather_shape([a], n) for a in roots]
    parts = [by_chip(grad_upper), by_chip(grad_lower)]

    def kernel(part, hidden_ref, cot, mix, out_mat, gain_ref, up, low, *refs):
        roots_in, refs = refs[: len(roots)], refs[len(roots) :]
        grad_hidden, grad_mixed, grad_output, gain_grad, up_sum, low_sum = refs[:6]
        roots_out, refs = refs[6 : 6 + len(roots)], refs[6 + len(roots) :]
        held, total, swapped, up_held, up_came, low_held, low_came, *sems = refs
        pairs = [tuple(sems[2 * t : 2 * t + 2]) for t in range(4 + len(roots))]
        i, j = lax.axis_index("dp"), lax.axis_index("mp")
        greet({"dp": n, "mp": m}, {"dp": i, "mp": j})
        stages = line_part_stages(part, held, total, pairs[0], "mp", m, j, 0.0, 6.0)
        stages += pair_part_stages(up, up_held, up_came, up_sum, pairs[1], "dp", n, i, 0.1, 1.0)
        stages += pair_part_stages(low, low_held, low_came, low_sum, pairs[2], "dp", n, i, 0.1, 1.0)
        for t, (x, out) in enumerate(zip(roots_in, roots_out)):
            own_of, put = gather_setup([x], out)
            put(i)
            stages += pair_gather_stages(own_of, pairs[4 + t], "dp", n, i, 2.0, 11.0)

        def back():
            mine = pl.ds(pl.multiple_of(j * share, share), share)
            hidden_own = hidden_ref[mine, :]
            scale = rms_scale(hidden_own)
            grad = total[...]
            whole_grad = cot[mine, :].astype(F32) + norm_back(hidden_own, scale, gain_ref[...], grad)
            grad_hidden[...] = whole_grad
            gain_grad[...] = jnp.sum(hidden_own * scale * grad, axis=0, keepdims=True)
            attend = whole_grad.astype(BF)
            for p in range(m):
                swapped[p] = nt(attend, out_mat[p * width : (p + 1) * width, :]).astype(BF)
            grad_mixed[j] = swapped[j]

        def output_grad():
            mine = pl.ds(pl.multiple_of(j * share, share), share)
            attend = grad_hidden[...].astype(BF)
            for p in range(m):
                grad_output[p * width : (p + 1) * width, :] = tn(mix[p, mine, :], attend).astype(BF)

        stages += [(71.0, back), (73.0, output_grad)]
        stages += direct_stages(
            lambda p: swapped.at[p], grad_mixed, pairs[3], "mp", m, j, 72.0, lambda: None, 75.0
        )
        run_stages(stages)

    block = lambda a: pltpu.VMEM(a.shape[:1] + a.shape[2:], BF)
    results = call_remote(
        kernel,
        "hidden_grads",
        4,
        [
            jax.ShapeDtypeStruct((share, D), F32),
            jax.ShapeDtypeStruct((m, share, width), BF),
            jax.ShapeDtypeStruct(output.shape, BF),
            jax.ShapeDtypeStruct((1, D), F32),
            jax.ShapeDtypeStruct(parts[0].shape[2:], F32),
            jax.ShapeDtypeStruct(parts[1].shape[2:], F32),
        ]
        + [shape for shape, _ in made],
        [
            pltpu.VMEM((2, m, share, D), BF),
            pltpu.VMEM((share, D), F32),
            pltpu.VMEM((m, share, width), BF),
            block(parts[0]),
            block(parts[0]),
            block(parts[1]),
            block(parts[1]),
        ]
        + dma_sems(2 * max(n, m)) * (4 + len(roots)),
        [part_two, hidden, cotangent, mixed, output, gain.reshape(1, D)] + parts + roots,
    )
    return list(results[:6]) + [shaper(a) for (_, shaper), a in zip(made, results[6:])]


def stream_grads(part_one, stream, grad_hidden, gain, own_row, to_slot, sums, grad_project, grad_output, slots):
    n, m = lax.axis_size("dp"), lax.axis_size("mp")
    share = part_one.shape[1]
    total_words = own_row.shape[1]
    block = total_words // n
    words = share * m
    width = total_words // to_slot.shape[0]
    parts = [by_chip(grad_project), by_chip(grad_output)]
    chunk = lambda a: jax.ShapeDtypeStruct((1,) + a.shape[-2:], F32)
    made = [gather_shape([chunk(a)], n) for a in (sums[0], sums[1], parts[0], parts[1])]

    def kernel(part, stream_ref, hidden_ref, gain_ref, row_ref, slot_ref, up, low, project, output, *refs):
        out, gain_grad, vectors, up_out, low_out, project_out, output_out = refs[:7]
        (held, total, project_sum, output_sum, line_held, picked, came,
         p_held, p_came, o_held, o_came, *sems) = refs[7:]
        pairs = [tuple(sems[2 * t : 2 * t + 2]) for t in range(10)]
        i, j = lax.axis_index("dp"), lax.axis_index("mp")
        greet({"dp": n, "mp": m}, {"dp": i, "mp": j})
        stages = line_part_stages(part, held, total, pairs[0], "mp", m, j, 0.0, 6.0)
        stages += pair_part_stages(project, p_held, p_came, project_sum.at[0], pairs[1], "dp", n, i, 0.1, 1.0)
        stages += pair_part_stages(output, o_held, o_came, output_sum.at[0], pairs[2], "dp", n, i, 0.1, 1.0)
        up_of, put_up = gather_setup([up], up_out)
        low_of, put_low = gather_setup([low], low_out)
        put_up(i)
        put_low(i)
        stages += pair_gather_stages(up_of, pairs[3], "dp", n, i, 2.0, 11.0)
        stages += pair_gather_stages(low_of, pairs[4], "dp", n, i, 2.0, 11.0)

        def back():
            mine = pl.ds(pl.multiple_of(j * share, share), share)
            stream_own = stream_ref[mine, :]
            scale = rms_scale(stream_own)
            grad = total[...]
            out[j] = (hidden_ref[...] + norm_back(stream_own, scale, gain_ref[...], grad)).astype(BF)
            gain_grad[...] = jnp.sum(stream_own * scale * grad, axis=0, keepdims=True)

        stages.append((71.0, back))
        stages += [
            (when if when < 90 else 199.0, run)
            for when, run in line_gather_stages(out, pairs[5], "mp", m, j, 72.0, 0.1)
        ]
        project_of, put_project = gather_setup([project_sum], project_out)
        output_of, put_output = gather_setup([output_sum], output_out)
        late = []

        def put_sums():
            put_project(i)
            line_held[j] = output_sum[0].astype(BF)

        def line_done():
            summed = line_held[0].astype(F32)
            for p in range(1, m):
                summed = summed + line_held[p].astype(F32)
            output_sum[0] = summed
            put_output(i)

        stages = [(60.0 if when == 80.0 else when, run) for when, run in stages]
        stages.append((72.01, put_sums))
        stages += [
            (when, run)
            for when, run in zip(
                (72.02, 72.25, 198.0),
                [run for _, run in pair_gather_stages(project_of, pairs[6], "dp", n, i, 0, 0)],
            )
        ]
        stages += direct_stages(
            lambda p: line_held.at[j], line_held, pairs[7], "mp", m, j, 72.03, line_done, 76.0
        )
        stages += [
            (when, run)
            for when, run in zip(
                (77.0, 81.5, 198.5),
                [run for _, run in pair_gather_stages(output_of, pairs[8], "dp", n, i, 0, 0)],
            )
        ]

        def pick(d):
            peer = lax.rem(i + d, n)
            rows = out[...].reshape(words, D)
            number = lax.broadcasted_iota(jnp.int32, (words, block), 0)
            picked[peer] = tn((number == row_ref[peer]).astype(BF), rows).astype(BF)
            if d:
                remote(picked.at[peer], came.at[i], pairs[9], d, "dp", peer).start()
            else:
                came[i] = picked[i]

        for d in range(n):
            stages.append((78.0 + (d - 1) % n * 0.1, functools.partial(pick, d)))

        def place():
            for d in range(1, n):
                remote(picked.at[i], came.at[i], pairs[9], d, "dp", i).wait()
            spread = spread_blocks(slot_ref[...], total_words, vectors.shape[0], width)
            vectors[...] = tn(spread, came[...].reshape(total_words, D)).astype(BF)

        stages.append((82.0, place))
        run_stages(stages)

    held_of = lambda a: pltpu.VMEM(a.shape[:1] + a.shape[2:], BF)
    results = call_remote(
        kernel,
        "stream_grads",
        6,
        [
            jax.ShapeDtypeStruct((m, share, D), BF),
            jax.ShapeDtypeStruct((1, D), F32),
            jax.ShapeDtypeStruct((slots * width, D), BF),
        ]
        + [shape for shape, _ in made],
        [
            pltpu.VMEM((2, m, share, D), BF),
            pltpu.VMEM((share, D), F32),
            pltpu.VMEM((1,) + parts[0].shape[2:], F32),
            pltpu.VMEM((1,) + parts[1].shape[2:], F32),
            pltpu.VMEM((m,) + parts[1].shape[2:], BF),
            pltpu.VMEM((n, block, D), BF),
            pltpu.VMEM((n, block, D), BF),
            held_of(parts[0]),
            held_of(parts[0]),
            held_of(parts[1]),
            held_of(parts[1]),
        ]
        + dma_sems(2 * max(n, m)) * 10,
        [
            part_one,
            stream,
            grad_hidden,
            gain.reshape(1, D),
            own_row.reshape(n, 1, block),
            to_slot,
            sums[0][None],
            sums[1][None],
        ]
        + parts,
    )
    return list(results[:3]) + [shaper(a) for (_, shaper), a in zip(made, results[3:])]


def local(
    word_inputs,
    character_embeddings,
    cotangent,
    char_count,
    word_place,
    block_home,
    documents,
    char_gain,
    word_gains,
    char_mixer,
    char_mixer_left,
    char_mixer_right,
    char_mixer_left_root,
    char_mixer_right_root,
    char_lift,
    char_lift_left,
    char_lift_right,
    char_lift_left_root,
    char_lift_right_root,
    word_project,
    word_project_left,
    word_project_right,
    word_project_left_root,
    word_project_right_root,
    word_output,
    word_output_left,
    word_output_right,
    word_output_left_root,
    word_output_right_root,
    feed_upper,
    feed_upper_left,
    feed_upper_right,
    feed_upper_left_root,
    feed_upper_right_root,
    feed_lower,
    feed_lower_left,
    feed_lower_right,
    feed_lower_left_root,
    feed_lower_right_root,
):
    slot_count, share_rows = (character_embeddings.shape[0], character_embeddings.shape[1])
    peer_count = lax.axis_size("dp")
    part_count = lax.axis_size("mp")
    owner_index = lax.axis_index("dp")
    pair_cap = -(-slot_count // peer_count)
    slot_total = peer_count * pair_cap
    rows_dev, length = (word_inputs.shape[0], word_inputs.shape[1])
    words_dev = rows_dev * length
    block_words = share_rows * part_count

    length = word_inputs.shape[1]
    own = lax.axis_index("mp").astype(jnp.int32).reshape(1)
    position = owner_index.astype(jnp.int32).reshape(1)
    peers = lax.broadcasted_iota(jnp.int32, (slot_count, peer_count), 1)
    owner_match = (block_home[:, None] == peers).astype(jnp.int32)
    earlier = (
        lax.broadcasted_iota(jnp.int32, (slot_count, slot_count), 1)
        < lax.broadcasted_iota(jnp.int32, (slot_count, slot_count), 0)
    )
    same_owner = block_home[:, None] == block_home[None, :]
    slot_rank = jnp.sum((earlier & same_owner).astype(jnp.int32), axis=1)
    slot_target = jnp.where(block_home >= 0, block_home * pair_cap + slot_rank, slot_total)
    to_slot = lax.broadcasted_iota(jnp.int32, (slot_total, slot_count), 0) == slot_target[None, :]

    sent_place = jnp.max(
        jnp.where(to_slot[:, :, None], word_place[None] + 1, 0), axis=1
    ) - 1
    char_whole, came_place, output_line = exchange(
        "gather_char",
        0,
        [
            ("gather", "dp", [char_mixer, char_lift]),
            ("swap", "dp", [sent_place.reshape(peer_count, pair_cap, block_words)]),
            ("gather", "mp", [word_output]),
        ],
    )
    came_place = came_place.reshape(slot_total, block_words)
    kind = char_kind(block_home, char_count, share_rows)
    counts = jnp.broadcast_to(
        char_count.astype(F32)[..., None], (slot_count, share_rows, 128)
    )
    word_vectors, kept, pooled, msum = char_forward(
        character_embeddings, kind, counts, char_gain, char_whole
    )

    live = jnp.max(came_place, axis=1) >= 0
    slots_before = (
        lax.broadcasted_iota(jnp.int32, (slot_total, slot_total), 1)
        < lax.broadcasted_iota(jnp.int32, (slot_total, slot_total), 0)
    )
    live_rank = jnp.sum((slots_before & live[None, :]).astype(jnp.int32), axis=1)
    live_rank = jnp.where(live, live_rank, OWNER_BLOCKS)
    to_live = lax.broadcasted_iota(jnp.int32, (OWNER_BLOCKS, slot_total), 0) == live_rank[None, :]
    live_place = jnp.max(jnp.where(to_live[:, :, None], came_place[None] + 1, 0), axis=1) - 1
    own_row = lax.dynamic_slice_in_dim(
        came_place.reshape(slot_total, part_count, share_rows), own[0], 1, 1
    ).reshape(1, -1)

    live_vectors, project_mat, upper_mat, lower_mat, output_mat = send_vectors(
        word_vectors,
        to_slot.astype(BF),
        to_live.astype(BF),
        share_rows,
        word_project.reshape((3,) + word_project.shape[2:]),
        feed_upper,
        feed_lower,
        output_line.reshape((part_count,) + word_output.shape[1:]),
    )
    place_parts = live_place.reshape(OWNER_BLOCKS, part_count, share_rows)
    place_flat = place_parts.transpose(1, 0, 2).reshape(-1)
    stream, normed_one, qkv, probs, mixed = word_forward(
        live_vectors.reshape(-1, D),
        place_flat,
        word_inputs.reshape(words_dev, D),
        documents,
        word_gains[0],
        project_mat,
    )
    mixed_all, mixer_root, lift_root = exchange(
        "gather_mixed",
        3,
        [
            ("line_gather", "mp", [mixed]),
            ("gather", "dp", [char_mixer_right_root]),
            ("gather", "dp", [char_lift_right_root]),
        ],
    )
    flat_cotangent = cotangent.reshape(words_dev, D)
    hidden, feed_part, part_two, grad_upper, grad_lower = feed(
        mixed_all, output_mat, stream, flat_cotangent, word_gains[1], upper_mat, lower_mat
    )
    shares = (part_count, words_dev // part_count, D)
    grad_hidden, grad_mixed, grad_output_mat, gain_two, part_upper, part_lower, *word_roots = hidden_grads(
        part_two.reshape(shares),
        hidden,
        flat_cotangent,
        mixed_all,
        output_mat,
        word_gains[1],
        grad_upper,
        grad_lower,
        [
            word_project_right_root.reshape((3,) + word_project_right_root.shape[2:]),
            word_output_right_root,
            feed_upper_right_root,
            feed_lower_right_root,
        ],
    )
    project_root, output_root, upper_root, lower_root = word_roots
    part_one, grad_project = word_backward(
        probs, qkv, grad_mixed.reshape(words_dev, -1), normed_one, project_mat
    )
    grad_words, gain_one, grad_vectors, sum_upper, sum_lower, sum_project, sum_output = stream_grads(
        part_one.reshape(shares),
        stream,
        grad_hidden,
        word_gains[0],
        own_row,
        to_slot.astype(BF),
        (part_upper, part_lower),
        grad_project,
        grad_output_mat,
        slot_count,
    )
    word_inputs_gradient = grad_words.reshape(word_inputs.shape)
    own_rows = word_output.shape[1] * peer_count
    sum_output = lax.dynamic_slice_in_dim(sum_output, own[0] * own_rows, own_rows, 0)
    grad_vectors, feed_part = lax.optimization_barrier((grad_vectors, feed_part))
    feed_total = lax.psum(feed_part, "mp").astype(F32)
    block_out = (hidden + feed_total).astype(BF).reshape(word_inputs.shape)
    char_embeds_gradient, char_grads, grad_char_gain = char_backward(
        character_embeddings, kind, counts, char_gain, char_whole, kept, pooled, msum, grad_vectors
    )
    small = jnp.concatenate(
        [
            jnp.pad(grad_char_gain, ((0, 0), (0, D - CHAR_BLOCK_WIDTH))),
            gain_one,
            gain_two,
            jnp.zeros((5, D), F32),
        ]
    )
    word_sums = (sum_project, sum_output, sum_upper, sum_lower)
    char_sums, small_sums = sum_char_grads(char_grads, small, word_sums)
    parameter_count = (
        sum(
            part_count * w.size * peer_count
            for w in (word_project, word_output, feed_upper, feed_lower)
        )
        + peer_count * (char_mixer.size + char_lift.size)
        + char_gain.size
        + word_gains.size
    )
    flat = lambda a: a.reshape((-1,) + a.shape[-2:])
    results = shampoo(
        0.5 * math.sqrt(parameter_count),
        position,
        char_sums,
        small_sums,
        char_gain,
        word_gains,
        word_sums,
        [
            tuple(flat(a) for a in group[:4]) + (group[4],)
            for group in (
                (char_mixer, char_mixer_left, char_mixer_right, char_mixer_left_root, mixer_root),
                (char_lift, char_lift_left, char_lift_right, char_lift_left_root, lift_root),
                (word_project, word_project_left, word_project_right, word_project_left_root, project_root),
                (word_output, word_output_left, word_output_right, word_output_left_root, output_root),
                (feed_upper, feed_upper_left, feed_upper_right, feed_upper_left_root, upper_root),
                (feed_lower, feed_lower_left, feed_lower_right, feed_lower_left_root, lower_root),
            )
        ],
    )
    norm, gain_grad, gains_grad, gain_new, gains_new = results[:5]
    stepped = []
    for t, group in enumerate(
        (
            (char_mixer, char_mixer_left, char_mixer_right),
            (char_lift, char_lift_left, char_lift_right),
            (word_project, word_project_left, word_project_right),
            (word_output, word_output_left, word_output_right),
            (feed_upper, feed_upper_left, feed_upper_right),
            (feed_lower, feed_lower_left, feed_lower_right),
        )
    ):
        master, left, right = group
        stepped += [
            a.reshape(b.shape)
            for a, b in zip(results[5 + 5 * t : 10 + 5 * t], (master, left, right, master, master))
        ]
    return (
        block_out,
        word_inputs_gradient,
        char_embeds_gradient,
        gain_grad[0],
        gains_grad,
        gain_new[0],
        gains_new,
        norm[0, 0],
        *stepped,
    )


def solution(mesh):
    placed = (
        P("dp", None, None),
        P("dp", "mp", None, None),
        P("dp", None, None),
        P("dp", "mp"),
        P("dp", None),
        P("dp"),
        P("dp", None),
        P(),
        P(),
        P(None, "dp", None),
        P(None, "dp", None),
        P(None, "dp", None),
        P(None, "dp", None),
        P(None, "dp", None),
        P(None, "dp", None),
        P(None, "dp", None),
        P(None, "dp", None),
        P(None, "dp", None),
        P(None, "dp", None),
        P(None, "mp", "dp", None),
        P(None, "mp", "dp", None),
        P(None, "mp", "dp", None),
        P(None, "mp", "dp", None),
        P(None, "mp", "dp", None),
        P("mp", "dp", None),
        P("mp", "dp", None),
        P("mp", "dp", None),
        P("mp", "dp", None),
        P("mp", "dp", None),
        P("mp", "dp", None),
        P("mp", "dp", None),
        P("mp", "dp", None),
        P("mp", "dp", None),
        P("mp", "dp", None),
        P("mp", "dp", None),
        P("mp", "dp", None),
        P("mp", "dp", None),
        P("mp", "dp", None),
        P("mp", "dp", None),
    )
    return jax.shard_map(
        local,
        mesh=mesh,
        in_specs=placed,
        out_specs=(
            P("dp", None, None),
            P("dp", None, None),
            P("dp", "mp", None, None),
            P(),
            P(),
            P(),
            P(),
            P(),
            P(None, "dp", None),
            P(None, "dp", None),
            P(None, "dp", None),
            P(None, "dp", None),
            P(None, "dp", None),
            P(None, "dp", None),
            P(None, "dp", None),
            P(None, "dp", None),
            P(None, "dp", None),
            P(None, "dp", None),
            P(None, "mp", "dp", None),
            P(None, "mp", "dp", None),
            P(None, "mp", "dp", None),
            P(None, "mp", "dp", None),
            P(None, "mp", "dp", None),
            P("mp", "dp", None),
            P("mp", "dp", None),
            P("mp", "dp", None),
            P("mp", "dp", None),
            P("mp", "dp", None),
            P("mp", "dp", None),
            P("mp", "dp", None),
            P("mp", "dp", None),
            P("mp", "dp", None),
            P("mp", "dp", None),
            P("mp", "dp", None),
            P("mp", "dp", None),
            P("mp", "dp", None),
            P("mp", "dp", None),
            P("mp", "dp", None),
        ),
        check_vma=False,
    )
```

profile of v0, /device:TPU:0, one launch (start us, length us, event | category | flops | bytes accessed | tf_op | source)
XLA Modules:
  0.0 388.3 jit_solution(10231190686060542141)
XLA Ops:
  8.3 0.9 convert_reduce_fusion.1
  9.2 1.2 compare_select_fusion.2
  14.4 13.2 %gather_char.1 = (bf16[256,1536]{1,0:T(8,128)(2,1)S(1)}, s32[8,3,128]{2,1,0:T(4,128)S(1)}, bf16[64,512]{1,0:T(8,128)(2,1)S(1)}) custom-call(f32[4,32,256]{2,1,0:T(8,128)S(1)} %copy-done.14, f32[1,32,512]{2,1,0:T(8,128)S(1)} %copy-done.22, s32[8,3,128]{2,1,0:T(4,128)S(1)} %sub.46.refs_2_, f32[1,16,512]{2,1,0:T(8,128)S(1)} %copy-done.24), custom_call_target="tpu_custom_call" | custom-call | tf_op jit(solution)/shard_map/gather_char/pallas_call | solution.py:632
  31.4 0.9 copy.92.doc_ref
  36.3 22.9 %char_forward.1 = (bf16[640,512]{1,0:T(8,128)(2,1)}, bf16[20,512,1536]{2,1,0:T(8,128)(2,1)}, bf16[640,256]{1,0:T(8,128)(2,1)}, f32[640,256]{1,0:T(8,128)}) custom-call(s32[20]{0:T(128)} %get-tuple-element.335.kind, bf16[20,512,256]{2,1,0:T(8,128)(2,1)} %bitcast.76, f32[20,32,128]{2,1,0:T(8,128)} %broadcast_in_dim.89.count_ref, f32[1,256]{1,0:T(1,128)} %bitcast.73, ...), custom_call_target="tpu_custom_call" | custom-call | flops 10737418240 | bytes 47185920 | tf_op jit(solution)/shard_map/char_forward/pallas_call | solution.py:155
  59.2 53.2 %send_vectors.1 = (bf16[4,320,512]{2,1,0:T(8,128)(2,1)}, bf16[512,384]{1,0:T(8,128)(2,1)}, bf16[512,512]{1,0:T(8,128)(2,1)}, bf16[512,512]{1,0:T(8,128)(2,1)}, bf16[4,128,512]{2,1,0:T(8,128)(2,1)}) custom-call(bf16[640,512]{1,0:T(8,128)(2,1)} %get-tuple-element.125.vec, bf16[24,20]{1,0:T(8,128)(2,1)} %get-tuple-element.332.slots.slot_ref, ...), custom_call_target="tpu_custom_call" | custom-call | tf_op jit(solution)/shard_map/send_vectors/pallas_call | solution.py:1205
  112.4 1.0 copy-done.5
  113.5 1.3 copy-done.7
  114.8 10.3 %word_forward.1 = (f32[1024,512]{1,0:T(8,128)}, bf16[1024,512]{1,0:T(8,128)(2,1)S(1)}, bf16[1024,384]{1,0:T(8,128)(2,1)S(1)}, bf16[2,1024,1024]{2,1,0:T(8,128)(2,1)}, bf16[1024,128]{1,0:T(8,128)(2,1)S(1)}) custom-call(bf16[1280,512]{1,0:T(8,128)(2,1)S(1)} %bitcast.49, s32[1,1280]{1,0:T(1,128)S(1)} %reshape_reshape.9.place_ref, ...), custom_call_target="tpu_custom_call" | custom-call | tf_op jit(solution)/shard_map/word_forward/pallas_call | solution.py:803
  125.1 24.2 %gather_mixed.1 = (bf16[4,1024,128]{2,1,0:T(8,128)(2,1)S(1)}, bf16[256,1024]{1,0:T(8,128)(2,1)S(1)}, bf16[512,512]{1,0:T(8,128)(2,1)S(1)}) custom-call(bf16[1024,128]{1,0:T(8,128)(2,1)S(1)} %get-tuple-element.130.refs_0_, f32[4,32,256]{2,1,0:T(8,128)S(1)} %copy-done.25, f32[1,64,512]{2,1,0:T(8,128)S(1)} %copy-done.26), custom_call_target="tpu_custom_call" | custom-call | tf_op jit(solution)/shard_map/gather_mixed/pallas_call | solution.py:632
  150.0 9.8 %feed.1 = (f32[1024,512]{1,0:T(8,128)}, bf16[1024,512]{1,0:T(8,128)(2,1)}, bf16[1024,512]{1,0:T(8,128)(2,1)S(1)}, bf16[512,512]{1,0:T(8,128)(2,1)S(1)}, bf16[512,512]{1,0:T(8,128)(2,1)S(1)}) custom-call(bf16[4,1024,128]{2,1,0:T(8,128)(2,1)S(1)} %get-tuple-element.131.mixed_ref.mix, bf16[512,512]{1,0:T(8,128)(2,1)S(1)} %bitcast.48, ...), custom_call_target="tpu_custom_call" | custom-call | tf_op jit(solution)/shard_map/feed/pallas_call | solution.py:884
  159.9 1.0 copy-done.9
  162.4 41.2 %hidden_grads.1 = (f32[256,512]{1,0:T(8,128)}, bf16[4,256,128]{2,1,0:T(8,128)(2,1)}, bf16[512,512]{1,0:T(8,128)(2,1)}, f32[1,512]{1,0:T(1,128)}, f32[64,512]{1,0...) custom-call(bf16[4,256,512]{2,1,0:T(8,128)(2,1)} %bitcast.50, ...), custom_call_target="tpu_custom_call" | custom-call | tf_op jit(solution)/shard_map/hidden_grads/pallas_call | solution.py:1205
  203.6 0.9 copy-done.23
  204.6 8.7 %word_backward.1 = (bf16[1024,512]{1,0:T(8,128)(2,1)S(1)}, bf16[512,384]{1,0:T(8,128)(2,1)S(1)}) custom-call(bf16[2,1024,1024]{2,1,0:T(8,128)(2,1)} %get-tuple-element.137.probs_ref, bf16[1024,384]{1,0:T(8,128)(2,1)S(1)} %get-tuple-element.138.qkv_ref.all_ref, bf16[1024,384]{1,0:T(8,128)(2,1)S(1)} %get-tuple-element.138.qkv_ref.all_ref, ...), custom_call_target="tpu_custom_call" | custom-call | tf_op jit(solution)/shard_map/word_backward/pallas_call | solution.py:1014
  213.3 1.0 copy-done.11
  215.0 77.6 %stream_grads.1 = (bf16[4,256,512]{2,1,0:T(8,128)(2,1)}, f32[1,512]{1,0:T(1,128)}, bf16[640,512]{1,0:T(8,128)(2,1)}, bf16[512,512]{1,0:T(8,128)(2,1)}, bf16[512,...) custom-call(bf16[4,256,512]{2,1,0:T(8,128)(2,1)} %bitcast.52, ...), custom_call_target="tpu_custom_call" | custom-call | tf_op jit(solution)/shard_map/stream_grads/pallas_call | solution.py:1205
  293.6 29.3 %char_backward.1 = (bf16[20,512,256]{2,1,0:T(8,128)(2,1)}, bf16[256,1536]{1,0:T(8,128)(2,1)}, f32[1,256]{1,0:T(1,128)}) custom-call(s32[20]{0:T(128)} %get-tuple-element.335.kind, bf16[20,512,256]{2,1,0:T(8,128)(2,1)} %bitcast.77, f32[20,32,128]{2,1,0:T(8,128)} %broadcast_in_dim.89.count_ref, bf16[20,512,1536]{2,1,0:T(8,128)(2,1)} %get-tuple-element.154.kept_ref, ...), custom_call_target="tpu_custom_call" | custom-call | flops 18790481920 | bytes 47185920 | tf_op jit(solution)/shard_map/char_backward/pallas_call | solution.py:290
  323.0 0.9 constant_dynamic-slice_fusion.refs_1_
  324.7 1.1 copy-done.13
  325.9 39.8 %sum_char_grads.1 = (bf16[256,1536]{1,0:T(8,128)(2,1)S(1)}, f32[8,512]{1,0:T(8,128)S(1)}) custom-call(bf16[4,2,32,1536]{3,2,1,0:T(8,128)(2,1)S(1)} %bitcast.53, f32[8,512]{1,0:T(8,128)S(1)} %fusion.5.s, bf16[512,384]{1,0:T(8,128)(2,1)S(1)} %copy-done.4, bf16[128,512]{1,0:T(8,128)(2,1)S(1)} %constant_dynamic-slice_fusion.refs_1_, ...), custom_call_target="tpu_custom_call" | custom-call | tf_op jit(solution)/shard_map/sum_char_grads/pallas_call | solution.py:719
  367.2 10.4 %shampoo.1 = (f32[1,1]{1,0:T(1,128)}, f32[1,256]{1,0:T(1,128)}, f32[2,512]{1,0:T(2,128)}, f32[1,256]{1,0:T(1,128)}, f32[2,512]{1,0:T(2,128)}, /*index=5*/f32[4,3...) custom-call(s32[1]{0:T(128)} %bitcast.23.position, ...), custom_call_target="tpu_custom_call" | custom-call | tf_op jit(solution)/shard_map/shampoo/pallas_call | solution.py:1148
  377.7 2.6 fusion
  380.3 1.0 copy.100
  (112 shorter events, 19.3 us)
Async XLA Ops:
  7.2 370.4 %all-reduce.3.cloned.1.call-start = ((), (), s32[]{:S(2)}) async-start(), calls=%async_computation | async-start | bytes 2097152 | tf_op jit(solution)/shard_map/psum | solution.py:1667
  31.4 81.0 %copy-start.29 = (f32[1,512]{1,0:T(1,128)}, f32[1,512]{1,0:T(1,128)S(1)}, u32[]{:S(2)}) copy-start(f32[1,512]{1,0:T(1,128)S(1)} %get-tuple-element.329.gain_ref) | copy-start | bytes 6148
  31.4 118.6 %copy-start.28 = (f32[1,512]{1,0:T(1,128)}, f32[1,512]{1,0:T(1,128)S(1)}, u32[]{:S(2)}) copy-start(f32[1,512]{1,0:T(1,128)S(1)} %get-tuple-element.328.gain_ref) | copy-start | bytes 6148
  36.3 76.1 %copy-start.10 = (bf16[1,1024,512]{2,1,0:T(8,128)(2,1)S(1)}, bf16[1,1024,512]{2,1,0:T(8,128)(2,1)}, u32[]{:S(2)}) copy-start(bf16[1,1024,512]{2,1,0:T(8,128)(2,1)} %param.39) | copy-start | bytes 3145732
  36.3 76.1 %copy-start.31 = (s32[1,1024]{1,0:T(1,128)S(1)}, s32[1,1024]{1,0:T(1,128)}, u32[]{:S(2)}) copy-start(s32[1,1024]{1,0:T(1,128)} %doc_row_ref.1) | copy-start | bytes 12292
  59.2 65.9 %copy-start.25 = (f32[4,32,256]{2,1,0:T(8,128)S(1)}, f32[4,32,256]{2,1,0:T(8,128)}, u32[]{:S(2)}) copy-start(f32[4,32,256]{2,1,0:T(8,128)} %refs_1_.6) | copy-start | bytes 393220
  59.2 65.9 %copy-start.26 = (f32[1,64,512]{2,1,0:T(8,128)S(1)}, f32[1,64,512]{2,1,0:T(8,128)}, u32[]{:S(2)}) copy-start(f32[1,64,512]{2,1,0:T(8,128)} %refs_2_.4) | copy-start | bytes 393220
  112.4 37.6 %copy-start.3 = (bf16[4,128,512]{2,1,0:T(8,128)(2,1)S(1)}, bf16[4,128,512]{2,1,0:T(8,128)(2,1)}, u32[]{:S(2)}) copy-start(bf16[4,128,512]{2,1,0:T(8,128)(2,1)} %get-tuple-element.132) | copy-start | bytes 1572868
  112.4 1.0 copy-start.5
  113.5 1.3 copy-start.7
  114.8 35.2 %copy-start.19 = (bf16[512,512]{1,0:T(8,128)(2,1)S(1)}, bf16[512,512]{1,0:T(8,128)(2,1)}, u32[]{:S(2)}) copy-start(bf16[512,512]{1,0:T(8,128)(2,1)} %get-tuple-element.134.upper_ref) | copy-start | bytes 1572868
  114.8 35.2 %copy-start.20 = (bf16[512,512]{1,0:T(8,128)(2,1)S(1)}, bf16[512,512]{1,0:T(8,128)(2,1)}, u32[]{:S(2)}) copy-start(bf16[512,512]{1,0:T(8,128)(2,1)} %get-tuple-element.135.lower_ref) | copy-start | bytes 1572868
  150.0 9.8 %copy-start = (bf16[4,1024,128]{2,1,0:T(8,128)(2,1)}, bf16[4,1024,128]{2,1,0:T(8,128)(2,1)S(1)}, u32[]{:S(2)}) copy-start(bf16[4,1024,128]{2,1,0:T(8,128)(2,1)S(1)} %get-tuple-element.131.mixed_ref.mix) | copy-start | bytes 3145732
  150.0 9.8 %copy-start.16 = (bf16[512,512]{1,0:T(8,128)(2,1)}, bf16[512,512]{1,0:T(8,128)(2,1)S(1)}, u32[]{:S(2)}) copy-start(bf16[512,512]{1,0:T(8,128)(2,1)S(1)} %get-tuple-element.170.refs_13_) | copy-start | bytes 1572868
  162.4 41.2 %copy-start.6 = (bf16[512,384]{1,0:T(8,128)(2,1)S(1)}, bf16[512,384]{1,0:T(8,128)(2,1)}, u32[]{:S(2)}) copy-start(bf16[512,384]{1,0:T(8,128)(2,1)} %get-tuple-element.129.project_ref) | copy-start | bytes 1179652
  293.6 30.3 %copy-start.35 = (f32[1,512]{1,0:T(1,128)S(1)}, f32[1,512]{1,0:T(1,128)}, u32[]{:S(2)}) copy-start(f32[1,512]{1,0:T(1,128)} %get-tuple-element.162) | copy-start | bytes 6148
  293.6 30.4 %copy-start.36 = (f32[1,512]{1,0:T(1,128)S(1)}, f32[1,512]{1,0:T(1,128)}, u32[]{:S(2)}) copy-start(f32[1,512]{1,0:T(1,128)} %get-tuple-element.161) | copy-start | bytes 6148
  293.6 31.2 %copy-start.1 = (bf16[512,512]{1,0:T(8,128)(2,1)S(1)}, bf16[512,512]{1,0:T(8,128)(2,1)}, u32[]{:S(2)}) copy-start(bf16[512,512]{1,0:T(8,128)(2,1)} %get-tuple-element.165.refs_2_) | copy-start | bytes 1572868
  293.6 31.2 %copy-start.2 = (bf16[512,512]{1,0:T(8,128)(2,1)S(1)}, bf16[512,512]{1,0:T(8,128)(2,1)}, u32[]{:S(2)}) copy-start(bf16[512,512]{1,0:T(8,128)(2,1)} %get-tuple-element.166.refs_3_) | copy-start | bytes 1572868
  293.6 31.1 %copy-start.4 = (bf16[512,384]{1,0:T(8,128)(2,1)S(1)}, bf16[512,384]{1,0:T(8,128)(2,1)}, u32[]{:S(2)}) copy-start(bf16[512,384]{1,0:T(8,128)(2,1)} %get-tuple-element.163.refs_0_) | copy-start | bytes 1179652
  323.9 43.3 %copy-start.8 = (bf16[128,512]{1,0:T(8,128)(2,1)}, bf16[128,512]{1,0:T(8,128)(2,1)S(1)}, u32[]{:S(2)}) copy-start(bf16[128,512]{1,0:T(8,128)(2,1)S(1)} %constant_dynamic-slice_fusion.refs_1_) | copy-start | bytes 393220
  324.7 1.1 copy-start.13
  367.2 10.4 %copy-start.33 = (f32[1024,512]{1,0:T(8,128)S(1)}, f32[1024,512]{1,0:T(8,128)}, u32[]{:S(2)}) copy-start(f32[1024,512]{1,0:T(8,128)} %get-tuple-element.136.hidden_ref) | copy-start | bytes 6291460
  377.6 2.7 copy-start.34
  (14 other events, 11.5 us)
Sparse Core Ops, SparseCore 0:
  292.7 51.3 all-reduce.2
where the time goes:
time: 393 us; the launch traced here: 388 us
  Pallas kernels  340 us (87%)
  local copies, waits for them, and re-layouts  21.7 us (6%)
  between operations  14.7 us (4%)
  other arithmetic  11.4 us (3%)
    pallas_call x3, Pallas kernels, call_remote(): pl.pallas_call(kernel, out_shape=outs, in_specs=[vmem] * len(inputs), out...  172 us
    pallas_call x1, Pallas kernels, sum_char_grads(): pl.pallas_call(kernel, out_shape=[jax.ShapeDtypeStruct((n * rows, cols) i...  39.8 us
    pallas_call x2, Pallas kernels, exchange(): pl.pallas_call(kernel, out_shape=outs, in_specs=[vmem] * total_ins, out_s...  37.3 us
    pallas_call x1, Pallas kernels, char_backward(): pl.pallas_call(functools.partial(char_backward_kernel, classes), grid_spe...  29.3 us
    pallas_call x1, Pallas kernels, char_forward(): pl.pallas_call(functools.partial(char_forward_kernel, classes), grid_spec...  22.9 us
    unnamed x75, local copies, waits for them, and re-layouts  16 us
    pallas_call x1, Pallas kernels, shampoo(): pl.pallas_call(functools.partial(shampoo_kernel, threshold), in_specs=[sm...  10.4 us
    pallas_call x1, Pallas kernels, word_forward(): pl.pallas_call(functools.partial(word_forward_kernel, width), grid=(lengt...  10.3 us
  transfers between devices with their start and end apart: 1, of which 0 were waited for; matrix products, arithmetic and copies ran while one was open for 1% of the time, Pallas kernels for 20%

commit v1 on v0

--- a/solution.py
+++ b/solution.py
@@ -40,9 +40,12 @@
     return lax.dot_general(a, b, (((0,), (0,)), ((), ())), preferred_element_type=F32)
 
 
+GROUPS = 4
+
+
 def char_classes(share):
     listed = [(1, 4, 32), (2, 8, 16), (4, 16, 8)]
-    return [c for c in listed if c[2] <= share]
+    return [(c, p, w, GROUPS // (share // w)) for c, p, w in listed if w <= share]
 
 
 def order_matrix(places, words):
@@ -59,41 +62,42 @@
 
 
 def char_forward_kernel(
-    classes, kind, x_ref, count_ref, gain_ref, mats_ref, *refs
+    classes, home, first, x_ref, counts_in, gain_ref, mats_ref, *refs
 ):
-    orders = refs[: len(classes)]
-    vec_ref, kept_ref, pooled_ref, msum_ref, sumx, counts = refs[len(classes) :]
-    step = pl.program_id(0)
-    share = count_ref.shape[1]
-    own = pl.ds(pl.multiple_of(step * share, share), share)
-    counts[own, :] = count_ref[0]
-
-    @pl.when(kind[step] == 0)
-    def _():
-        sumx[own, :] = jnp.zeros((share, CW), F32)
-        msum_ref[own, :] = jnp.zeros((share, CW), F32)
-
-    def block(places, words, order_ref):
-        groups = share // words
-        kept_x = []
-        normed = []
-        for g in range(groups):
-            x = nn(order_ref[...], x_ref[0, pl.ds(g * words * SPOTS, words * SPOTS), :])
-            scale = lax.rsqrt(jnp.mean(x * x, axis=-1, keepdims=True) + epsilon)
-            normed.append((x * scale * gain_ref[...]).astype(BF))
-            cnt = count_ref[0, pl.ds(g * words, words), :]
-            cnt2 = jnp.concatenate([cnt, cnt], axis=1)
-            place = lax.broadcasted_iota(jnp.int32, (places, words, CW), 0).astype(F32)
-            x3 = x.reshape(places, words, CW)
-            sumx[pl.ds(pl.multiple_of(step * share + g * words, words), words), :] = jnp.sum(
-                jnp.where(place < cnt2[None], x3, 0.0), axis=0
-            )
-        rows = groups * 128
-        normed = jnp.concatenate(normed, axis=0) if groups > 1 else normed[0]
-        for t in range(3):
-            kept_ref[0, :rows, t * CW : (t + 1) * CW] = nn(
-                normed, mats_ref[:, t * CW : (t + 1) * CW]
-            ).astype(BF)
+    orders, refs = refs[-len(classes) :], refs[: -len(classes)]
+    vec_ref, kept_out, pooled_ref, msum_ref, kept, sumx, count_ref, kind, ids, batch_kind, sems = refs
+    slots, share = count_ref.shape[:2]
+    batches = plan_batches(classes, home, first, kind, ids, batch_kind)
+    count_ref[...] = spread_counts(counts_in[...]).reshape(count_ref.shape)
+    for (_, places, words, _), order_ref in zip(classes, orders):
+        order_ref[...] = order_matrix(places, words)
+    sumx[...] = jnp.zeros_like(sumx)
+    msum_ref[...] = jnp.zeros_like(msum_ref)
+
+    def save(slot, rows):
+        return pltpu.make_async_copy(
+            kept.at[slot, pl.ds(0, rows)], kept_out.at[slot, pl.ds(0, rows)], sems.at[slot]
+        )
+
+    def block(places, words, per, order_ref, number):
+        chosen = [ids[number * GROUPS + t] for t in range(per)]
+        chosen = [jnp.where(c < 0, chosen[0], c) for c in chosen]
+        groups = [(c, g) for c in chosen for g in range(share // words)]
+        cnts = [count_ref[c, pl.ds(g * words, words), :] for c, g in groups]
+        xs = [
+            nn(order_ref[...], x_ref[c, pl.ds(g * words * SPOTS, words * SPOTS), :]) for c, g in groups
+        ]
+        normed = jnp.concatenate(
+            [
+                (
+                    x * lax.rsqrt(jnp.mean(x * x, axis=-1, keepdims=True) + epsilon) * gain_ref[...]
+                ).astype(BF)
+                for x in xs
+            ],
+            axis=0,
+        )
+        qkv = nn(normed, mats_ref[:, : 3 * CW]).astype(BF)
+        place = lax.broadcasted_iota(jnp.int32, (places, words, CW), 0).astype(F32)
         lane = lax.broadcasted_iota(jnp.int32, (words, CHEADS * 128), 1) % 128
         word = lax.broadcasted_iota(jnp.int32, (words, CHEADS * 128), 0)
         mine = lane % words == word
@@ -101,235 +105,363 @@
         head_row = lax.broadcasted_iota(jnp.int32, (CHEADS * 128, CW), 0) // 128
         head_col = lax.broadcasted_iota(jnp.int32, (CHEADS * 128, CW), 1) // CHD
         same_head = (head_row == head_col).astype(BF)
-        for g in range(groups):
-            at = g * 128
-            q = kept_ref[0, at : at + 128, :CW]
-            k = kept_ref[0, at : at + 128, CW : 2 * CW]
-            v = kept_ref[0, at : at + 128, 2 * CW : 3 * CW]
-            s = nt(k, head_stack(q, 1.0 / math.sqrt(CHD))).reshape(places, words, CHEADS * 128)
-            cnt = count_ref[0, pl.ds(g * words, words), :]
-            cnt4 = jnp.concatenate([cnt] * CHEADS, axis=1)
-            place = lax.broadcasted_iota(jnp.int32, (places, words, CHEADS * 128), 0).astype(F32)
-            s = jnp.where(place < cnt4[None], s, -1e30)
+        far = lax.broadcasted_iota(jnp.int32, (places, words, CHEADS * 128), 0).astype(F32)
+        scores = []
+        for t in range(GROUPS):
+            rows = qkv[t * 128 : (t + 1) * 128]
+            scores.append(nt(rows[:, CW : 2 * CW], head_stack(rows[:, :CW], 1.0 / math.sqrt(CHD))))
+        sums = []
+        for t in range(GROUPS):
+            shown = place < jnp.concatenate([cnts[t], cnts[t]], axis=1)[None]
+            sums.append(jnp.sum(jnp.where(shown, xs[t].reshape(places, words, CW), 0.0), axis=0))
+        probs = []
+        for t in range(GROUPS):
+            cnt4 = jnp.concatenate([cnts[t]] * CHEADS, axis=1)
+            s = jnp.where(far < cnt4[None], scores[t].reshape(places, words, CHEADS * 128), -1e30)
             e = jnp.exp(s - jnp.max(s, axis=0)[None])
             r = jnp.where(mine & (spot < cnt4), 1.0 / jnp.sum(e, axis=0), 0.0)
-            p = (e * r[None]).astype(BF).reshape(128, CHEADS * 128)
-            kept_ref[0, at : at + 128, 3 * CW : 3 * CW + CHEADS * 128] = p
-            c = nn(p, same_head)
-            kept_ref[0, at : at + 128, 3 * CW + CHEADS * 128 :] = c.astype(BF)
-            msum_ref[pl.ds(pl.multiple_of(step * share + g * words, words), words), :] = jnp.sum(
-                (c * v.astype(F32)).reshape(places, words, CW), axis=0
+            probs.append((e * r[None]).astype(BF).reshape(128, CHEADS * 128))
+        columns = [nn(p, same_head) for p in probs]
+        for t, (c, g) in enumerate(groups):
+            rows = qkv[t * 128 : (t + 1) * 128]
+            at = pl.ds(g * 128, 128)
+            kept[c, at, : 3 * CW] = rows
+            kept[c, at, 3 * CW : 3 * CW + CHEADS * 128] = probs[t]
+            kept[c, at, 3 * CW + CHEADS * 128 :] = columns[t].astype(BF)
+            own = pl.ds(pl.multiple_of(c * share + g * words, words), words)
+            msum_ref[own, :] = jnp.sum(
+                (columns[t] * rows[:, 2 * CW :].astype(F32)).reshape(places, words, CW), axis=0
             )
-
-    for (number, places, words), order_ref in zip(classes, orders):
-        pl.when(kind[step] == number)(functools.partial(block, places, words, order_ref))
-
-    @pl.when(step == pl.num_programs(0) - 1)
-    def _():
-        cnt2 = jnp.concatenate([counts[...]] * 2, axis=1)
-        summed = sumx[...] + nn(msum_ref[...].astype(BF), mats_ref[:, 3 * CW : 4 * CW])
-        pooled = (summed / cnt2).astype(BF)
-        pooled_ref[...] = pooled
-        vec_ref[...] = nn(pooled, mats_ref[:, 4 * CW :]).astype(BF)
-
-
-def char_kind(block_home, char_count, share):
-    places = jnp.max(char_count, axis=1)
-    kind = jnp.where(places <= 8, 2, 4)
-    if share >= 32:
-        kind = jnp.where(places <= 4, 1, kind)
-    return jnp.where(block_home >= 0, kind, 0).astype(jnp.int32)
-
-
-def whole(shape):
-    return pl.BlockSpec(shape, lambda i, *_: (0,) * len(shape))
-
-
-def char_forward(x, kind, counts, gain, mats):
+            sumx[own, :] = sums[t]
+        for t in range(per):
+            slot = ids[number * GROUPS + t]
+
+            @pl.when(slot >= 0)
+            def _(slot=slot):
+                save(slot, share * places).start()
+
+    def batch(number, carry):
+        for (which, places, words, per), order_ref in zip(classes, orders):
+            pl.when(batch_kind[number] == which)(
+                functools.partial(block, places, words, per, order_ref, number)
+            )
+        return carry
+
+    lax.fori_loop(0, batches, batch, 0)
+    cnt2 = jnp.concatenate([count_ref[...].reshape(slots * share, 128)] * 2, axis=1)
+    summed = sumx[...] + nn(msum_ref[...].astype(BF), mats_ref[:, 3 * CW : 4 * CW])
+    pooled = (summed / cnt2).astype(BF)
+    pooled_ref[...] = pooled
+    vec_ref[...] = nn(pooled, mats_ref[:, 4 * CW :]).astype(BF)
+
+    def finish(slot, carry):
+        for which, places, words, per in classes:
+
+            @pl.when(kind[slot] == which)
+            def _(places=places):
+                save(slot, share * places).wait()
+
+        return carry
+
+    lax.fori_loop(0, slots, finish, 0)
+
+
+def plan_batches(classes, home, count, kind, ids, batch_kind):
+    slots = home.shape[0]
+    coarse = classes[0][0] == 1
+
+    def sort(slot, carry):
+        places = count[slot, 0]
+        which = jnp.where(places <= 8, 2, 4)
+        if coarse:
+            which = jnp.where(places <= 4, 1, which)
+        kind[slot] = jnp.where(home[slot] >= 0, which, 0)
+        for t in range(GROUPS):
+            ids[slot * GROUPS + t] = -1
+        return carry
+
+    lax.fori_loop(0, slots, sort, 0)
+    batch = jnp.int32(0)
+    for which, _, _, per in classes:
+
+        def take(slot, carry):
+            batch, place = carry
+            hit = kind[slot] == which
+
+            @pl.when(hit)
+            def _():
+                ids[batch * GROUPS + place] = slot
+                batch_kind[batch] = which
+
+            place = jnp.where(hit, place + 1, place)
+            full = place == per
+            return jnp.where(full, batch + 1, batch), jnp.where(full, 0, place)
+
+        batch, place = lax.fori_loop(0, slots, take, (batch, jnp.int32(0)))
+        batch = jnp.where(place > 0, batch + 1, batch)
+    return batch
+
+
+def spread_counts(count):
+    slots, share = count.shape
+    row = lax.broadcasted_iota(jnp.int32, (slots * share, slots), 0) // share
+    pick = (row == lax.broadcasted_iota(jnp.int32, (slots * share, slots), 1)).astype(BF)
+    wide = nn(pick, count.astype(F32).astype(BF))
+    mine = lax.broadcasted_iota(jnp.int32, (slots * share, share), 0) % share
+    mine = mine == lax.broadcasted_iota(jnp.int32, (slots * share, share), 1)
+    return nn(jnp.where(mine, wide, 0.0).astype(BF), jnp.ones((share, 128), BF))
+
+
+def char_call(kernel, name, inputs, scalars, outs, scratch, in_hbm, out_hbm, flops, limit):
+    vmem = pl.BlockSpec(memory_space=pltpu.VMEM)
+    smem = pl.BlockSpec(memory_space=pltpu.SMEM)
+    hbm = pl.BlockSpec(memory_space=pltpu.HBM)
+    return pl.pallas_call(
+        kernel,
+        in_specs=[smem] * len(scalars) + [hbm if t in in_hbm else vmem for t in range(len(inputs))],
+        out_specs=[hbm if t in out_hbm else vmem for t in range(len(outs))],
+        out_shape=outs,
+        scratch_shapes=scratch,
+        cost_estimate=pl.CostEstimate(flops=flops, bytes_accessed=60 << 20, transcendentals=0),
+        compiler_params=pltpu.CompilerParams(vmem_limit_bytes=limit << 20),
+        name=name,
+    )(*scalars, *inputs)
+
+
+def plan_scratch(slots, share):
+    return [
+        pltpu.VMEM((slots, share, 128), F32),
+        pltpu.SMEM((slots,), jnp.int32),
+        pltpu.SMEM((slots * GROUPS,), jnp.int32),
+        pltpu.SMEM((slots,), jnp.int32),
+    ]
+
+
+def char_forward(x, home, counts, gain, mats):
     slots, share = x.shape[:2]
     classes = char_classes(share)
     rows = share * SPOTS
-    orders = [order_matrix(p, w) for _, p, w in classes]
+    orders = [pltpu.VMEM((128, SPOTS * c[2]), BF) for c in classes]
     words_all = slots * share
-    per_slot = lambda shape: pl.BlockSpec((1,) + shape, lambda i, *_: (i,) + (0,) * len(shape))
-    return pl.pallas_call(
+    return char_call(
         functools.partial(char_forward_kernel, classes),
-        grid_spec=pltpu.PrefetchScalarGridSpec(
-            num_scalar_prefetch=1,
-            grid=(slots,),
-            in_specs=[
-                per_slot((rows, CW)),
-                per_slot((share, 128)),
-                whole((1, CW)),
-                whole(mats.shape),
-            ]
-            + [whole(o.shape) for o in orders],
-            out_specs=[
-                whole((words_all, D)),
-                per_slot((rows, KEPT)),
-                whole((words_all, CW)),
-                whole((words_all, CW)),
-            ],
-            scratch_shapes=[
-                pltpu.VMEM((words_all, CW), F32),
-                pltpu.VMEM((words_all, 128), F32),
-            ],
-        ),
-        out_shape=[
+        "char_forward",
+        [x.reshape(slots, rows, CW), counts, gain.reshape(1, CW), mats],
+        (home, counts),
+        [
             jax.ShapeDtypeStruct((words_all, D), BF),
             jax.ShapeDtypeStruct((slots, rows, KEPT), BF),
             jax.ShapeDtypeStruct((words_all, CW), BF),
             jax.ShapeDtypeStruct((words_all, CW), F32),
         ],
-        compiler_params=pltpu.CompilerParams(vmem_limit_bytes=60 << 20),
-        cost_estimate=pl.CostEstimate(
-            flops=slots * rows * CW * CW * 16, bytes_accessed=slots * rows * KEPT * 3, transcendentals=0
-        ),
-        name="char_forward",
-    )(kind, x.reshape(slots, rows, CW), counts, gain.reshape(1, CW), mats, *orders)
+        [
+            pltpu.VMEM((slots, rows, KEPT), BF),
+            pltpu.VMEM((words_all, CW), F32),
+        ]
+        + plan_scratch(slots, share)
+        + [pltpu.SemaphoreType.DMA((slots,))]
+        + orders,
+        (),
+        (1,),
+        slots * rows * CW * CW * 16,
+        46,
+    )
 
 
 def char_backward_kernel(
-    classes, kind, x_ref, count_ref, kept_ref, all_counts_ref, gv_ref, pooled_ref, msum_ref,
-    gain_ref, mats_ref, *refs
+    classes, home, first, x_in, counts_in, kept_in, gv_ref, pooled_ref, msum_ref, gain_ref, mats_ref, *refs
 ):
-    orders = refs[: len(classes)]
-    dx_ref, grads_ref, dgain_ref, gp_all, gm_all, dh, normed_all, dqkv_sum = refs[len(classes) :]
-    step = pl.program_id(0)
-    share = count_ref.shape[1]
-    base = step * share
-
-    @pl.when(step == 0)
-    def _():
-        gv = gv_ref[...]
-        cnt2 = jnp.concatenate([all_counts_ref[...]] * 2, axis=1)
-        gp = nt(gv, mats_ref[:, 4 * CW :]) / cnt2
-        gp_all[...] = gp
-        gpb = gp.astype(BF)
-        gm_all[...] = nt(gpb, mats_ref[:, 3 * CW : 4 * CW]).astype(BF).astype(F32)
-        grads_ref[:, 4 * CW :] = tn(pooled_ref[...], gv).astype(BF)
-        grads_ref[:, 3 * CW : 4 * CW] = tn(msum_ref[...].astype(BF), gpb).astype(BF)
-        dqkv_sum[...] = jnp.zeros_like(dqkv_sum)
-        dgain_ref[...] = jnp.zeros_like(dgain_ref)
-
-    @pl.when(kind[step] == 0)
-    def _():
-        dx_ref[...] = jnp.zeros_like(dx_ref)
-
-    def block(places, words, order_ref):
-        groups = share // words
-        rows = groups * 128
+    orders, refs = refs[-len(classes) :], refs[: -len(classes)]
+    dx_out, grads_ref, dgain_ref, x_ref, kept, dx_ref, gp_all, gm_all, dqkv_sum, count_ref = refs[:10]
+    kind, ids, batch_kind, x_sems, kept_sems, dx_sems = refs[10:]
+    slots, share = count_ref.shape[:2]
+    batches = plan_batches(classes, home, first, kind, ids, batch_kind)
+
+    def load_x(slot):
+        return pltpu.make_async_copy(x_in.at[slot], x_ref.at[slot], x_sems.at[slot])
+
+    def load_kept(slot, rows):
+        return pltpu.make_async_copy(
+            kept_in.at[slot, pl.ds(0, rows)], kept.at[slot, pl.ds(0, rows)], kept_sems.at[slot]
+        )
+
+    def save(slot):
+        return pltpu.make_async_copy(dx_ref.at[slot], dx_out.at[slot], dx_sems.at[slot])
+
+    def begin(number, carry):
+        for which, places, words, per in classes:
+
+            @pl.when(batch_kind[number] == which)
+            def _(places=places, per=per):
+                for t in range(per):
+                    slot = ids[number * GROUPS + t]
+
+                    @pl.when(slot >= 0)
+                    def _(slot=slot):
+                        load_x(slot).start()
+                        load_kept(slot, share * places).start()
+
+        return carry
+
+    lax.fori_loop(0, batches, begin, 0)
+
+    count_ref[...] = spread_counts(counts_in[...]).reshape(count_ref.shape)
+    for (_, places, words, _), order_ref in zip(classes, orders):
+        order_ref[...] = order_matrix(places, words)
+    gv = gv_ref[...]
+    cnt2 = jnp.concatenate([count_ref[...].reshape(slots * share, 128)] * 2, axis=1)
+    gp = nt(gv, mats_ref[:, 4 * CW :]) / cnt2
+    gp_all[...] = gp
+    gpb = gp.astype(BF)
+    gm_all[...] = nt(gpb, mats_ref[:, 3 * CW : 4 * CW]).astype(BF).astype(F32)
+    grads_ref[:, 4 * CW :] = tn(pooled_ref[...], gv).astype(BF)
+    grads_ref[:, 3 * CW : 4 * CW] = tn(msum_ref[...].astype(BF), gpb).astype(BF)
+    dqkv_sum[...] = jnp.zeros_like(dqkv_sum)
+    dgain_ref[...] = jnp.zeros_like(dgain_ref)
+
+    def block(places, words, per, order_ref, number):
+        picked = [ids[number * GROUPS + t] for t in range(per)]
+        chosen = [jnp.where(c < 0, picked[0], c) for c in picked]
+        weights = [jnp.where(c < 0, 0.0, 1.0) for c in picked]
+        targets = [jnp.where(c < 0, slots, c) for c in picked]
+        for slot in picked:
+
+            @pl.when(slot >= 0)
+            def _(slot=slot):
+                load_x(slot).wait()
+                load_kept(slot, share * places).wait()
+
+        groups = [
+            (c, g, weight, target)
+            for c, weight, target in zip(chosen, weights, targets)
+            for g in range(share // words)
+        ]
         gain = gain_ref[...]
-        xs = []
-        scales = []
-        gps = []
-        for g in range(groups):
-            at = g * 128
-            x = nn(order_ref[...], x_ref[0, pl.ds(g * words * SPOTS, words * SPOTS), :])
-            scale = lax.rsqrt(jnp.mean(x * x, axis=-1, keepdims=True) + epsilon)
-            normed_all[at : at + 128, :] = (x * scale * gain).astype(BF)
-            xs.append(x)
-            scales.append(scale)
-            mine = pl.ds(pl.multiple_of(base + g * words, words), words)
-            cnt = count_ref[0, pl.ds(g * words, words), :]
-            cnt2 = jnp.concatenate([cnt, cnt], axis=1)
-            place = lax.broadcasted_iota(jnp.int32, (places, words, CW), 0).astype(F32)
-            shown = place < cnt2[None]
-            gps.append(jnp.where(shown, gp_all[mine, :][None], 0.0).reshape(128, CW))
-            gm_word = gm_all[mine, :]
-            gm = jnp.where(shown, gm_word[None], 0.0).reshape(128, CW).astype(BF)
-            q = kept_ref[0, at : at + 128, :CW]
-            k = kept_ref[0, at : at + 128, CW : 2 * CW]
-            v = kept_ref[0, at : at + 128, 2 * CW : 3 * CW]
-            p = kept_ref[0, at : at + 128, 3 * CW : 3 * CW + CHEADS * 128].astype(F32)
-            c = kept_ref[0, at : at + 128, 3 * CW + CHEADS * 128 :].astype(F32)
-            dp = nt(v, head_stack(gm, 1.0))
+        eighth = 1.0 / math.sqrt(CHD)
+        place = lax.broadcasted_iota(jnp.int32, (places, words, CW), 0).astype(F32)
+        word_grads = []
+        row_grads = []
+        out_grads = []
+        for t, (c, g, weight, _) in enumerate(groups):
+            mine = pl.ds(pl.multiple_of(c * share + g * words, words), words)
+            cnt = count_ref[c, pl.ds(g * words, words), :]
+            shown = place < jnp.concatenate([cnt, cnt], axis=1)[None]
+            word_grads.append(gm_all[mine, :] * weight)
+            out_grads.append(jnp.where(shown, (gp_all[mine, :] * weight)[None], 0.0).reshape(128, CW))
+            row_grads.append(
+                jnp.where(shown, word_grads[t][None], 0.0).reshape(128, CW).astype(BF)
+            )
+        at = [pl.ds(g * 128, 128) for _, g, _, _ in groups]
+        queries = [kept[c, at[t], :CW] for t, (c, *_) in enumerate(groups)]
+        keys = [kept[c, at[t], CW : 2 * CW] for t, (c, *_) in enumerate(groups)]
+        products = [
+            nt(kept[c, at[t], 2 * CW : 3 * CW], head_stack(row_grads[t], 1.0))
+            for t, (c, *_) in enumerate(groups)
+        ]
+        scores = []
+        for t, (c, *_) in enumerate(groups):
+            p = kept[c, at[t], 3 * CW : 3 * CW + CHEADS * 128].astype(F32)
             p3 = p.reshape(places, words, CHEADS * 128)
-            t = p3 * dp.reshape(places, words, CHEADS * 128)
-            ds = (t - p3 * jnp.sum(t, axis=0)[None]).astype(BF).reshape(128, CHEADS * 128)
-            eighth = 1.0 / math.sqrt(CHD)
-            dk = nn(ds, head_stack(q, eighth))
-            ds_rows = jnp.concatenate([ds[:, h * 128 : (h + 1) * 128] for h in range(CHEADS)], axis=0)
-            dq = tn(ds_rows, head_stack(k, eighth))
-            dv = (c.reshape(places, words, CW) * gm_word[None]).reshape(128, CW)
-            dh[at : at + 128, :CW] = dq.astype(BF)
-            dh[at : at + 128, CW : 2 * CW] = dk.astype(BF)
-            dh[at : at + 128, 2 * CW :] = dv.astype(BF)
-        grads = dh[:rows, :]
-        dqkv_sum[...] += tn(normed_all[:rows, :], grads)
+            u = p3 * products[t].reshape(places, words, CHEADS * 128)
+            scores.append((u - p3 * jnp.sum(u, axis=0)[None]).astype(BF).reshape(128, CHEADS * 128))
+        xs = [
+            nn(order_ref[...], x_ref[c, pl.ds(g * words * SPOTS, words * SPOTS), :])
+            for c, g, _, _ in groups
+        ]
+        scales = [lax.rsqrt(jnp.mean(x * x, axis=-1, keepdims=True) + epsilon) for x in xs]
+        normed = jnp.concatenate([(x * s * gain).astype(BF) for x, s in zip(xs, scales)], axis=0)
+        grads = []
+        for t, (c, *_) in enumerate(groups):
+            dk = nn(scores[t], head_stack(queries[t], eighth))
+            stacked = jnp.concatenate(
+                [scores[t][:, h * 128 : (h + 1) * 128] for h in range(CHEADS)], axis=0
+            )
+            dq = tn(stacked, head_stack(keys[t], eighth))
+            column = kept[c, at[t], 3 * CW + CHEADS * 128 :].astype(F32)
+            dv = (column.reshape(places, words, CW) * word_grads[t][None]).reshape(128, CW)
+            grads.append(jnp.concatenate([dq.astype(BF), dk.astype(BF), dv.astype(BF)], axis=1))
+        grads = jnp.concatenate(grads, axis=0)
         dn_all = nt(grads, mats_ref[:, : 3 * CW])
+        dqkv_sum[...] += tn(normed, grads)
         dgain = jnp.zeros((1, CW), F32)
-        for g in range(groups):
-            x, scale = xs[g], scales[g]
-            dn = dn_all[g * 128 : (g + 1) * 128]
+        for t, (c, g, _, target) in enumerate(groups):
+            x, scale = xs[t], scales[t]
+            dn = dn_all[t * 128 : (t + 1) * 128]
             xr = x * scale
             dgain = dgain + jnp.sum(xr * dn, axis=0, keepdims=True)
             w = dn * gain
             inner = jnp.mean(xr * w, axis=-1, keepdims=True)
-            dx = gps[g] + scale * (w - xr * inner)
-            dx_ref[0, pl.ds(g * words * SPOTS, words * SPOTS), :] = tn(
+            dx = out_grads[t] + scale * (w - xr * inner)
+            dx_ref[target, pl.ds(g * words * SPOTS, words * SPOTS), :] = tn(
                 order_ref[...], dx.astype(BF)
             ).astype(BF)
         dgain_ref[...] += dgain
-
-    for (number, places, words), order_ref in zip(classes, orders):
-        pl.when(kind[step] == number)(functools.partial(block, places, words, order_ref))
-
-    @pl.when(step == pl.num_programs(0) - 1)
-    def _():
-        grads_ref[:, : 3 * CW] = dqkv_sum[...].astype(BF)
-
-
-def char_backward(x, kind, counts, gain, mats, kept, pooled, msum, grad_vectors):
+        for slot in picked:
+
+            @pl.when(slot >= 0)
+            def _(slot=slot):
+                save(slot).start()
+
+    def batch(number, carry):
+        for (which, places, words, per), order_ref in zip(classes, orders):
+            pl.when(batch_kind[number] == which)(
+                functools.partial(block, places, words, per, order_ref, number)
+            )
+        return carry
+
+    lax.fori_loop(0, batches, batch, 0)
+    grads_ref[:, : 3 * CW] = dqkv_sum[...].astype(BF)
+
+    def empty(slot, carry):
+        @pl.when(kind[slot] == 0)
+        def _():
+            dx_ref[slot] = jnp.zeros(dx_ref.shape[1:], BF)
+            save(slot).start()
+
+        return carry
+
+    lax.fori_loop(0, slots, empty, 0)
+
+    def finish(slot, carry):
+        save(slot).wait()
+        return carry
+
+    lax.fori_loop(0, slots, finish, 0)
+
+
+def char_backward(x, home, counts, gain, mats, kept, pooled, msum, grad_vectors):
     slots, share = x.shape[:2]
     classes = char_classes(share)
     rows = share * SPOTS
-    orders = [order_matrix(p, w) for _, p, w in classes]
+    orders = [pltpu.VMEM((128, SPOTS * c[2]), BF) for c in classes]
     words_all = slots * share
-    per_slot = lambda shape: pl.BlockSpec((1,) + shape, lambda i, *_: (i,) + (0,) * len(shape))
-    dx, grads, dgain = pl.pallas_call(
+    dx, grads, dgain = char_call(
         functools.partial(char_backward_kernel, classes),
-        grid_spec=pltpu.PrefetchScalarGridSpec(
-            num_scalar_prefetch=1,
-            grid=(slots,),
-            in_specs=[
-                per_slot((rows, CW)),
-                per_slot((share, 128)),
-                per_slot((rows, KEPT)),
-                whole((words_all, 128)),
-                whole((words_all, D)),
-                whole((words_all, CW)),
-                whole((words_all, CW)),
-                whole((1, CW)),
-                whole(mats.shape),
-            ]
-            + [whole(o.shape) for o in orders],
-            out_specs=[
-                per_slot((rows, CW)),
-                whole(mats.shape),
-                whole((1, CW)),
-            ],
-            scratch_shapes=[
-                pltpu.VMEM((words_all, CW), F32),
-                pltpu.VMEM((words_all, CW), F32),
-                pltpu.VMEM((rows, 3 * CW), BF),
-                pltpu.VMEM((rows, CW), BF),
-                pltpu.VMEM((CW, 3 * CW), F32),
-            ],
-        ),
-        out_shape=[
+        "char_backward",
+        [
+            x.reshape(slots, rows, CW), counts, kept, grad_vectors, pooled, msum, gain.reshape(1, CW), mats,
+        ],
+        (home, counts),
+        [
             jax.ShapeDtypeStruct((slots, rows, CW), BF),
             jax.ShapeDtypeStruct(mats.shape, BF),
             jax.ShapeDtypeStruct((1, CW), F32),
         ],
-        compiler_params=pltpu.CompilerParams(vmem_limit_bytes=60 << 20),
-        cost_estimate=pl.CostEstimate(
-            flops=slots * rows * CW * CW * 28, bytes_accessed=slots * rows * KEPT * 3, transcendentals=0
-        ),
-        name="char_backward",
-    )(
-        kind, x.reshape(slots, rows, CW), counts, kept, counts.reshape(words_all, 128), grad_vectors,
-        pooled, msum, gain.reshape(1, CW), mats, *orders,
+        [
+            pltpu.VMEM((slots, rows, CW), BF),
+            pltpu.VMEM((slots, rows, KEPT), BF),
+            pltpu.VMEM((slots + 1, rows, CW), BF),
+            pltpu.VMEM((words_all, CW), F32),
+            pltpu.VMEM((words_all, CW), F32),
+            pltpu.VMEM((CW, 3 * CW), F32),
+        ]
+        + plan_scratch(slots, share)
+        + [pltpu.SemaphoreType.DMA((slots,))] * 3
+        + orders,
+        (0, 2),
+        (0,),
+        slots * rows * CW * CW * 28,
+        53,
     )
     return dx.reshape(x.shape), grads, dgain
 
@@ -416,7 +548,10 @@
     return [(begin, start), (late, onward), (80.0, finish)]
 
 
-def line_gather_stages(out, sems, axis, n, mine, begin, each):
+def line_gather_stages(out, sems, axis, n, mine, begin, each, cols=None):
+    def piece(block):
+        return out.at[block] if cols is None else out.at[block, :, cols]
+
     def step(k):
         for way in range(2):
             block = mine - k if way == 0 else mine + k
@@ -429,13 +564,13 @@
 
                 @pl.when(here)
                 def _(way=way, block=block):
-                    remote(out.at[block], out.at[block], sems, way * n + k - 1, axis, mine).wait_recv()
+                    remote(piece(block), piece(block), sems, way * n + k - 1, axis, mine).wait_recv()
 
             if k < n - 1:
 
                 @pl.when(here & room)
                 def _(way=way, block=block, peer=peer):
-                    remote(out.at[block], out.at[block], sems, way * n + k, axis, peer).start()
+                    remote(piece(block), piece(block), sems, way * n + k, axis, peer).start()
 
     def finish():
         for way in range(2):
@@ -445,7 +580,7 @@
 
                 @pl.when(sent)
                 def _(way=way, k=k):
-                    remote(out.at[mine], out.at[mine], sems, way * n + k, axis, mine).wait_send()
+                    remote(piece(mine), piece(mine), sems, way * n + k, axis, mine).wait_send()
 
     stages = [(begin + each * k, functools.partial(step, k)) for k in range(n)]
     return stages + [(95.0, finish)]
@@ -496,15 +631,18 @@
     return stages + [(70.0, finish)]
 
 
-def direct_stages(source_of, target, sems, axis, n, mine, begin, done, end):
+def direct_stages(source_of, target, sems, axis, n, mine, begin, done, end, cols=None):
+    def piece(block):
+        return target.at[block] if cols is None else target.at[block, :, cols]
+
     def start():
         for d in range(1, n):
             peer = lax.rem(mine + d, n)
-            remote(source_of(peer), target.at[mine], sems, d, axis, peer).start()
+            remote(source_of(peer), piece(mine), sems, d, axis, peer).start()
 
     def finish():
         for d in range(1, n):
-            remote(source_of(mine), target.at[mine], sems, d, axis, mine).wait()
+            remote(source_of(mine), piece(mine), sems, d, axis, mine).wait()
         done()
 
     return [(begin, start), (end, finish)]
@@ -594,7 +732,7 @@
                         own_of = lambda i, out=out: out.at[i]
                     own_of(mine)[...] = x[...]
                 if axis == "dp":
-                    stages += pair_gather_stages(own_of, sems, axis, n, mine, 0.2, 7.0)
+                    stages += pair_gather_stages(own_of, sems, axis, n, mine, 0.2, 6.0 * lax.axis_size("mp") - 11.5)
                 else:
 
                     def start(own_of=own_of, sems=sems, axis=axis, n=n, mine=mine):
@@ -636,7 +774,7 @@
         out_specs=[vmem] * len(tasks),
         scratch_shapes=scratch,
         compiler_params=pltpu.CompilerParams(
-            collective_id=number, has_side_effects=True, vmem_limit_bytes=48 << 20
+            collective_id=number, has_side_effects=True, vmem_limit_bytes=24 << 20
         ),
         name=name,
     )(*[array for _, _, arrays in tasks for array in arrays])
@@ -647,13 +785,14 @@
     return array.reshape(lax.axis_size("dp") // 2, 2, -1, array.shape[-1])
 
 
-def sum_char_grads(grads, small, word_sums):
+def sum_char_grads(grads, gains, word_sums, block_rows):
     n, m = lax.axis_size("dp"), lax.axis_size("mp")
     grads = by_chip(grads)
     rows, cols = grads.shape[2:]
     slim = cols // m
-
-    def kernel(x, s, *refs):
+    small = jax.ShapeDtypeStruct((8, D), F32)
+
+    def kernel(x, gain_char, gain_one, gain_two, *refs):
         words = refs[: len(word_sums)]
         (out, small_out, held, came, total_dp, cut, cut_held, merged, small_dp, small_mp, *sems) = refs[len(word_sums) :]
         pairs = [tuple(sems[2 * t : 2 * t + 2]) for t in range(6)]
@@ -664,11 +803,17 @@
         ]
         part[0]()
         squares = jnp.zeros((1, 1), F32)
-        for word in words:
-            wide = word[...].astype(F32)
+        for t, word in enumerate(words):
+            if t == 1:
+                wide = word[pl.ds(pl.multiple_of(j * block_rows, 16), block_rows), :].astype(F32)
+            else:
+                wide = word[...].astype(F32)
             squares = squares + jnp.sum(jnp.sum(wide * wide, axis=0, keepdims=True), axis=1, keepdims=True)
-        row = lax.broadcasted_iota(jnp.int32, s.shape, 0)
-        small_dp[i] = s[...] + jnp.where(row == 3, squares * (1.0 / n), 0.0)
+        row = lax.broadcasted_iota(jnp.int32, (8, D), 0)
+        small_dp[i] = jnp.where(row == 3, squares * (1.0 / n), 0.0)
+        small_dp[i, 0:1, : gain_char.shape[1]] = gain_char[...]
+        small_dp[i, 1:2, :] = gain_one[...]
+        small_dp[i, 2:3, :] = gain_two[...]
         part[1]()
 
         def small_done():
@@ -722,7 +867,7 @@
             jax.ShapeDtypeStruct((n * rows, cols) if rows % 16 == 0 else (n, rows, cols), BF),
             jax.ShapeDtypeStruct(small.shape, F32),
         ],
-        in_specs=[vmem] * (2 + len(word_sums)),
+        in_specs=[vmem] * (4 + len(word_sums)),
         out_specs=[vmem] * 2,
         scratch_shapes=[
             pltpu.VMEM((n // 2, rows, cols), BF),
@@ -736,10 +881,10 @@
         ]
         + [pltpu.SemaphoreType.DMA((2 * max(n, m),))] * 12,
         compiler_params=pltpu.CompilerParams(
-            collective_id=20, has_side_effects=True, vmem_limit_bytes=48 << 20
+            collective_id=20, has_side_effects=True, vmem_limit_bytes=24 << 20
         ),
         name="sum_char_grads",
-    )(grads, small, *word_sums)
+    )(grads, *gains, *word_sums)
     return sums.reshape(n * rows, cols), smalls
 
 
@@ -757,12 +902,24 @@
 
 
 def word_forward_kernel(
-    width, vec_ref, place_ref, words_ref, doc_ref, doc_row_ref, gain_ref, project_ref,
-    stream_ref, normed_ref, qkv_ref, probs_ref, mixed_ref, keys, values
+    width, vec_ref, place_ref, words_ref, doc_all_ref, doc_row_ref, gain_ref, project_ref,
+    stream_ref, normed_ref, qkv_ref, probs_ref, mixed_ref, keys, values, doc_ref
 ):
     step = pl.program_id(0)
-    numbers = lax.broadcasted_iota(jnp.int32, (ROWS, place_ref.shape[1]), 0) + step * ROWS
-    placed = nn((numbers == place_ref[...]).astype(BF), vec_ref[...])
+    parts, kept_rows = vec_ref.shape[:2]
+    words = kept_rows // OWNER_BLOCKS
+
+    @pl.when(step == 0)
+    def _():
+        doc_ref[...] = tn(doc_all_ref[...].astype(F32).astype(BF), jnp.ones((1, 128), BF))
+
+    numbers = lax.broadcasted_iota(jnp.int32, (ROWS, parts * words), 0) + step * ROWS
+    placed = jnp.zeros((ROWS, D), F32)
+    for k in range(0, OWNER_BLOCKS, 2):
+        pair = range(k, min(k + 2, OWNER_BLOCKS))
+        hits = [(numbers == place_ref[b : b + 1, :]).astype(BF) for b in pair]
+        vectors = [vec_ref[p, b * words : (b + 1) * words, :] for b in pair for p in range(parts)]
+        placed = placed + nn(jnp.concatenate(hits, axis=1), jnp.concatenate(vectors, axis=0))
     stream = words_ref[...].astype(F32) + placed
     stream_ref[...] = stream
     normed = (stream * rms_scale(stream) * gain_ref[...]).astype(BF)
@@ -776,7 +933,7 @@
 
     def attend(number):
         count = (number + 1) * ROWS
-        same = doc_ref[:count, :] == doc_row_ref[...]
+        same = jnp.concatenate([doc_ref[:count, :]] * (ROWS // 128), axis=1) == doc_row_ref[...].astype(F32)
         key_at = lax.broadcasted_iota(jnp.int32, (count, ROWS), 0)
         query_at = lax.broadcasted_iota(jnp.int32, (count, ROWS), 1) + number * ROWS
         allowed = same & (key_at <= query_at)
@@ -790,7 +947,7 @@
             parts.append(tn(values[:count, at], probs).T)
         mixed_ref[...] = jnp.concatenate(parts, axis=1).astype(BF)
 
-    for number in range(doc_ref.shape[0] // ROWS):
+    for number in range(doc_all_ref.shape[1] // ROWS):
         pl.when(step == number)(functools.partial(attend, number))
 
 
@@ -805,9 +962,9 @@
         grid=(length // ROWS,),
         in_specs=[
             full(vectors.shape),
-            full((1, places.shape[0])),
+            full(places.shape),
             rows(D),
-            full((length, 1)),
+            full((1, length)),
             pl.BlockSpec((1, ROWS), lambda i: (0, i)),
             full((1, D)),
             full(project.shape),
@@ -826,14 +983,18 @@
             jax.ShapeDtypeStruct((heads, length, length), BF),
             jax.ShapeDtypeStruct((length, width), BF),
         ],
-        scratch_shapes=[pltpu.VMEM((length, width), BF), pltpu.VMEM((length, width), BF)],
-        compiler_params=pltpu.CompilerParams(vmem_limit_bytes=48 << 20),
+        scratch_shapes=[
+            pltpu.VMEM((length, width), BF),
+            pltpu.VMEM((length, width), BF),
+            pltpu.VMEM((length, 128), F32),
+        ],
+        compiler_params=pltpu.CompilerParams(vmem_limit_bytes=32 << 20),
         name="word_forward",
     )(
         vectors,
-        places.reshape(1, -1),
+        places,
         words,
-        documents.reshape(length, 1),
+        documents.reshape(1, length),
         documents.reshape(1, length),
         gain.reshape(1, D),
         project,
@@ -902,7 +1063,7 @@
             jax.ShapeDtypeStruct(lower.shape, BF),
         ],
         scratch_shapes=[pltpu.VMEM(upper.shape, F32), pltpu.VMEM(lower.shape, F32)],
-        compiler_params=pltpu.CompilerParams(vmem_limit_bytes=48 << 20),
+        compiler_params=pltpu.CompilerParams(vmem_limit_bytes=32 << 20),
         name="feed",
     )(mixed, output, stream, cotangent, gain.reshape(1, D), upper, lower)
 
@@ -956,7 +1117,7 @@
             jax.ShapeDtypeStruct(output.shape, BF),
             jax.ShapeDtypeStruct((1, D), F32),
         ],
-        compiler_params=pltpu.CompilerParams(vmem_limit_bytes=48 << 20),
+        compiler_params=pltpu.CompilerParams(vmem_limit_bytes=32 << 20),
         name="hidden_back",
     )(own, grad, hidden, cotangent, mixed, output, gain.reshape(1, D))
 
@@ -1032,7 +1193,7 @@
             pltpu.VMEM((heads, length, HD), F32),
             pltpu.VMEM((heads, length, HD), F32),
         ],
-        compiler_params=pltpu.CompilerParams(vmem_limit_bytes=48 << 20),
+        compiler_params=pltpu.CompilerParams(vmem_limit_bytes=32 << 20),
         name="word_backward",
     )(probs, qkv, qkv, grad_mixed, normed, project)
 
@@ -1070,11 +1231,27 @@
     )(own, grad, stream, hidden_grad, gain.reshape(1, D))
 
 
-def shampoo_kernel(threshold, position, char_ref, small_ref, gain_ref, gains_ref, *refs):
-    sums, refs = refs[:4], refs[4:]
-    given, refs = [refs[5 * t : 5 * t + 5] for t in range(6)], refs[30:]
-    norm_ref, gain_grad_ref, gains_grad_ref, gain_new_ref, gains_new_ref = refs[:5]
-    made = [refs[5 + 5 * t : 10 + 5 * t] for t in range(6)]
+def shampoo_kernel(
+    threshold, position, char_ref, small_ref, gain_ref, gains_ref, project, output, upper, lower, hidden_in, feed_in, *refs
+):
+    given_in, refs = refs[:30], refs[30:]
+    norm_ref, gain_grad_ref, gains_grad_ref, gain_new_ref, gains_new_ref, block_out = refs[:6]
+    made_out, refs = refs[6:36], refs[36:]
+    given, made = refs[:30], refs[30:60]
+    hidden, feed_sum, total, in_sems, out_sems = refs[60:]
+    loads = [pltpu.make_async_copy(a, b, in_sems.at[t]) for t, (a, b) in enumerate(zip(given_in, given))]
+    loads += [
+        pltpu.make_async_copy(hidden_in, hidden, in_sems.at[30]),
+        pltpu.make_async_copy(feed_in, feed_sum, in_sems.at[31]),
+    ]
+    order = (4, 5, 2, 3, 0, 1)
+    for number in order:
+        for t in range(5):
+            loads[5 * number + t].start()
+    loads[30].start()
+    loads[31].start()
+    saves = [pltpu.make_async_copy(a, b, out_sems.at[t]) for t, (a, b) in enumerate(zip(made, made_out))]
+    saves.append(pltpu.make_async_copy(total, block_out, out_sems.at[30]))
     me = position[0]
     char = char_ref[...].astype(F32)
     small = small_ref[...]
@@ -1097,7 +1274,8 @@
     gains_grad = small[1:3, :] * factor
     gains_grad_ref[...] = gains_grad
     gains_new_ref[...] = gains_ref[...] - gain_rate * gains_grad
-    width = sums[0].shape[1] // 3
+    width = project.shape[1] // 3
+    own = pl.ds(pl.multiple_of(position[1] * width, 16), width)
 
     def whole_of(number, t):
         if number == 0:
@@ -1105,54 +1283,76 @@
         if number == 1:
             return char_ref[:, 4 * CW :]
         if number == 2:
-            return sums[0][:, t * width : (t + 1) * width]
-        return sums[number - 2][...]
+            return project[:, t * width : (t + 1) * width]
+        return (output[own, :], upper[...], lower[...])[number - 3]
 
     def chosen(rows, cols):
         row = lax.broadcasted_iota(jnp.int32, (rows, cols), 0) + me * rows
         return (row == lax.broadcasted_iota(jnp.int32, (rows, cols), 1)).astype(BF)
 
     half = (1.0 - decay_rate) * factor * factor
-    for number in range(6):
-        master, left, right, left_root, right_root = given[number]
-        grad_out, left_out, right_out, new_out, copy_out = made[number]
+    for number in order:
+        for t in range(5):
+            loads[5 * number + t].wait()
+        master, left, right, left_root, right_root = given[5 * number : 5 * number + 5]
+        grad_out, left_out, right_out, new_out, copy_out = made[5 * number : 5 * number + 5]
         for t in range(master.shape[0]):
             grad = whole_of(number, t)
-            own = nn(chosen(master.shape[1], grad.shape[0]), grad)
-            grad_out[t] = own * factor
-            left_out[t] = decay_rate * left[t] + half * nt(own.astype(BF), grad)
+            rows = nn(chosen(master.shape[1], grad.shape[0]), grad)
+            grad_out[t] = rows * factor
+            left_out[t] = decay_rate * left[t] + half * nt(rows.astype(BF), grad)
             cols = nt(grad, chosen(right.shape[1], grad.shape[1])).astype(BF)
             right_out[t] = decay_rate * right[t] + half * tn(cols, grad)
             turned = (nn(left_root[t].astype(BF), grad) * factor).astype(BF)
-            new = master[t] - learn_rate * nn(turned, right_root[:, t * grad.shape[1] : (t + 1) * grad.shape[1]])
+            root = right_root[:, t * grad.shape[1] : (t + 1) * grad.shape[1]]
+            new = master[t] - learn_rate * nn(turned, root)
             new_out[t] = new
             copy_out[t] = new.astype(BF)
-
-
-def shampoo(threshold, position, char_sums, small, gain, gains, word_sums, given):
+        for t in range(5):
+            saves[5 * number + t].start()
+    loads[30].wait()
+    loads[31].wait()
+    total[...] = (hidden[...] + feed_sum[...].astype(F32)).astype(BF)
+    saves[30].start()
+    for save in saves:
+        save.wait()
+
+
+def shampoo(threshold, position, char_sums, small, gain, gains, word_sums, hidden, feed_sum, given):
     flat = []
-    shapes = [
+    shapes = []
+    for master, left, right, left_root, right_root in given:
+        flat += [master, left, right, left_root, right_root]
+        shapes += [
+            jax.ShapeDtypeStruct(a.shape, F32) for a in (master, left, right, master)
+        ] + [jax.ShapeDtypeStruct(master.shape, BF)]
+    first = [
         jax.ShapeDtypeStruct((1, 1), F32),
         jax.ShapeDtypeStruct((1, CW), F32),
         jax.ShapeDtypeStruct((2, D), F32),
         jax.ShapeDtypeStruct((1, CW), F32),
         jax.ShapeDtypeStruct((2, D), F32),
     ]
-    for master, left, right, left_root, right_root in given:
-        flat += [master, left, right, left_root, right_root]
-        shapes += [
-            jax.ShapeDtypeStruct(a.shape, F32) for a in (master, left, right, master)
-        ] + [jax.ShapeDtypeStruct(master.shape, BF)]
     vmem = pl.BlockSpec(memory_space=pltpu.VMEM)
     smem = pl.BlockSpec(memory_space=pltpu.SMEM)
+    hbm = pl.BlockSpec(memory_space=pltpu.HBM)
     return pl.pallas_call(
         functools.partial(shampoo_kernel, threshold),
-        in_specs=[smem] + [vmem] * (4 + len(word_sums) + len(flat)),
-        out_specs=[vmem] * len(shapes),
-        out_shape=shapes,
-        compiler_params=pltpu.CompilerParams(vmem_limit_bytes=56 << 20),
+        in_specs=[smem] + [vmem] * 8 + [hbm] * 32,
+        out_specs=[vmem] * 5 + [hbm] * 31,
+        out_shape=first + [jax.ShapeDtypeStruct(feed_sum.shape, BF)] + shapes,
+        scratch_shapes=[pltpu.VMEM(a.shape, a.dtype) for a in flat]
+        + [pltpu.VMEM(a.shape, a.dtype) for a in shapes]
+        + [
+            pltpu.VMEM(hidden.shape, F32),
+            pltpu.VMEM(feed_sum.shape, BF),
+            pltpu.VMEM(feed_sum.shape, BF),
+            pltpu.SemaphoreType.DMA((32,)),
+            pltpu.SemaphoreType.DMA((31,)),
+        ],
+        compiler_params=pltpu.CompilerParams(vmem_limit_bytes=60 << 20),
         name="shampoo",
-    )(position, char_sums, small, gain.reshape(1, CW), gains, *word_sums, *flat)
+    )(position, char_sums, small, gain.reshape(1, CW), gains, *word_sums, hidden, feed_sum, *flat)
 
 
 def run_stages(stages):
@@ -1209,10 +1409,124 @@
         out_specs=[vmem] * len(outs),
         scratch_shapes=scratch,
         compiler_params=pltpu.CompilerParams(
-            collective_id=number, has_side_effects=True, vmem_limit_bytes=56 << 20
+            collective_id=number, has_side_effects=True, vmem_limit_bytes=28 << 20
         ),
         name=name,
     )(*inputs)
+
+
+def gather_char(mixer, lift, output, home, places):
+    n, m = lax.axis_size("dp"), lax.axis_size("mp")
+    slots, block_words = places.shape
+    cap = -(-slots // n)
+    total = n * cap
+    share = block_words // m
+    shape, shaper = gather_shape([mixer, lift], n)
+    rows = output.shape[1]
+
+    def kernel(
+        mixer_in, lift_in, output_in, home_row, place_ref,
+        mats, line, to_slot, live, live_place, own_row, mixer_ref, lift_ref, output_ref, sent, came, local, *sems
+    ):
+        pairs = [tuple(sems[2 * t : 2 * t + 2]) for t in range(3)]
+        i, j = lax.axis_index("dp"), lax.axis_index("mp")
+        loads = [
+            pltpu.make_async_copy(a, b, local.at[t])
+            for t, (a, b) in enumerate(
+                ((mixer_in, mixer_ref), (lift_in, lift_ref), (output_in, output_ref))
+            )
+        ]
+        for load in loads:
+            load.start()
+        own_of, put = gather_setup([mixer_ref, lift_ref], mats)
+        greet({"dp": n, "mp": m}, {"dp": i, "mp": j})
+        for load in loads:
+            load.wait()
+        put(i)
+        line[j] = output_ref[0].astype(BF)
+        stages = pair_gather_stages(own_of, pairs[0], "dp", n, i, 0.0, 2.0)
+
+        def send_places():
+            before = lax.broadcasted_iota(jnp.int32, (slots, slots), 0)
+            before = before < lax.broadcasted_iota(jnp.int32, (slots, slots), 1)
+            home_col = tn(home_row[...].astype(F32).astype(BF), jnp.ones((1, 128), BF))[:, :slots]
+            same = (home_col == home_row[...].astype(F32)) & before
+            rank = jnp.sum(same.astype(F32), axis=0, keepdims=True)
+            target = jnp.where(
+                home_row[...] >= 0, home_row[...].astype(F32) * cap + rank, float(total)
+            )
+            hit = lax.broadcasted_iota(jnp.int32, (total, slots), 0).astype(F32) == target
+            chosen = hit.astype(F32)
+            to_slot[...] = chosen.astype(BF)
+            placed = jnp.zeros((total, block_words), F32) - 1.0
+            for s in range(slots):
+                placed = jnp.where(
+                    chosen[:, s : s + 1] > 0.0, place_ref[s : s + 1, :].astype(F32), placed
+                )
+            for p in range(n):
+                sent[p] = placed[p * cap : (p + 1) * cap, :].astype(jnp.int32)
+            came[i] = sent[i]
+
+        def use_places():
+            placed = jnp.concatenate([came[p] for p in range(n)], axis=0).astype(F32)
+            held = jnp.max(placed, axis=1, keepdims=True) >= 0.0
+            filled = jnp.where(held, jnp.ones((total, 128), F32), 0.0)
+            lower = lax.broadcasted_iota(jnp.int32, (total, total), 1)
+            lower = (lower < lax.broadcasted_iota(jnp.int32, (total, total), 0)).astype(BF)
+            rank = nn(lower, filled.astype(BF))
+            lane = lax.broadcasted_iota(jnp.int32, (total, 128), 1).astype(F32)
+            chosen = jnp.where((rank == lane) & (filled > 0.0), 1.0, 0.0).astype(BF)
+            live[...] = chosen
+            high = jnp.floor((placed + 1.0) * (1.0 / 32.0))
+            low = placed + 1.0 - high * 32.0
+            high, low = high.astype(BF), low.astype(BF)
+            found = tn(chosen, high) * 32.0 + tn(chosen, low) - 1.0
+            live_place[...] = found[: live_place.shape[0], :].astype(jnp.int32)
+            block = cap * share
+            for p in range(n):
+                col = lax.broadcasted_iota(jnp.int32, (block_words, block), 1) % share + j * share
+                pick = (col == lax.broadcasted_iota(jnp.int32, (block_words, block), 0)).astype(BF)
+                row = lax.broadcasted_iota(jnp.int32, (total, block), 0) - p * cap
+                mine = row == lax.broadcasted_iota(jnp.int32, (total, block), 1) // share
+                value = nn(high, pick) * 32.0 + nn(low, pick) - 1.0
+                own_row[p] = jnp.sum(jnp.where(mine, value, 0.0), axis=0, keepdims=True).astype(jnp.int32)
+
+        stages.append((0.1, send_places))
+        stages += direct_stages(lambda p: sent.at[p], came, pairs[1], "dp", n, i, 0.2, lambda: None, 1.0)
+        stages += direct_stages(lambda p: line.at[j], line, pairs[2], "mp", m, j, 0.3, lambda: None, 50.0)
+        stages.append((1.5, use_places))
+        run_stages(stages)
+
+    vmem = pl.BlockSpec(memory_space=pltpu.VMEM)
+    hbm = pl.BlockSpec(memory_space=pltpu.HBM)
+    lines = max(16, -(-OWNER_BLOCKS // 8) * 8)
+    results = pl.pallas_call(
+        kernel,
+        out_shape=[
+            shape,
+            jax.ShapeDtypeStruct((m, rows, D), BF),
+            jax.ShapeDtypeStruct((total, slots), BF),
+            jax.ShapeDtypeStruct((total, 128), BF),
+            jax.ShapeDtypeStruct((lines, block_words), jnp.int32),
+            jax.ShapeDtypeStruct((n, 1, cap * share), jnp.int32),
+        ],
+        in_specs=[hbm] * 3 + [vmem] * 2,
+        out_specs=[vmem] * 6,
+        scratch_shapes=[
+            pltpu.VMEM(mixer.shape, F32),
+            pltpu.VMEM(lift.shape, F32),
+            pltpu.VMEM(output.shape, F32),
+            pltpu.VMEM((n, cap, block_words), jnp.int32),
+            pltpu.VMEM((n, cap, block_words), jnp.int32),
+            pltpu.SemaphoreType.DMA((3,)),
+        ]
+        + dma_sems(2 * max(n, m)) * 3,
+        compiler_params=pltpu.CompilerParams(
+            collective_id=0, has_side_effects=True, vmem_limit_bytes=60 << 20
+        ),
+        name="gather_char",
+    )(mixer, lift, output, home.reshape(1, slots), places)
+    return [shaper(results[0])] + list(results[1:])
 
 
 def send_vectors(vectors, to_slot, to_live, share, project, upper, lower, output_line):
@@ -1230,7 +1544,7 @@
         weights, line = refs[:3], refs[3]
         out, wides, output = refs[4], refs[5:8], refs[8]
         sent, came, *sems = refs[9:]
-        pairs = [tuple(sems[2 * t : 2 * t + 2]) for t in range(6)]
+        pairs = [tuple(sems[2 * t : 2 * t + 2]) for t in range(8)]
         i, j = lax.axis_index("dp"), lax.axis_index("mp")
         sent[...] = (
             nn(spread_blocks(slots[...], total, vec.shape[0], share), vec[...])
@@ -1241,23 +1555,35 @@
         came[i] = sent[i]
         stages = []
 
-        def compact():
-            out[j] = nn(
-                spread_blocks(live[...], kept, total, share), came[...].reshape(total, D)
-            ).astype(BF)
-
-        stages += direct_stages(lambda p: sent.at[p], came, pairs[0], "dp", n, i, 0.0, compact, 1.0)
-        stages += line_gather_stages(out, pairs[1], "mp", m, j, 2.0, 6.0)
+        def compact(cols):
+            up = lax.broadcasted_iota(jnp.int32, (kept, 128), 0) // share
+            up = (up == lax.broadcasted_iota(jnp.int32, (kept, 128), 1)).astype(BF)
+            blocks = nt(up, live[...]).astype(BF)
+            down = lax.broadcasted_iota(jnp.int32, (blocks.shape[1], total), 1) // share
+            down = (down == lax.broadcasted_iota(jnp.int32, (blocks.shape[1], total), 0)).astype(BF)
+            row = lax.broadcasted_iota(jnp.int32, (kept, total), 0) % share
+            col = lax.broadcasted_iota(jnp.int32, (kept, total), 1) % share
+            spread = jnp.where(row == col, nn(blocks, down), 0.0).astype(BF)
+            out[j, :, cols] = nn(spread, came[:, :, cols].reshape(total, D // 2)).astype(BF)
+
+        for half in range(2):
+            cols = slice(half * (D // 2), (half + 1) * (D // 2))
+            stages += direct_stages(
+                lambda p, cols=cols: sent.at[p, :, cols], came, pairs[6 * half], "dp", n, i, 0.1 * half,
+                functools.partial(compact, cols), 1.0 + half, cols,
+            )
+            begin = 1.5 + half * (m - 1.5)
+            stages += line_gather_stages(out, pairs[1 + 6 * half], "mp", m, j, begin, 1.0, cols)
         for t, (x, wide) in enumerate(zip(weights, wides)):
             own_of, put = gather_setup([x], wide)
             put(i)
-            stages += pair_gather_stages(own_of, pairs[2 + t], "dp", n, i, 2.1, 9.0)
+            stages += pair_gather_stages(own_of, pairs[2 + t], "dp", n, i, 0.3, 2.0 * m + 0.5)
         if aligned:
             output_of = lambda d: output.at[:, pl.ds(pl.multiple_of(d * line_rows, 16), line_rows), :]
         else:
             output_of = lambda d: output.at[d]
         output_of(i)[...] = line[...]
-        stages += pair_gather_stages(output_of, pairs[5], "dp", n, i, 2.1, 9.0)
+        stages += pair_gather_stages(output_of, pairs[5], "dp", n, i, 0.3, 2.0 * m + 0.5)
         run_stages(stages)
 
     results = call_remote(
@@ -1267,7 +1593,7 @@
         [jax.ShapeDtypeStruct((m, kept, D), BF)]
         + [shape for shape, _ in made]
         + [jax.ShapeDtypeStruct(output_shape, BF)],
-        [pltpu.VMEM((n, block, D), BF)] * 2 + dma_sems(2 * max(n, m)) * 6,
+        [pltpu.VMEM((n, block, D), BF)] * 2 + dma_sems(2 * max(n, m)) * 8,
         [vectors, to_slot, to_live, project, upper, lower, output_line],
     )
     output = results[4]
@@ -1301,7 +1627,7 @@
         for t, (x, out) in enumerate(zip(roots_in, roots_out)):
             own_of, put = gather_setup([x], out)
             put(i)
-            stages += pair_gather_stages(own_of, pairs[4 + t], "dp", n, i, 2.0, 11.0)
+            stages += pair_gather_stages(own_of, pairs[4 + t], "dp", n, i, 2.0, 72.5)
 
         def back():
             mine = pl.ds(pl.multiple_of(j * share, share), share)
@@ -1360,8 +1686,8 @@
 def stream_grads(part_one, stream, grad_hidden, gain, own_row, to_slot, sums, grad_project, grad_output, slots):
     n, m = lax.axis_size("dp"), lax.axis_size("mp")
     share = part_one.shape[1]
-    total_words = own_row.shape[1]
-    block = total_words // n
+    block = own_row.shape[2]
+    total_words = n * block
     words = share * m
     width = total_words // to_slot.shape[0]
     parts = [by_chip(grad_project), by_chip(grad_output)]
@@ -1372,7 +1698,7 @@
         out, gain_grad, vectors, up_out, low_out, project_out, output_out = refs[:7]
         (held, total, project_sum, output_sum, line_held, picked, came,
          p_held, p_came, o_held, o_came, *sems) = refs[7:]
-        pairs = [tuple(sems[2 * t : 2 * t + 2]) for t in range(10)]
+        pairs = [tuple(sems[2 * t : 2 * t + 2]) for t in range(12)]
         i, j = lax.axis_index("dp"), lax.axis_index("mp")
         greet({"dp": n, "mp": m}, {"dp": i, "mp": j})
         stages = line_part_stages(part, held, total, pairs[0], "mp", m, j, 0.0, 6.0)
@@ -1382,8 +1708,8 @@
         low_of, put_low = gather_setup([low], low_out)
         put_up(i)
         put_low(i)
-        stages += pair_gather_stages(up_of, pairs[3], "dp", n, i, 2.0, 11.0)
-        stages += pair_gather_stages(low_of, pairs[4], "dp", n, i, 2.0, 11.0)
+        stages += pair_gather_stages(up_of, pairs[3], "dp", n, i, 2.0, 71.9)
+        stages += pair_gather_stages(low_of, pairs[4], "dp", n, i, 2.0, 71.9)
 
         def back():
             mine = pl.ds(pl.multiple_of(j * share, share), share)
@@ -1394,23 +1720,45 @@
             gain_grad[...] = jnp.sum(stream_own * scale * grad, axis=0, keepdims=True)
 
         stages.append((71.0, back))
-        stages += [
-            (when if when < 90 else 199.0, run)
-            for when, run in line_gather_stages(out, pairs[5], "mp", m, j, 72.0, 0.1)
-        ]
+        for half in range(2):
+            cols = slice(half * (D // 2), (half + 1) * (D // 2))
+            begin = 72.0 + 0.1 * half * (m - 1.5)
+            stages += [
+                (when if when < 90 else 199.0, run)
+                for when, run in line_gather_stages(out, pairs[5 + 5 * half], "mp", m, j, begin, 0.1, cols)
+            ]
         project_of, put_project = gather_setup([project_sum], project_out)
         output_of, put_output = gather_setup([output_sum], output_out)
-        late = []
 
         def put_sums():
             put_project(i)
             line_held[j] = output_sum[0].astype(BF)
 
+        target = i // (n // m)
+
+        def line_send():
+            @pl.when(j != target)
+            def _():
+                remote(line_held.at[j], line_held.at[j], pairs[7], j, "mp", target).start()
+
         def line_done():
-            summed = line_held[0].astype(F32)
-            for p in range(1, m):
-                summed = summed + line_held[p].astype(F32)
-            output_sum[0] = summed
+            @pl.when(j != target)
+            def _():
+                remote(line_held.at[j], line_held.at[j], pairs[7], j, "mp", target).wait_send()
+
+            @pl.when(j == target)
+            def _():
+                for p in range(m):
+
+                    @pl.when(j != p)
+                    def _(p=p):
+                        remote(line_held.at[p], line_held.at[p], pairs[7], p, "mp", target).wait_recv()
+
+                summed = line_held[0].astype(F32)
+                for p in range(1, m):
+                    summed = summed + line_held[p].astype(F32)
+                output_sum[0] = summed
+
             put_output(i)
 
         stages = [(60.0 if when == 80.0 else when, run) for when, run in stages]
@@ -1422,33 +1770,40 @@
                 [run for _, run in pair_gather_stages(project_of, pairs[6], "dp", n, i, 0, 0)],
             )
         ]
-        stages += direct_stages(
-            lambda p: line_held.at[j], line_held, pairs[7], "mp", m, j, 72.03, line_done, 76.0
-        )
+        late_line = 72.0 + 0.1 * 2 * m
+        stages += [(72.03, line_send), (late_line + 0.01, line_done)]
         stages += [
             (when, run)
             for when, run in zip(
-                (77.0, 81.5, 198.5),
+                (late_line + 0.02, 81.5, 198.5),
                 [run for _, run in pair_gather_stages(output_of, pairs[8], "dp", n, i, 0, 0)],
             )
         ]
 
-        def pick(d):
-            peer = lax.rem(i + d, n)
-            rows = out[...].reshape(words, D)
+        def pick(half):
+            cols = slice(half * (D // 2), (half + 1) * (D // 2))
+            rows = out[:, :, cols].reshape(words, D // 2)
             number = lax.broadcasted_iota(jnp.int32, (words, block), 0)
-            picked[peer] = tn((number == row_ref[peer]).astype(BF), rows).astype(BF)
-            if d:
-                remote(picked.at[peer], came.at[i], pairs[9], d, "dp", peer).start()
-            else:
-                came[i] = picked[i]
-
-        for d in range(n):
-            stages.append((78.0 + (d - 1) % n * 0.1, functools.partial(pick, d)))
+            for d in list(range(1, n)) + [0]:
+                peer = lax.rem(i + d, n)
+                picked[peer, :, cols] = tn((number == row_ref[peer]).astype(BF), rows).astype(BF)
+                if d:
+                    remote(
+                        picked.at[peer, :, cols], came.at[i, :, cols], pairs[9 + 2 * half], d, "dp", peer
+                    ).start()
+            came[i, :, cols] = picked[i, :, cols]
+
+        for half in range(2):
+            begin = 72.0 + 0.1 * half * (m - 1.5)
+            stages.append((begin + 0.1 * (m - 1) + 0.011, functools.partial(pick, half)))
 
         def place():
-            for d in range(1, n):
-                remote(picked.at[i], came.at[i], pairs[9], d, "dp", i).wait()
+            for half in range(2):
+                cols = slice(half * (D // 2), (half + 1) * (D // 2))
+                for d in range(1, n):
+                    remote(
+                        picked.at[i, :, cols], came.at[i, :, cols], pairs[9 + 2 * half], d, "dp", i
+                    ).wait()
             spread = spread_blocks(slot_ref[...], total_words, vectors.shape[0], width)
             vectors[...] = tn(spread, came[...].reshape(total_words, D)).astype(BF)
 
@@ -1479,13 +1834,13 @@
             held_of(parts[1]),
             held_of(parts[1]),
         ]
-        + dma_sems(2 * max(n, m)) * 10,
+        + dma_sems(2 * max(n, m)) * 12,
         [
             part_one,
             stream,
             grad_hidden,
             gain.reshape(1, D),
-            own_row.reshape(n, 1, block),
+            own_row,
             to_slot,
             sums[0][None],
             sums[1][None],
@@ -1540,75 +1895,28 @@
     peer_count = lax.axis_size("dp")
     part_count = lax.axis_size("mp")
     owner_index = lax.axis_index("dp")
-    pair_cap = -(-slot_count // peer_count)
-    slot_total = peer_count * pair_cap
-    rows_dev, length = (word_inputs.shape[0], word_inputs.shape[1])
-    words_dev = rows_dev * length
-    block_words = share_rows * part_count
-
-    length = word_inputs.shape[1]
-    own = lax.axis_index("mp").astype(jnp.int32).reshape(1)
-    position = owner_index.astype(jnp.int32).reshape(1)
-    peers = lax.broadcasted_iota(jnp.int32, (slot_count, peer_count), 1)
-    owner_match = (block_home[:, None] == peers).astype(jnp.int32)
-    earlier = (
-        lax.broadcasted_iota(jnp.int32, (slot_count, slot_count), 1)
-        < lax.broadcasted_iota(jnp.int32, (slot_count, slot_count), 0)
-    )
-    same_owner = block_home[:, None] == block_home[None, :]
-    slot_rank = jnp.sum((earlier & same_owner).astype(jnp.int32), axis=1)
-    slot_target = jnp.where(block_home >= 0, block_home * pair_cap + slot_rank, slot_total)
-    to_slot = lax.broadcasted_iota(jnp.int32, (slot_total, slot_count), 0) == slot_target[None, :]
-
-    sent_place = jnp.max(
-        jnp.where(to_slot[:, :, None], word_place[None] + 1, 0), axis=1
-    ) - 1
-    char_whole, came_place, output_line = exchange(
-        "gather_char",
-        0,
-        [
-            ("gather", "dp", [char_mixer, char_lift]),
-            ("swap", "dp", [sent_place.reshape(peer_count, pair_cap, block_words)]),
-            ("gather", "mp", [word_output]),
-        ],
-    )
-    came_place = came_place.reshape(slot_total, block_words)
-    kind = char_kind(block_home, char_count, share_rows)
-    counts = jnp.broadcast_to(
-        char_count.astype(F32)[..., None], (slot_count, share_rows, 128)
+    words_dev = word_inputs.shape[0] * word_inputs.shape[1]
+    position = jnp.stack([owner_index, lax.axis_index("mp")]).astype(jnp.int32)
+
+    char_whole, output_line, to_slot, live, live_place, own_row = gather_char(
+        char_mixer, char_lift, word_output, block_home, word_place
     )
     word_vectors, kept, pooled, msum = char_forward(
-        character_embeddings, kind, counts, char_gain, char_whole
-    )
-
-    live = jnp.max(came_place, axis=1) >= 0
-    slots_before = (
-        lax.broadcasted_iota(jnp.int32, (slot_total, slot_total), 1)
-        < lax.broadcasted_iota(jnp.int32, (slot_total, slot_total), 0)
-    )
-    live_rank = jnp.sum((slots_before & live[None, :]).astype(jnp.int32), axis=1)
-    live_rank = jnp.where(live, live_rank, OWNER_BLOCKS)
-    to_live = lax.broadcasted_iota(jnp.int32, (OWNER_BLOCKS, slot_total), 0) == live_rank[None, :]
-    live_place = jnp.max(jnp.where(to_live[:, :, None], came_place[None] + 1, 0), axis=1) - 1
-    own_row = lax.dynamic_slice_in_dim(
-        came_place.reshape(slot_total, part_count, share_rows), own[0], 1, 1
-    ).reshape(1, -1)
-
+        character_embeddings, block_home, char_count, char_gain, char_whole
+    )
     live_vectors, project_mat, upper_mat, lower_mat, output_mat = send_vectors(
         word_vectors,
-        to_slot.astype(BF),
-        to_live.astype(BF),
+        to_slot,
+        live,
         share_rows,
         word_project.reshape((3,) + word_project.shape[2:]),
         feed_upper,
         feed_lower,
-        output_line.reshape((part_count,) + word_output.shape[1:]),
-    )
-    place_parts = live_place.reshape(OWNER_BLOCKS, part_count, share_rows)
-    place_flat = place_parts.transpose(1, 0, 2).reshape(-1)
+        output_line,
+    )
     stream, normed_one, qkv, probs, mixed = word_forward(
-        live_vectors.reshape(-1, D),
-        place_flat,
+        live_vectors,
+        live_place,
         word_inputs.reshape(words_dev, D),
         documents,
         word_gains[0],
@@ -1654,31 +1962,22 @@
         grad_hidden,
         word_gains[0],
         own_row,
-        to_slot.astype(BF),
+        to_slot,
         (part_upper, part_lower),
         grad_project,
         grad_output_mat,
         slot_count,
     )
     word_inputs_gradient = grad_words.reshape(word_inputs.shape)
-    own_rows = word_output.shape[1] * peer_count
-    sum_output = lax.dynamic_slice_in_dim(sum_output, own[0] * own_rows, own_rows, 0)
     grad_vectors, feed_part = lax.optimization_barrier((grad_vectors, feed_part))
-    feed_total = lax.psum(feed_part, "mp").astype(F32)
-    block_out = (hidden + feed_total).astype(BF).reshape(word_inputs.shape)
+    feed_total = lax.psum(feed_part, "mp")
     char_embeds_gradient, char_grads, grad_char_gain = char_backward(
-        character_embeddings, kind, counts, char_gain, char_whole, kept, pooled, msum, grad_vectors
-    )
-    small = jnp.concatenate(
-        [
-            jnp.pad(grad_char_gain, ((0, 0), (0, D - CHAR_BLOCK_WIDTH))),
-            gain_one,
-            gain_two,
-            jnp.zeros((5, D), F32),
-        ]
+        character_embeddings, block_home, char_count, char_gain, char_whole, kept, pooled, msum, grad_vectors
     )
     word_sums = (sum_project, sum_output, sum_upper, sum_lower)
-    char_sums, small_sums = sum_char_grads(char_grads, small, word_sums)
+    char_sums, small_sums = sum_char_grads(
+        char_grads, (grad_char_gain, gain_one, gain_two), word_sums, word_output.shape[1] * peer_count
+    )
     parameter_count = (
         sum(
             part_count * w.size * peer_count
@@ -1697,6 +1996,8 @@
         char_gain,
         word_gains,
         word_sums,
+        hidden,
+        feed_total,
         [
             tuple(flat(a) for a in group[:4]) + (group[4],)
             for group in (
@@ -1709,7 +2010,7 @@
             )
         ],
     )
-    norm, gain_grad, gains_grad, gain_new, gains_new = results[:5]
+    norm, gain_grad, gains_grad, gain_new, gains_new, block_out = results[:6]
     stepped = []
     for t, group in enumerate(
         (
@@ -1724,10 +2025,10 @@
         master, left, right = group
         stepped += [
             a.reshape(b.shape)
-            for a, b in zip(results[5 + 5 * t : 10 + 5 * t], (master, left, right, master, master))
+            for a, b in zip(results[6 + 5 * t : 11 + 5 * t], (master, left, right, master, master))
         ]
     return (
-        block_out,
+        block_out.reshape(word_inputs.shape),
         word_inputs_gradient,
         char_embeds_gradient,
         gain_grad[0],

time: 393 us -> 327 us (0.83)
  Pallas kernels: 340 us -> 292 us
  other arithmetic: 11.4 us -> 0.65 us
  local copies, waits for them, and re-layouts: 21.7 us -> 16 us
    pallas_call x3, Pallas kernels: 172 us -> 137 us  [call_remote(): pl.pallas_call(kernel, out_shape=outs, in_specs=[vmem] * len(inputs), out...]
    pallas_call x2 -> x1, Pallas kernels: 37.3 us -> 23.8 us  [exchange(): pl.pallas_call(kernel, out_shape=outs, in_specs=[vmem] * total_ins, out_s...]
    unnamed x75 -> x89, local copies, waits for them, and re-layouts: 16 us -> 15.2 us
    pallas_call x2 -> x3, Pallas kernels: 52.2 us -> 51.8 us  [the longest x2 35.3 us: char_call(): pl.pallas_call(kernel, in_specs=[smem] * len(scalars) + [hbm if t in in_h...]
  transfers between devices with their start and end apart: 1 -> 1, of which waited for: 0 -> 0; matrix products, arithmetic and copies ran while one was open for 1% -> 0% of each run, Pallas kernels for 20% -> 20%
where the time goes in v1:
time: 327 us; the launch traced here: 323 us
  Pallas kernels  292 us (89%)
  local copies, waits for them, and re-layouts  16 us (5%)
  between operations  14.9 us (5%)
    pallas_call x3, Pallas kernels, call_remote(): pl.pallas_call(kernel, out_shape=outs, in_specs=[vmem] * len(inputs), out...  137 us
    pallas_call x1, Pallas kernels, sum_char_grads(): pl.pallas_call(kernel, out_shape=[jax.ShapeDtypeStruct((n * rows, cols) i...  41.5 us
    pallas_call x2, Pallas kernels, char_call(): pl.pallas_call(kernel, in_specs=[smem] * len(scalars) + [hbm if t in in_h...  35.3 us
    pallas_call x1, Pallas kernels, exchange(): pl.pallas_call(kernel, out_shape=outs, in_specs=[vmem] * total_ins, out_s...  23.8 us
    pallas_call x1, Pallas kernels, gather_char(): pl.pallas_call(kernel, out_shape=[shape, jax.ShapeDtypeStruct((m, rows, D...  16.5 us
    unnamed x89, local copies, waits for them, and re-layouts  15.2 us
    pallas_call x1, Pallas kernels, shampoo(): pl.pallas_call(functools.partial(shampoo_kernel, threshold), in_specs=[sm...  12 us
    pallas_call x1, Pallas kernels, word_forward(): pl.pallas_call(functools.partial(word_forward_kernel, width), grid=(lengt...  10.2 us
  transfers between devices with their start and end apart: 1, of which 0 were waited for; matrix products, arithmetic and copies ran while one was open for 0% of the time, Pallas kernels for 20%

profile of v1, /device:TPU:0, one launch (start us, length us, event | category | flops | bytes accessed | tf_op | source)
XLA Modules:
  0.0 323.2 jit_solution(8874461792732432193)
XLA Ops:
  8.0 16.5 %gather_char.1 = (bf16[256,1536]{1,0:T(8,128)(2,1)}, bf16[4,16,512]{2,1,0:T(8,128)(2,1)}, bf16[24,20]{1,0:T(8,128)(2,1)}, bf16[24,128]{1,0:T(8,128)(2,1)}, s32[16,128]{1,0:T(8,128)}, /*index=5*/s32[8,1,96]{2,1,0:T(1,128)}) custom-call(f32[4,32,256]{2,1,0:T(8,128)} %refs_0_.1, f32[1,32,512]{2,1,0:T(8,128)} %refs_5_.1, f32[1,16,512]{2,1,0:T(8,128)} %refs_15_.1, ...), custom_call_target="tpu_custom_call" | custom-call | tf_op jit(solution)/shard_map/gather_char/pallas_call | solution.py:1503
  25.8 2.5 copy-done.36
  28.3 1.1 copy-done.37
  30.3 13.5 %char_forward.1 = (bf16[640,512]{1,0:T(8,128)(2,1)S(1)}, bf16[20,512,1536]{2,1,0:T(8,128)(2,1)}, bf16[640,256]{1,0:T(8,128)(2,1)S(1)}, f32[640,256]{1,0:T(8,128)S(1)}) custom-call(s32[20]{0:T(128)S(1)} %copy-done.34, s32[20,32]{1,0:T(8,128)S(1)} %copy-done.39, bf16[20,512,256]{2,1,0:T(8,128)(2,1)S(1)} %bitcast.68, s32[20,32]{1,0:T(8,128)S(1)} %copy-done.39, ...), custom_call_target="tpu_custom_call" | custom-call | flops 10737418240 | bytes 62914560 | tf_op jit(solution)/shard_map/char_forward/pallas_call | solution.py:219
  43.9 48.6 %send_vectors.1 = (bf16[4,320,512]{2,1,0:T(8,128)(2,1)S(1)}, bf16[512,384]{1,0:T(8,128)(2,1)S(1)}, bf16[512,512]{1,0:T(8,128)(2,1)S(1)}, bf16[512,512]{1,0:T(8,128)(2,1)S(1)}, bf16[4,128,512]{2,1,0:T(8,128)(2,1)S(1)}) custom-call(bf16[640,512]{1,0:T(8,128)(2,1)S(1)} %get-tuple-element.130.vec, bf16[24,20]{1,0:T(8,128)(2,1)S(1)} %copy-done.26, ...), custom_call_target="tpu_custom_call" | custom-call | tf_op jit(solution)/shard_map/send_vectors/pallas_call | solution.py:1405
  92.6 10.2 %word_forward.1 = (f32[1024,512]{1,0:T(8,128)S(1)}, bf16[1024,512]{1,0:T(8,128)(2,1)S(1)}, bf16[1024,384]{1,0:T(8,128)(2,1)S(1)}, bf16[2,1024,1024]{2,1,0:T(8,128)(2,1)S(1)}, bf16[1024,128]{1,0:T(8,128)(2,1)S(1)}) custom-call(bf16[4,320,512]{2,1,0:T(8,128)(2,1)S(1)} %get-tuple-element.134.vec_ref, s32[16,128]{1,0:T(8,128)S(1)} %copy-done.29, ...), custom_call_target="tpu_custom_call" | custom-call | tf_op jit(solution)/shard_map/word_forward/pallas_call | solution.py:960
  102.8 23.8 %gather_mixed.1 = (bf16[4,1024,128]{2,1,0:T(8,128)(2,1)S(1)}, bf16[256,1024]{1,0:T(8,128)(2,1)S(1)}, bf16[512,512]{1,0:T(8,128)(2,1)S(1)}) custom-call(bf16[1024,128]{1,0:T(8,128)(2,1)S(1)} %get-tuple-element.139.refs_0_, f32[4,32,256]{2,1,0:T(8,128)S(1)} %copy-done.21, f32[1,64,512]{2,1,0:T(8,128)S(1)} %copy-done.22), custom_call_target="tpu_custom_call" | custom-call | tf_op jit(solution)/shard_map/gather_mixed/pallas_call | solution.py:770
  126.6 0.8 copy-done.12
  127.4 0.8 copy-done.13
  128.2 7.3 %feed.1 = (f32[1024,512]{1,0:T(8,128)S(1)}, bf16[1024,512]{1,0:T(8,128)(2,1)S(1)}, bf16[1024,512]{1,0:T(8,128)(2,1)S(1)}, bf16[512,512]{1,0:T(8,128)(2,1)S(1)}, bf16[512,512]{1,0:T(8,128)(2,1)S(1)}) custom-call(bf16[4,1024,128]{2,1,0:T(8,128)(2,1)S(1)} %get-tuple-element.140.mixed_ref.mix, bf16[512,512]{1,0:T(8,128)(2,1)S(1)} %bitcast.46, ...), custom_call_target="tpu_custom_call" | custom-call | tf_op jit(solution)/shard_map/feed/pallas_call | solution.py:1045
  135.6 1.0 copy-done.7
  136.6 30.9 %hidden_grads.1 = (f32[256,512]{1,0:T(8,128)S(1)}, bf16[4,256,128]{2,1,0:T(8,128)(2,1)S(1)}, bf16[512,512]{1,0:T(8,128)(2,1)S(1)}, f32[1,512]{1,0:T(1,128)S(1)},...) custom-call(bf16[4,256,512]{2,1,0:T(8,128)(2,1)S(1)} %bitcast.48, ...), custom_call_target="tpu_custom_call" | custom-call | tf_op jit(solution)/shard_map/hidden_grads/pallas_call | solution.py:1405
  167.4 0.8 copy-done.14
  168.2 0.8 copy-done.15
  169.0 0.8 copy-done.16
  169.8 8.0 %word_backward.1 = (bf16[1024,512]{1,0:T(8,128)(2,1)S(1)}, bf16[512,384]{1,0:T(8,128)(2,1)S(1)}) custom-call(bf16[2,1024,1024]{2,1,0:T(8,128)(2,1)S(1)} %get-tuple-element.137.probs_ref, bf16[1024,384]{1,0:T(8,128)(2,1)S(1)} %get-tuple-element.138.qkv_ref.all_ref, bf16[1024,384]{1,0:T(8,128)(2,1)S(1)} %get-tuple-element.138.qkv_ref.all_ref, ...), custom_call_target="tpu_custom_call" | custom-call | tf_op jit(solution)/shard_map/word_backward/pallas_call | solution.py:1175
  177.9 57.5 %stream_grads.1 = (bf16[4,256,512]{2,1,0:T(8,128)(2,1)S(1)}, f32[1,512]{1,0:T(1,128)S(1)}, bf16[640,512]{1,0:T(8,128)(2,1)S(1)}, bf16[512,512]{1,0:T(8,128)(2,1)...) custom-call(bf16[4,256,512]{2,1,0:T(8,128)(2,1)S(1)} %bitcast.51, ...), custom_call_target="tpu_custom_call" | custom-call | tf_op jit(solution)/shard_map/stream_grads/pallas_call | solution.py:1405
  235.4 0.9 copy-done.38
  236.4 21.8 %char_backward.1 = (bf16[20,512,256]{2,1,0:T(8,128)(2,1)}, bf16[256,1536]{1,0:T(8,128)(2,1)}, f32[1,256]{1,0:T(1,128)S(1)}) custom-call(s32[20]{0:T(128)S(1)} %copy-done.35, s32[20,32]{1,0:T(8,128)S(1)} %copy-done.40, bf16[20,512,256]{2,1,0:T(8,128)(2,1)} %bitcast.67, s32[20,32]{1,0:T(8,128)S(1)} %copy-done.40, ...), custom_call_target="tpu_custom_call" | custom-call | flops 18790481920 | bytes 62914560 | tf_op jit(solution)/shard_map/char_backward/pallas_call | solution.py:219
  258.3 1.1 copy-done.9
  259.4 41.5 %sum_char_grads.1 = (bf16[256,1536]{1,0:T(8,128)(2,1)S(1)}, f32[8,512]{1,0:T(8,128)S(1)}) custom-call(bf16[4,2,32,1536]{3,2,1,0:T(8,128)(2,1)S(1)} %bitcast.52, f32[1,256]{1,0:T(1,128)S(1)} %get-tuple-element.164.gain_char, f32[1,512]{1,0:T(1,128)S(1)} %get-tuple-element.165.gain_one, f32[1,512]{1,0:T(1,128)S(1)} %get-tuple-element.166.gain_two, ...), custom_call_target="tpu_custom_call" | custom-call | tf_op jit(solution)/shard_map/sum_char_grads/pallas_call | solution.py:864
  301.0 0.9 copy-done.8
  303.1 12.0 %shampoo.1 = (f32[1,1]{1,0:T(1,128)}, f32[1,256]{1,0:T(1,128)}, f32[2,512]{1,0:T(2,128)}, f32[1,256]{1,0:T(1,128)}, f32[2,512]{1,0:T(2,128)}, /*index=5*/bf16[10...) custom-call(s32[2]{0:T(128)} %pad_add_fusion.position, ...), custom_call_target="tpu_custom_call" | custom-call | tf_op jit(solution)/shard_map/shampoo/pallas_call | solution.py:1339
  315.1 1.0 copy.84
  (82 shorter events, 4.3 us)
Async XLA Ops:
  7.2 295.9 %all-reduce.2.cloned.1.call-start = ((), (), s32[]{:S(2)}) async-start(), calls=%async_computation | async-start | bytes 2097152 | tf_op jit(solution)/shard_map/psum | solution.py:1973
  30.2 13.7 %copy-start.26 = (bf16[24,20]{1,0:T(8,128)(2,1)S(1)}, bf16[24,20]{1,0:T(8,128)(2,1)}, u32[]{:S(2)}) copy-start(bf16[24,20]{1,0:T(8,128)(2,1)} %get-tuple-element.131.slots.slot_ref) | copy-start | bytes 2884
  30.2 62.3 %copy-start.6 = (bf16[1,1024,512]{2,1,0:T(8,128)(2,1)S(1)}, bf16[1,1024,512]{2,1,0:T(8,128)(2,1)}, u32[]{:S(2)}) copy-start(bf16[1,1024,512]{2,1,0:T(8,128)(2,1)} %param.39) | copy-start | bytes 3145732
  30.2 62.3 %copy-start.28 = (s32[1,1024]{1,0:T(1,128)S(1)}, s32[1,1024]{1,0:T(1,128)}, u32[]{:S(2)}) copy-start(s32[1,1024]{1,0:T(1,128)} %doc_row_ref.1) | copy-start | bytes 12292
  30.2 62.3 %copy-start.29 = (s32[16,128]{1,0:T(8,128)S(1)}, s32[16,128]{1,0:T(8,128)}, u32[]{:S(2)}) copy-start(s32[16,128]{1,0:T(8,128)} %get-tuple-element.135.place_ref) | copy-start | bytes 24580
  30.2 72.6 %copy-start.21 = (f32[4,32,256]{2,1,0:T(8,128)S(1)}, f32[4,32,256]{2,1,0:T(8,128)}, u32[]{:S(2)}) copy-start(f32[4,32,256]{2,1,0:T(8,128)} %refs_1_.5) | copy-start | bytes 393220
  30.2 72.6 %copy-start.22 = (f32[1,64,512]{2,1,0:T(8,128)S(1)}, f32[1,64,512]{2,1,0:T(8,128)}, u32[]{:S(2)}) copy-start(f32[1,64,512]{2,1,0:T(8,128)} %refs_2_.5) | copy-start | bytes 393220
  43.8 91.8 %copy-start.41 = (f32[640,256]{1,0:T(8,128)}, f32[640,256]{1,0:T(8,128)S(1)}, u32[]{:S(2)}) copy-start(f32[640,256]{1,0:T(8,128)S(1)} %get-tuple-element.162.msum_ref) | copy-start | bytes 1966084
  43.8 91.8 %copy-start.42 = (bf16[640,256]{1,0:T(8,128)(2,1)}, bf16[640,256]{1,0:T(8,128)(2,1)S(1)}, u32[]{:S(2)}) copy-start(bf16[640,256]{1,0:T(8,128)(2,1)S(1)} %get-tuple-element.161.pooled_ref) | copy-start | bytes 983044
  43.8 84.4 %copy-start.1 = (bf16[1,1024,512]{2,1,0:T(8,128)(2,1)S(1)}, bf16[1,1024,512]{2,1,0:T(8,128)(2,1)}, u32[]{:S(2)}) copy-start(bf16[1,1024,512]{2,1,0:T(8,128)(2,1)} %param.41) | copy-start | bytes 3145732
  92.5 44.0 %copy-start.18 = (f32[1,64,512]{2,1,0:T(8,128)S(1)}, f32[1,64,512]{2,1,0:T(8,128)}, u32[]{:S(2)}) copy-start(f32[1,64,512]{2,1,0:T(8,128)} %refs_1_.6) | copy-start | bytes 393220
  92.6 44.0 %copy-start.19 = (f32[1,64,512]{2,1,0:T(8,128)S(1)}, f32[1,64,512]{2,1,0:T(8,128)}, u32[]{:S(2)}) copy-start(f32[1,64,512]{2,1,0:T(8,128)} %refs_2_.6) | copy-start | bytes 393220
  92.6 44.0 %copy-start.20 = (f32[1,64,512]{2,1,0:T(8,128)S(1)}, f32[1,64,512]{2,1,0:T(8,128)}, u32[]{:S(2)}) copy-start(f32[1,64,512]{2,1,0:T(8,128)} %refs_3_.2) | copy-start | bytes 393220
  92.6 44.0 %copy-start.25 = (f32[3,1,16,128]{3,2,1,0:T(8,128)S(1)}, f32[3,1,16,128]{3,2,1,0:T(8,128)}, u32[]{:S(2)}) copy-start(f32[3,1,16,128]{3,2,1,0:T(8,128)} %param.62) | copy-start | bytes 73732
  136.5 41.3 %copy-start = (f32[1024,512]{1,0:T(8,128)}, f32[1024,512]{1,0:T(8,128)S(1)}, u32[]{:S(2)}) copy-start(f32[1024,512]{1,0:T(8,128)S(1)} %get-tuple-element.146.hidden_ref.hidden_in) | copy-start | bytes 6291460
  169.8 65.6 %copy-start.23 = (bf16[128,384]{1,0:T(8,128)(2,1)}, bf16[128,384]{1,0:T(8,128)(2,1)S(1)}, u32[]{:S(2)}) copy-start(bf16[128,384]{1,0:T(8,128)(2,1)S(1)} %get-tuple-element.176.refs_14_) | copy-start | bytes 294916
  177.8 58.5 %copy-start.33 = (f32[256]{0:T(256)S(1)}, f32[256]{0:T(256)}, u32[]{:S(2)}) copy-start(f32[256]{0:T(256)} %param.46) | copy-start | bytes 3076
  177.9 58.5 %copy-start.35 = (s32[20]{0:T(128)S(1)}, s32[20]{0:T(128)}, u32[]{:S(2)}) copy-start(s32[20]{0:T(128)} %home.3) | copy-start | bytes 244
  177.9 58.5 %copy-start.40 = (s32[20,32]{1,0:T(8,128)S(1)}, s32[20,32]{1,0:T(8,128)}, u32[]{:S(2)}) copy-start(s32[20,32]{1,0:T(8,128)} %counts_in.3) | copy-start | bytes 7684
  177.9 58.5 %copy-start.43 = (bf16[640,256]{1,0:T(8,128)(2,1)S(1)}, bf16[640,256]{1,0:T(8,128)(2,1)}, u32[]{:S(2)}) copy-start(bf16[640,256]{1,0:T(8,128)(2,1)} %copy-done.42) | copy-start | bytes 983044
  236.3 21.9 %copy-start.2 = (bf16[512,512]{1,0:T(8,128)(2,1)}, bf16[512,512]{1,0:T(8,128)(2,1)S(1)}, u32[]{:S(2)}) copy-start(bf16[512,512]{1,0:T(8,128)(2,1)S(1)} %get-tuple-element.169.refs_2_.upper) | copy-start | bytes 1572868
  236.3 21.9 %copy-start.3 = (bf16[512,512]{1,0:T(8,128)(2,1)}, bf16[512,512]{1,0:T(8,128)(2,1)S(1)}, u32[]{:S(2)}) copy-start(bf16[512,512]{1,0:T(8,128)(2,1)S(1)} %get-tuple-element.170.refs_3_.lower) | copy-start | bytes 1572868
  236.3 21.9 %copy-start.4 = (bf16[512,512]{1,0:T(8,128)(2,1)}, bf16[512,512]{1,0:T(8,128)(2,1)S(1)}, u32[]{:S(2)}) copy-start(bf16[512,512]{1,0:T(8,128)(2,1)S(1)} %get-tuple-element.168.refs_1_.output) | copy-start | bytes 1572868
  236.3 21.9 %copy-start.5 = (bf16[512,384]{1,0:T(8,128)(2,1)}, bf16[512,384]{1,0:T(8,128)(2,1)S(1)}, u32[]{:S(2)}) copy-start(bf16[512,384]{1,0:T(8,128)(2,1)S(1)} %get-tuple-element.167.refs_0_.project) | copy-start | bytes 1179652
  (21 other events, 90.6 us)
Sparse Core Ops, SparseCore 0:
  236.5 58.3 all-reduce.1

commit v2 on v1

--- a/solution.py
+++ b/solution.py
@@ -54,6 +54,12 @@
     return ((row % words) * SPOTS + row // words == col).astype(BF)
 
 
+def back_matrix(places, words):
+    row = lax.broadcasted_iota(jnp.int32, (SPOTS * words, 128), 0)
+    col = lax.broadcasted_iota(jnp.int32, (SPOTS * words, 128), 1)
+    return ((col % words) * SPOTS + col // words == row).astype(BF)
+
+
 def head_stack(rows, scale):
     lane = lax.broadcasted_iota(jnp.int32, (1, CW), 1) // CHD
     return jnp.concatenate(
@@ -62,12 +68,31 @@
 
 
 def char_forward_kernel(
-    classes, home, first, x_ref, counts_in, gain_ref, mats_ref, *refs
+    classes, home, first, x_in, counts_in, gain_ref, mats_ref, *refs
 ):
     orders, refs = refs[-len(classes) :], refs[: -len(classes)]
-    vec_ref, kept_out, pooled_ref, msum_ref, kept, sumx, count_ref, kind, ids, batch_kind, sems = refs
+    vec_ref, kept_out, pooled_ref, msum_ref, kept, sumx, x_ref, vec, count_ref, kind, ids, batch_kind, target, taken, sems, x_sems = refs
     slots, share = count_ref.shape[:2]
     batches = plan_batches(classes, home, first, kind, ids, batch_kind)
+
+    def load_x(slot):
+        return pltpu.make_async_copy(x_in.at[slot], x_ref.at[slot], x_sems.at[slot])
+
+    def begin(number, carry):
+        for which, places, words, per in classes:
+
+            @pl.when(batch_kind[number] == which)
+            def _(per=per):
+                for t in range(per):
+                    slot = ids[number * GROUPS + t]
+
+                    @pl.when(slot >= 0)
+                    def _(slot=slot):
+                        load_x(slot).start()
+
+        return carry
+
+    lax.fori_loop(0, batches, begin, 0)
     count_ref[...] = spread_counts(counts_in[...]).reshape(count_ref.shape)
     for (_, places, words, _), order_ref in zip(classes, orders):
         order_ref[...] = order_matrix(places, words)
@@ -80,8 +105,14 @@
         )
 
     def block(places, words, per, order_ref, number):
-        chosen = [ids[number * GROUPS + t] for t in range(per)]
-        chosen = [jnp.where(c < 0, chosen[0], c) for c in chosen]
+        picked = [ids[number * GROUPS + t] for t in range(per)]
+        for slot in picked:
+
+            @pl.when(slot >= 0)
+            def _(slot=slot):
+                load_x(slot).wait()
+
+        chosen = [jnp.where(c < 0, picked[0], c) for c in picked]
         groups = [(c, g) for c in chosen for g in range(share // words)]
         cnts = [count_ref[c, pl.ds(g * words, words), :] for c, g in groups]
         xs = [
@@ -152,7 +183,18 @@
     summed = sumx[...] + nn(msum_ref[...].astype(BF), mats_ref[:, 3 * CW : 4 * CW])
     pooled = (summed / cnt2).astype(BF)
     pooled_ref[...] = pooled
-    vec_ref[...] = nn(pooled, mats_ref[:, 4 * CW :]).astype(BF)
+    vec[...] = nn(pooled, mats_ref[:, 4 * CW :]).astype(BF)
+    plan_targets(home, target, taken, taken.shape[0])
+    vec_ref[...] = jnp.zeros_like(vec_ref)
+
+    def put(slot, carry):
+        @pl.when(target[slot] >= 0)
+        def _():
+            vec_ref[target[slot]] = vec[pl.ds(pl.multiple_of(slot * share, share), share), :]
+
+        return carry
+
+    lax.fori_loop(0, slots, put, 0)
 
     def finish(slot, carry):
         for which, places, words, per in classes:
@@ -200,6 +242,26 @@
         batch, place = lax.fori_loop(0, slots, take, (batch, jnp.int32(0)))
         batch = jnp.where(place > 0, batch + 1, batch)
     return batch
+
+
+def plan_targets(home, target, taken, owners):
+    slots = home.shape[0]
+    cap = -(-slots // owners)
+
+    def clear(owner, carry):
+        taken[owner] = 0
+        return carry
+
+    lax.fori_loop(0, owners, clear, 0)
+
+    def take(slot, carry):
+        owner = jnp.maximum(home[slot], 0)
+        live = home[slot] >= 0
+        target[slot] = jnp.where(live, owner * cap + taken[owner], -1)
+        taken[owner] = taken[owner] + jnp.where(live, 1, 0)
+        return carry
+
+    lax.fori_loop(0, slots, take, 0)
 
 
 def spread_counts(count):
@@ -228,17 +290,20 @@
     )(*scalars, *inputs)
 
 
-def plan_scratch(slots, share):
+def plan_scratch(slots, share, owners):
     return [
         pltpu.VMEM((slots, share, 128), F32),
         pltpu.SMEM((slots,), jnp.int32),
         pltpu.SMEM((slots * GROUPS,), jnp.int32),
         pltpu.SMEM((slots,), jnp.int32),
+        pltpu.SMEM((slots,), jnp.int32),
+        pltpu.SMEM((owners,), jnp.int32),
     ]
 
 
-def char_forward(x, home, counts, gain, mats):
+def char_forward(x, home, counts, gain, mats, owners):
     slots, share = x.shape[:2]
+    total = -(-slots // owners) * owners
     classes = char_classes(share)
     rows = share * SPOTS
     orders = [pltpu.VMEM((128, SPOTS * c[2]), BF) for c in classes]
@@ -249,7 +314,7 @@
         [x.reshape(slots, rows, CW), counts, gain.reshape(1, CW), mats],
         (home, counts),
         [
-            jax.ShapeDtypeStruct((words_all, D), BF),
+            jax.ShapeDtypeStruct((total, share, D), BF),
             jax.ShapeDtypeStruct((slots, rows, KEPT), BF),
             jax.ShapeDtypeStruct((words_all, CW), BF),
             jax.ShapeDtypeStruct((words_all, CW), F32),
@@ -257,23 +322,26 @@
         [
             pltpu.VMEM((slots, rows, KEPT), BF),
             pltpu.VMEM((words_all, CW), F32),
+            pltpu.VMEM((slots, rows, CW), BF),
+            pltpu.VMEM((words_all, D), BF),
         ]
-        + plan_scratch(slots, share)
-        + [pltpu.SemaphoreType.DMA((slots,))]
+        + plan_scratch(slots, share, owners)
+        + [pltpu.SemaphoreType.DMA((slots,))] * 2
         + orders,
-        (),
+        (0,),
         (1,),
         slots * rows * CW * CW * 16,
-        46,
+        60,
     )
 
 
 def char_backward_kernel(
-    classes, home, first, x_in, counts_in, kept_in, gv_ref, pooled_ref, msum_ref, gain_ref, mats_ref, *refs
+    classes, home, first, x_in, counts_in, kept_in, gv_ref, pooled_ref, msum_ref, gain_ref, mats_ref, stream_in, *refs
 ):
+    backs, refs = refs[-len(classes) :], refs[: -len(classes)]
     orders, refs = refs[-len(classes) :], refs[: -len(classes)]
-    dx_out, grads_ref, dgain_ref, x_ref, kept, dx_ref, gp_all, gm_all, dqkv_sum, count_ref = refs[:10]
-    kind, ids, batch_kind, x_sems, kept_sems, dx_sems = refs[10:]
+    dx_out, grads_ref, dgain_ref, stream_out, x_ref, kept, dx_ref, gp_all, gm_all, dqkv_sum, gv_all, count_ref = refs[:12]
+    kind, ids, batch_kind, target, taken, x_sems, kept_sems, dx_sems, stream_sem = refs[12:]
     slots, share = count_ref.shape[:2]
     batches = plan_batches(classes, home, first, kind, ids, batch_kind)
 
@@ -304,11 +372,30 @@
         return carry
 
     lax.fori_loop(0, batches, begin, 0)
+    stream_copy = pltpu.make_async_copy(stream_in, stream_out, stream_sem.at[0])
+    stream_copy.start()
 
     count_ref[...] = spread_counts(counts_in[...]).reshape(count_ref.shape)
-    for (_, places, words, _), order_ref in zip(classes, orders):
+    for (_, places, words, _), order_ref, back_ref in zip(classes, orders, backs):
         order_ref[...] = order_matrix(places, words)
-    gv = gv_ref[...]
+        back_ref[...] = back_matrix(places, words)
+    plan_targets(home, target, taken, taken.shape[0])
+
+    def take(slot, carry):
+        here = pl.ds(pl.multiple_of(slot * share, share), share)
+
+        @pl.when(target[slot] >= 0)
+        def _():
+            gv_all[here, :] = gv_ref[target[slot]]
+
+        @pl.when(target[slot] < 0)
+        def _():
+            gv_all[here, :] = jnp.zeros((share, D), BF)
+
+        return carry
+
+    lax.fori_loop(0, slots, take, 0)
+    gv = gv_all[...]
     cnt2 = jnp.concatenate([count_ref[...].reshape(slots * share, 128)] * 2, axis=1)
     gp = nt(gv, mats_ref[:, 4 * CW :]) / cnt2
     gp_all[...] = gp
@@ -319,7 +406,7 @@
     dqkv_sum[...] = jnp.zeros_like(dqkv_sum)
     dgain_ref[...] = jnp.zeros_like(dgain_ref)
 
-    def block(places, words, per, order_ref, number):
+    def block(places, words, per, order_ref, back_ref, number):
         picked = [ids[number * GROUPS + t] for t in range(per)]
         chosen = [jnp.where(c < 0, picked[0], c) for c in picked]
         weights = [jnp.where(c < 0, 0.0, 1.0) for c in picked]
@@ -392,8 +479,8 @@
             w = dn * gain
             inner = jnp.mean(xr * w, axis=-1, keepdims=True)
             dx = out_grads[t] + scale * (w - xr * inner)
-            dx_ref[target, pl.ds(g * words * SPOTS, words * SPOTS), :] = tn(
-                order_ref[...], dx.astype(BF)
+            dx_ref[target, pl.ds(g * words * SPOTS, words * SPOTS), :] = nn(
+                back_ref[...], dx.astype(BF)
             ).astype(BF)
         dgain_ref[...] += dgain
         for slot in picked:
@@ -403,9 +490,9 @@
                 save(slot).start()
 
     def batch(number, carry):
-        for (which, places, words, per), order_ref in zip(classes, orders):
+        for (which, places, words, per), order_ref, back_ref in zip(classes, orders, backs):
             pl.when(batch_kind[number] == which)(
-                functools.partial(block, places, words, per, order_ref, number)
+                functools.partial(block, places, words, per, order_ref, back_ref, number)
             )
         return carry
 
@@ -427,25 +514,28 @@
         return carry
 
     lax.fori_loop(0, slots, finish, 0)
-
-
-def char_backward(x, home, counts, gain, mats, kept, pooled, msum, grad_vectors):
+    stream_copy.wait()
+
+
+def char_backward(x, home, counts, gain, mats, kept, pooled, msum, grad_vectors, grad_stream, owners):
     slots, share = x.shape[:2]
     classes = char_classes(share)
     rows = share * SPOTS
     orders = [pltpu.VMEM((128, SPOTS * c[2]), BF) for c in classes]
     words_all = slots * share
-    dx, grads, dgain = char_call(
+    dx, grads, dgain, stream = char_call(
         functools.partial(char_backward_kernel, classes),
         "char_backward",
         [
             x.reshape(slots, rows, CW), counts, kept, grad_vectors, pooled, msum, gain.reshape(1, CW), mats,
+            grad_stream,
         ],
         (home, counts),
         [
             jax.ShapeDtypeStruct((slots, rows, CW), BF),
             jax.ShapeDtypeStruct(mats.shape, BF),
             jax.ShapeDtypeStruct((1, CW), F32),
+            jax.ShapeDtypeStruct(grad_stream.shape, grad_stream.dtype),
         ],
         [
             pltpu.VMEM((slots, rows, CW), BF),
@@ -454,16 +544,19 @@
             pltpu.VMEM((words_all, CW), F32),
             pltpu.VMEM((words_all, CW), F32),
             pltpu.VMEM((CW, 3 * CW), F32),
+            pltpu.VMEM((words_all, D), BF),
         ]
-        + plan_scratch(slots, share)
+        + plan_scratch(slots, share, owners)
         + [pltpu.SemaphoreType.DMA((slots,))] * 3
-        + orders,
+        + [pltpu.SemaphoreType.DMA((1,))]
+        + orders
+        + [pltpu.VMEM((SPOTS * c[2], 128), BF) for c in classes],
         (0, 2),
-        (0,),
+        (0, 3),
         slots * rows * CW * CW * 28,
         53,
     )
-    return dx.reshape(x.shape), grads, dgain
+    return dx.reshape(x.shape), grads, dgain, stream
 
 
 MESH_ID = pl.DeviceIdType.MESH
@@ -548,9 +641,9 @@
     return [(begin, start), (late, onward), (80.0, finish)]
 
 
-def line_gather_stages(out, sems, axis, n, mine, begin, each, cols=None):
+def line_gather_stages(out, sems, axis, n, mine, begin, each, cut=()):
     def piece(block):
-        return out.at[block] if cols is None else out.at[block, :, cols]
+        return out.at[(block,) + cut]
 
     def step(k):
         for way in range(2):
@@ -586,7 +679,7 @@
     return stages + [(95.0, finish)]
 
 
-def line_part_stages(x, held, out, sems, axis, n, mine, begin, each):
+def line_part_stages(x, held, out, sems, axis, n, mine, begin, each, end=70.0, cut=()):
     def step(t):
         for way in range(2):
             distance = mine if way == 0 else n - 1 - mine
@@ -599,24 +692,28 @@
 
             @pl.when(here & (distance == 0))
             def _(way=way, block=block, peer=peer, at=at):
-                remote(x.at[block], held.at[way, block], sems, at, axis, peer).start()
+                remote(
+                    x.at[(block,) + cut], held.at[(way, block) + cut], sems, at, axis, peer
+                ).start()
 
             @pl.when(here & (distance > 0))
             def _(way=way, block=block, peer=peer, at=at):
-                place = held.at[way, block]
+                place = held.at[(way, block) + cut]
                 remote(place, place, sems, at, axis, mine).wait_recv()
-                held[way, block] = (held[way, block].astype(F32) + x[block].astype(F32)).astype(x.dtype)
+                held[(way, block) + cut] = (
+                    held[(way, block) + cut].astype(F32) + x[(block,) + cut].astype(F32)
+                ).astype(x.dtype)
                 remote(place, place, sems, at, axis, peer).start()
 
     def finish():
-        out[...] = x[mine].astype(F32)
+        out[cut or ...] = x[(mine,) + cut].astype(F32)
         for way, there in ((0, mine > 0), (1, mine < n - 1)):
 
             @pl.when(there)
             def _(way=way):
-                here = held.at[way, mine]
+                here = held.at[(way, mine) + cut]
                 remote(here, here, sems, way * n + mine, axis, mine).wait_recv()
-                out[...] += held[way, mine].astype(F32)
+                out[cut or ...] += held[(way, mine) + cut].astype(F32)
 
         for way in range(2):
             for block in range(n):
@@ -624,11 +721,15 @@
 
                 @pl.when(further)
                 def _(way=way, block=block):
-                    here = held.at[way, block]
+                    here = held.at[(way, block) + cut]
                     remote(here, here, sems, way * n + block, axis, mine).wait_send()
 
     stages = [(begin + each * k, functools.partial(step, k)) for k in range(n - 1)]
-    return stages + [(70.0, finish)]
+    return stages + [(end, finish)]
+
+
+def halves(rows):
+    return [(slice(h * (rows // 2), (h + 1) * (rows // 2)), slice(None)) for h in range(2)]
 
 
 def direct_stages(source_of, target, sems, axis, n, mine, begin, done, end, cols=None):
@@ -678,7 +779,7 @@
         outs.append(made)
         shapers.append(shaper)
         counts.append(len(arrays))
-        scratch += [pltpu.SemaphoreType.DMA((2 * n,)), pltpu.SemaphoreType.DMA((2 * n,))]
+        scratch += [pltpu.SemaphoreType.DMA((4 * n,)), pltpu.SemaphoreType.DMA((4 * n,))]
         if kind == "part":
             scratch += [pltpu.VMEM((n // 2,) + block, array.dtype)] * 2
         if kind == "total":
@@ -702,7 +803,9 @@
             n, mine, x = sizes[axis], me[axis], xs[0]
             if kind == "line_gather":
                 out[mine] = x[...]
-                stages += line_gather_stages(out, sems, axis, n, mine, 0.0, 6.0)
+                for h, cut in enumerate(halves(x.shape[0])):
+                    sems_half = tuple(s.at[pl.ds(2 * n * h, 2 * n)] for s in sems)
+                    stages += line_gather_stages(out, sems_half, axis, n, mine, 0.05 * h, 6.0, cut)
             elif kind == "line_part":
                 stages += line_part_stages(x, rest.pop(0), out, sems, axis, n, mine, 0.0, 6.0)
             elif kind == "part":
@@ -903,7 +1006,7 @@
 
 def word_forward_kernel(
     width, vec_ref, place_ref, words_ref, doc_all_ref, doc_row_ref, gain_ref, project_ref,
-    stream_ref, normed_ref, qkv_ref, probs_ref, mixed_ref, keys, values, doc_ref
+    stream_ref, normed_ref, qkv_ref, probs_ref, mixed_ref, keys, values, doc_ref, placed
 ):
     step = pl.program_id(0)
     parts, kept_rows = vec_ref.shape[:2]
@@ -912,15 +1015,15 @@
     @pl.when(step == 0)
     def _():
         doc_ref[...] = tn(doc_all_ref[...].astype(F32).astype(BF), jnp.ones((1, 128), BF))
-
-    numbers = lax.broadcasted_iota(jnp.int32, (ROWS, parts * words), 0) + step * ROWS
-    placed = jnp.zeros((ROWS, D), F32)
-    for k in range(0, OWNER_BLOCKS, 2):
-        pair = range(k, min(k + 2, OWNER_BLOCKS))
-        hits = [(numbers == place_ref[b : b + 1, :]).astype(BF) for b in pair]
-        vectors = [vec_ref[p, b * words : (b + 1) * words, :] for b in pair for p in range(parts)]
-        placed = placed + nn(jnp.concatenate(hits, axis=1), jnp.concatenate(vectors, axis=0))
-    stream = words_ref[...].astype(F32) + placed
+        numbers = lax.broadcasted_iota(jnp.int32, (placed.shape[0], parts * words), 0)
+        hits = [(numbers == place_ref[b : b + 1, :]).astype(BF) for b in range(OWNER_BLOCKS)]
+        vectors = [
+            vec_ref[p, b * words : (b + 1) * words, :] for b in range(OWNER_BLOCKS) for p in range(parts)
+        ]
+        placed[...] = nn(jnp.concatenate(hits, axis=1), jnp.concatenate(vectors, axis=0))
+
+    here = pl.ds(pl.multiple_of(step * ROWS, ROWS), ROWS)
+    stream = words_ref[...].astype(F32) + placed[here, :]
     stream_ref[...] = stream
     normed = (stream * rms_scale(stream) * gain_ref[...]).astype(BF)
     normed_ref[...] = normed
@@ -987,6 +1090,7 @@
             pltpu.VMEM((length, width), BF),
             pltpu.VMEM((length, width), BF),
             pltpu.VMEM((length, 128), F32),
+            pltpu.VMEM((length, D), F32),
         ],
         compiler_params=pltpu.CompilerParams(vmem_limit_bytes=32 << 20),
         name="word_forward",
@@ -999,6 +1103,9 @@
         gain.reshape(1, D),
         project,
     )
+
+
+FEED_ROWS = 512
 
 
 def feed_kernel(
@@ -1040,13 +1147,13 @@
 
 def feed(mixed, output, stream, cotangent, gain, upper, lower):
     length = stream.shape[0]
-    rows = pl.BlockSpec((ROWS, D), lambda i: (i, 0))
+    rows = pl.BlockSpec((FEED_ROWS, D), lambda i: (i, 0))
     full = lambda shape: pl.BlockSpec(shape, lambda i: (0,) * len(shape))
     return pl.pallas_call(
         feed_kernel,
-        grid=(length // ROWS,),
+        grid=(length // FEED_ROWS,),
         in_specs=[
-            pl.BlockSpec((mixed.shape[0], ROWS, mixed.shape[2]), lambda i: (0, i, 0)),
+            pl.BlockSpec((mixed.shape[0], FEED_ROWS, mixed.shape[2]), lambda i: (0, i, 0)),
             full(output.shape),
             rows,
             rows,
@@ -1360,17 +1467,6 @@
         run()
 
 
-def spread_blocks(chosen, rows, cols, share):
-    up = lax.broadcasted_iota(jnp.int32, (rows, chosen.shape[0]), 0) // share
-    up = (up == lax.broadcasted_iota(jnp.int32, (rows, chosen.shape[0]), 1)).astype(BF)
-    down = lax.broadcasted_iota(jnp.int32, (chosen.shape[1], cols), 1) // share
-    down = (down == lax.broadcasted_iota(jnp.int32, (chosen.shape[1], cols), 0)).astype(BF)
-    wide = nn(nn(up, chosen).astype(BF), down)
-    row = lax.broadcasted_iota(jnp.int32, (rows, cols), 0) % share
-    col = lax.broadcasted_iota(jnp.int32, (rows, cols), 1) % share
-    return jnp.where(row == col, wide, 0.0).astype(BF)
-
-
 def gather_setup(xs, out):
     rows = xs[0].shape[1]
 
@@ -1426,7 +1522,7 @@
 
     def kernel(
         mixer_in, lift_in, output_in, home_row, place_ref,
-        mats, line, to_slot, live, live_place, own_row, mixer_ref, lift_ref, output_ref, sent, came, local, *sems
+        mats, line, live, live_place, own_row, mixer_ref, lift_ref, output_ref, sent, came, local, *sems
     ):
         pairs = [tuple(sems[2 * t : 2 * t + 2]) for t in range(3)]
         i, j = lax.axis_index("dp"), lax.axis_index("mp")
@@ -1457,7 +1553,6 @@
             )
             hit = lax.broadcasted_iota(jnp.int32, (total, slots), 0).astype(F32) == target
             chosen = hit.astype(F32)
-            to_slot[...] = chosen.astype(BF)
             placed = jnp.zeros((total, block_words), F32) - 1.0
             for s in range(slots):
                 placed = jnp.where(
@@ -1505,13 +1600,12 @@
         out_shape=[
             shape,
             jax.ShapeDtypeStruct((m, rows, D), BF),
-            jax.ShapeDtypeStruct((total, slots), BF),
             jax.ShapeDtypeStruct((total, 128), BF),
             jax.ShapeDtypeStruct((lines, block_words), jnp.int32),
             jax.ShapeDtypeStruct((n, 1, cap * share), jnp.int32),
         ],
         in_specs=[hbm] * 3 + [vmem] * 2,
-        out_specs=[vmem] * 6,
+        out_specs=[vmem] * 5,
         scratch_shapes=[
             pltpu.VMEM(mixer.shape, F32),
             pltpu.VMEM(lift.shape, F32),
@@ -1529,10 +1623,10 @@
     return [shaper(results[0])] + list(results[1:])
 
 
-def send_vectors(vectors, to_slot, to_live, share, project, upper, lower, output_line):
+def send_vectors(sent, to_live, share, project, upper, lower, output_line):
     n, m = lax.axis_size("dp"), lax.axis_size("mp")
-    total = to_slot.shape[0] * share
-    block = total // n
+    block = sent.shape[1]
+    total = n * block
     kept = OWNER_BLOCKS * share
     made = [gather_shape([a], n) for a in (project, upper, lower)]
     made[0] = gather_shape([project], n)
@@ -1540,22 +1634,17 @@
     aligned = line_rows % 16 == 0
     output_shape = (lead, n * line_rows, line_cols) if aligned else (n, lead, line_rows, line_cols)
 
-    def kernel(vec, slots, live, *refs):
+    def kernel(sent, live, *refs):
         weights, line = refs[:3], refs[3]
         out, wides, output = refs[4], refs[5:8], refs[8]
-        sent, came, *sems = refs[9:]
+        came, spread, *sems = refs[9:]
         pairs = [tuple(sems[2 * t : 2 * t + 2]) for t in range(8)]
         i, j = lax.axis_index("dp"), lax.axis_index("mp")
-        sent[...] = (
-            nn(spread_blocks(slots[...], total, vec.shape[0], share), vec[...])
-            .astype(BF)
-            .reshape(sent.shape)
-        )
         greet({"dp": n, "mp": m}, {"dp": i, "mp": j})
         came[i] = sent[i]
         stages = []
 
-        def compact(cols):
+        def make_spread():
             up = lax.broadcasted_iota(jnp.int32, (kept, 128), 0) // share
             up = (up == lax.broadcasted_iota(jnp.int32, (kept, 128), 1)).astype(BF)
             blocks = nt(up, live[...]).astype(BF)
@@ -1563,8 +1652,12 @@
             down = (down == lax.broadcasted_iota(jnp.int32, (blocks.shape[1], total), 0)).astype(BF)
             row = lax.broadcasted_iota(jnp.int32, (kept, total), 0) % share
             col = lax.broadcasted_iota(jnp.int32, (kept, total), 1) % share
-            spread = jnp.where(row == col, nn(blocks, down), 0.0).astype(BF)
-            out[j, :, cols] = nn(spread, came[:, :, cols].reshape(total, D // 2)).astype(BF)
+            spread[...] = jnp.where(row == col, nn(blocks, down), 0.0).astype(BF)
+
+        stages.append((0.4, make_spread))
+
+        def compact(cols):
+            out[j, :, cols] = nn(spread[...], came[:, :, cols].reshape(total, D // 2)).astype(BF)
 
         for half in range(2):
             cols = slice(half * (D // 2), (half + 1) * (D // 2))
@@ -1572,8 +1665,9 @@
                 lambda p, cols=cols: sent.at[p, :, cols], came, pairs[6 * half], "dp", n, i, 0.1 * half,
                 functools.partial(compact, cols), 1.0 + half, cols,
             )
-            begin = 1.5 + half * (m - 1.5)
-            stages += line_gather_stages(out, pairs[1 + 6 * half], "mp", m, j, begin, 1.0, cols)
+            stages += line_gather_stages(
+                out, pairs[1 + 6 * half], "mp", m, j, 1.5 + 0.6 * half, 1.0, (slice(None), cols)
+            )
         for t, (x, wide) in enumerate(zip(weights, wides)):
             own_of, put = gather_setup([x], wide)
             put(i)
@@ -1593,8 +1687,8 @@
         [jax.ShapeDtypeStruct((m, kept, D), BF)]
         + [shape for shape, _ in made]
         + [jax.ShapeDtypeStruct(output_shape, BF)],
-        [pltpu.VMEM((n, block, D), BF)] * 2 + dma_sems(2 * max(n, m)) * 8,
-        [vectors, to_slot, to_live, project, upper, lower, output_line],
+        [pltpu.VMEM((n, block, D), BF), pltpu.VMEM((kept, total), BF)] + dma_sems(2 * max(n, m)) * 8,
+        [sent, to_live, project, upper, lower, output_line],
     )
     output = results[4]
     if not aligned:
@@ -1618,10 +1712,14 @@
         grad_hidden, grad_mixed, grad_output, gain_grad, up_sum, low_sum = refs[:6]
         roots_out, refs = refs[6 : 6 + len(roots)], refs[6 + len(roots) :]
         held, total, swapped, up_held, up_came, low_held, low_came, *sems = refs
-        pairs = [tuple(sems[2 * t : 2 * t + 2]) for t in range(4 + len(roots))]
+        pairs = [tuple(sems[2 * t : 2 * t + 2]) for t in range(5 + len(roots))]
         i, j = lax.axis_index("dp"), lax.axis_index("mp")
         greet({"dp": n, "mp": m}, {"dp": i, "mp": j})
-        stages = line_part_stages(part, held, total, pairs[0], "mp", m, j, 0.0, 6.0)
+        stages = []
+        for h, cut in enumerate(halves(share)):
+            stages += line_part_stages(
+                part, held, total, pairs[(0, 4 + len(roots))[h]], "mp", m, j, 0.05 * h, 6.0, 70.0 + 0.1 * h, cut
+            )
         stages += pair_part_stages(up, up_held, up_came, up_sum, pairs[1], "dp", n, i, 0.1, 1.0)
         stages += pair_part_stages(low, low_held, low_came, low_sum, pairs[2], "dp", n, i, 0.1, 1.0)
         for t, (x, out) in enumerate(zip(roots_in, roots_out)):
@@ -1677,31 +1775,34 @@
             block(parts[1]),
             block(parts[1]),
         ]
-        + dma_sems(2 * max(n, m)) * (4 + len(roots)),
+        + dma_sems(2 * max(n, m)) * (5 + len(roots)),
         [part_two, hidden, cotangent, mixed, output, gain.reshape(1, D)] + parts + roots,
     )
     return list(results[:6]) + [shaper(a) for (_, shaper), a in zip(made, results[6:])]
 
 
-def stream_grads(part_one, stream, grad_hidden, gain, own_row, to_slot, sums, grad_project, grad_output, slots):
+def stream_grads(part_one, stream, grad_hidden, gain, own_row, sums, grad_project, grad_output):
     n, m = lax.axis_size("dp"), lax.axis_size("mp")
     share = part_one.shape[1]
     block = own_row.shape[2]
     total_words = n * block
     words = share * m
-    width = total_words // to_slot.shape[0]
     parts = [by_chip(grad_project), by_chip(grad_output)]
     chunk = lambda a: jax.ShapeDtypeStruct((1,) + a.shape[-2:], F32)
     made = [gather_shape([chunk(a)], n) for a in (sums[0], sums[1], parts[0], parts[1])]
 
-    def kernel(part, stream_ref, hidden_ref, gain_ref, row_ref, slot_ref, up, low, project, output, *refs):
-        out, gain_grad, vectors, up_out, low_out, project_out, output_out = refs[:7]
-        (held, total, project_sum, output_sum, line_held, picked, came,
+    def kernel(part, stream_ref, hidden_ref, gain_ref, row_ref, up, low, project, output, *refs):
+        out, gain_grad, came, up_out, low_out, project_out, output_out = refs[:7]
+        (held, total, project_sum, output_sum, line_held, picked, hits,
          p_held, p_came, o_held, o_came, *sems) = refs[7:]
-        pairs = [tuple(sems[2 * t : 2 * t + 2]) for t in range(12)]
+        pairs = [tuple(sems[2 * t : 2 * t + 2]) for t in range(13)]
         i, j = lax.axis_index("dp"), lax.axis_index("mp")
         greet({"dp": n, "mp": m}, {"dp": i, "mp": j})
-        stages = line_part_stages(part, held, total, pairs[0], "mp", m, j, 0.0, 6.0)
+        stages = []
+        for h, cut in enumerate(halves(share)):
+            stages += line_part_stages(
+                part, held, total, pairs[(0, 12)[h]], "mp", m, j, 0.05 * h, 6.0, 70.0 + 0.1 * h, cut
+            )
         stages += pair_part_stages(project, p_held, p_came, project_sum.at[0], pairs[1], "dp", n, i, 0.1, 1.0)
         stages += pair_part_stages(output, o_held, o_came, output_sum.at[0], pairs[2], "dp", n, i, 0.1, 1.0)
         up_of, put_up = gather_setup([up], up_out)
@@ -1722,10 +1823,11 @@
         stages.append((71.0, back))
         for half in range(2):
             cols = slice(half * (D // 2), (half + 1) * (D // 2))
-            begin = 72.0 + 0.1 * half * (m - 1.5)
             stages += [
                 (when if when < 90 else 199.0, run)
-                for when, run in line_gather_stages(out, pairs[5 + 5 * half], "mp", m, j, begin, 0.1, cols)
+                for when, run in line_gather_stages(
+                    out, pairs[5 + 5 * half], "mp", m, j, 72.0 + 0.05 * half, 0.1, (slice(None), cols)
+                )
             ]
         project_of, put_project = gather_setup([project_sum], project_out)
         output_of, put_output = gather_setup([output_sum], output_out)
@@ -1780,22 +1882,34 @@
             )
         ]
 
+        def make_hits():
+            lane = lax.broadcasted_iota(jnp.int32, (block, 128), 1).astype(F32)
+            ones = jnp.ones((1, 128), BF)
+            for p in range(n):
+                place = row_ref[p].astype(F32) + 1.0
+                high = jnp.floor(place * (1.0 / 32.0))
+                low = place - high * 32.0
+                col = tn(high.astype(BF), ones) * 32.0 + tn(low.astype(BF), ones) - 1.0
+                for t in range(words // 128):
+                    hits[p * block : (p + 1) * block, t * 128 : (t + 1) * 128] = (
+                        col == lane + 128.0 * t
+                    ).astype(BF)
+
+        stages.append((2.5, make_hits))
+
         def pick(half):
             cols = slice(half * (D // 2), (half + 1) * (D // 2))
-            rows = out[:, :, cols].reshape(words, D // 2)
-            number = lax.broadcasted_iota(jnp.int32, (words, block), 0)
-            for d in list(range(1, n)) + [0]:
+            rows = nn(hits[...], out[:, :, cols].reshape(words, D // 2)).astype(BF)
+            picked[:, :, cols] = rows.reshape(n, block, D // 2)
+            for d in range(1, n):
                 peer = lax.rem(i + d, n)
-                picked[peer, :, cols] = tn((number == row_ref[peer]).astype(BF), rows).astype(BF)
-                if d:
-                    remote(
-                        picked.at[peer, :, cols], came.at[i, :, cols], pairs[9 + 2 * half], d, "dp", peer
-                    ).start()
+                remote(
+                    picked.at[peer, :, cols], came.at[i, :, cols], pairs[9 + 2 * half], d, "dp", peer
+                ).start()
             came[i, :, cols] = picked[i, :, cols]
 
         for half in range(2):
-            begin = 72.0 + 0.1 * half * (m - 1.5)
-            stages.append((begin + 0.1 * (m - 1) + 0.011, functools.partial(pick, half)))
+            stages.append((72.011 + 0.1 * (m - 1) + 0.05 * half, functools.partial(pick, half)))
 
         def place():
             for half in range(2):
@@ -1804,8 +1918,6 @@
                     remote(
                         picked.at[i, :, cols], came.at[i, :, cols], pairs[9 + 2 * half], d, "dp", i
                     ).wait()
-            spread = spread_blocks(slot_ref[...], total_words, vectors.shape[0], width)
-            vectors[...] = tn(spread, came[...].reshape(total_words, D)).astype(BF)
 
         stages.append((82.0, place))
         run_stages(stages)
@@ -1818,7 +1930,7 @@
         [
             jax.ShapeDtypeStruct((m, share, D), BF),
             jax.ShapeDtypeStruct((1, D), F32),
-            jax.ShapeDtypeStruct((slots * width, D), BF),
+            jax.ShapeDtypeStruct((n, block, D), BF),
         ]
         + [shape for shape, _ in made],
         [
@@ -1828,20 +1940,19 @@
             pltpu.VMEM((1,) + parts[1].shape[2:], F32),
             pltpu.VMEM((m,) + parts[1].shape[2:], BF),
             pltpu.VMEM((n, block, D), BF),
-            pltpu.VMEM((n, block, D), BF),
+            pltpu.VMEM((total_words, words), BF),
             held_of(parts[0]),
             held_of(parts[0]),
             held_of(parts[1]),
             held_of(parts[1]),
         ]
-        + dma_sems(2 * max(n, m)) * 12,
+        + dma_sems(2 * max(n, m)) * 13,
         [
             part_one,
             stream,
             grad_hidden,
             gain.reshape(1, D),
             own_row,
-            to_slot,
             sums[0][None],
             sums[1][None],
         ]
@@ -1898,15 +2009,14 @@
     words_dev = word_inputs.shape[0] * word_inputs.shape[1]
     position = jnp.stack([owner_index, lax.axis_index("mp")]).astype(jnp.int32)
 
-    char_whole, output_line, to_slot, live, live_place, own_row = gather_char(
+    char_whole, output_line, live, live_place, own_row = gather_char(
         char_mixer, char_lift, word_output, block_home, word_place
     )
     word_vectors, kept, pooled, msum = char_forward(
-        character_embeddings, block_home, char_count, char_gain, char_whole
+        character_embeddings, block_home, char_count, char_gain, char_whole, peer_count
     )
     live_vectors, project_mat, upper_mat, lower_mat, output_mat = send_vectors(
-        word_vectors,
-        to_slot,
+        word_vectors.reshape(peer_count, -1, D),
         live,
         share_rows,
         word_project.reshape((3,) + word_project.shape[2:]),
@@ -1962,17 +2072,17 @@
         grad_hidden,
         word_gains[0],
         own_row,
-        to_slot,
         (part_upper, part_lower),
         grad_project,
         grad_output_mat,
-        slot_count,
-    )
-    word_inputs_gradient = grad_words.reshape(word_inputs.shape)
+    )
     grad_vectors, feed_part = lax.optimization_barrier((grad_vectors, feed_part))
     feed_total = lax.psum(feed_part, "mp")
-    char_embeds_gradient, char_grads, grad_char_gain = char_backward(
-        character_embeddings, block_home, char_count, char_gain, char_whole, kept, pooled, msum, grad_vectors
+    char_embeds_gradient, char_grads, grad_char_gain, grad_stream = char_backward(
+        character_embeddings, block_home, char_count, char_gain, char_whole, kept, pooled, msum,
+        grad_vectors.reshape(-1, share_rows, D),
+        grad_words,
+        peer_count,
     )
     word_sums = (sum_project, sum_output, sum_upper, sum_lower)
     char_sums, small_sums = sum_char_grads(
@@ -2029,7 +2139,7 @@
         ]
     return (
         block_out.reshape(word_inputs.shape),
-        word_inputs_gradient,
+        grad_stream.reshape(word_inputs.shape),
         char_embeds_gradient,
         gain_grad[0],
         gains_grad,

time: 327 us -> 313 us (0.957)
  local copies, waits for them, and re-layouts: 16 us -> 8.23 us
  Pallas kernels: 292 us -> 285 us
    pallas_call x2, Pallas kernels: 35.3 us -> 48.7 us  [char_call(): pl.pallas_call(kernel, in_specs=[smem] * len(scalars) + [hbm if t in in_h...]
    pallas_call x3, Pallas kernels: 137 us -> 127 us  [call_remote(): pl.pallas_call(kernel, out_shape=outs, in_specs=[vmem] * len(inputs), out...]
    unnamed x89 -> x74, local copies, waits for them, and re-layouts: 15.2 us -> 7.46 us
    pallas_call x1, Pallas kernels: 41.5 us -> 34.9 us  [sum_char_grads(): pl.pallas_call(kernel, out_shape=[jax.ShapeDtypeStruct((n * rows, cols) i...]
where the time goes in v2:
time: 313 us; the launch traced here: 309 us
  Pallas kernels  285 us (91%)
  between operations  14.9 us (5%)
  local copies, waits for them, and re-layouts  8.23 us (3%)
    pallas_call x3, Pallas kernels, call_remote(): pl.pallas_call(kernel, out_shape=outs, in_specs=[vmem] * len(inputs), out...  127 us
    pallas_call x2, Pallas kernels, char_call(): pl.pallas_call(kernel, in_specs=[smem] * len(scalars) + [hbm if t in in_h...  48.7 us
    pallas_call x1, Pallas kernels, sum_char_grads(): pl.pallas_call(kernel, out_shape=[jax.ShapeDtypeStruct((n * rows, cols) i...  34.9 us
    pallas_call x1, Pallas kernels, exchange(): pl.pallas_call(kernel, out_shape=outs, in_specs=[vmem] * total_ins, out_s...  21.7 us
    pallas_call x1, Pallas kernels, gather_char(): pl.pallas_call(kernel, out_shape=[shape, jax.ShapeDtypeStruct((m, rows, D...  16.4 us
    pallas_call x1, Pallas kernels, shampoo(): pl.pallas_call(functools.partial(shampoo_kernel, threshold), in_specs=[sm...  12 us
    pallas_call x1, Pallas kernels, word_forward(): pl.pallas_call(functools.partial(word_forward_kernel, width), grid=(lengt...  9.8 us
    pallas_call x1, Pallas kernels, word_backward(): pl.pallas_call(functools.partial(word_backward_kernel, width), grid=(leng...  8.05 us
  transfers between devices with their start and end apart: 1, of which 0 were waited for; matrix products, arithmetic and copies ran while one was open for 0% of the time, Pallas kernels for 20%

profile of v2, /device:TPU:0, one launch (start us, length us, event | category | flops | bytes accessed | tf_op | source)
XLA Modules:
  0.0 309.1 jit_solution(270327496187740152)
XLA Ops:
  7.2 0.0 all-reduce.2.cloned.1.call-start
  7.3 0.8 fusion
  8.0 16.4 %gather_char.1 = (bf16[256,1536]{1,0:T(8,128)(2,1)}, bf16[4,16,512]{2,1,0:T(8,128)(2,1)}, bf16[24,128]{1,0:T(8,128)(2,1)}, s32[16,128]{1,0:T(8,128)}, s32[8,1,96]{2,1,0:T(1,128)}) custom-call(f32[4,32,256]{2,1,0:T(8,128)} %refs_0_.1, f32[1,32,512]{2,1,0:T(8,128)} %refs_5_.1, f32[1,16,512]{2,1,0:T(8,128)} %refs_15_.1, s32[1,20]{1,0:T(1,128)} %bitcast.68, ...), custom_call_target="tpu_custom_call" | custom-call | tf_op jit(solution)/shard_map/gather_char/pallas_call | solution.py:1598
  24.6 20.6 %char_forward.1 = (bf16[24,32,512]{2,1,0:T(8,128)(2,1)}, bf16[20,512,1536]{2,1,0:T(8,128)(2,1)}, bf16[640,256]{1,0:T(8,128)(2,1)}, f32[640,256]{1,0:T(8,128)}) custom-call(s32[20]{0:T(128)} %home.3, s32[20,32]{1,0:T(8,128)} %counts_in.3, bf16[20,512,256]{2,1,0:T(8,128)(2,1)} %bitcast.73, s32[20,32]{1,0:T(8,128)} %counts_in.3, f32[1,256]{1,0:T(1,128)} %bitcast.65, ...), custom_call_target="tpu_custom_call" | custom-call | flops 10737418240 | bytes 62914560 | tf_op jit(solution)/shard_map/char_forward/pallas_call | solution.py:281
  45.2 1.2 copy-done.8
  46.4 39.2 %send_vectors.1 = (bf16[4,320,512]{2,1,0:T(8,128)(2,1)S(1)}, bf16[512,384]{1,0:T(8,128)(2,1)S(1)}, bf16[512,512]{1,0:T(8,128)(2,1)S(1)}, bf16[512,512]{1,0:T(8,128)(2,1)S(1)}, bf16[4,128,512]{2,1,0:T(8,128)(2,1)S(1)}) custom-call(bf16[8,96,512]{2,1,0:T(8,128)(2,1)S(1)} %bitcast.53, bf16[24,128]{1,0:T(8,128)(2,1)S(1)} %copy-done.29, ...), custom_call_target="tpu_custom_call" | custom-call | tf_op jit(solution)/shard_map/send_vectors/pallas_call | solution.py:1501
  85.8 9.8 %word_forward.1 = (f32[1024,512]{1,0:T(8,128)S(1)}, bf16[1024,512]{1,0:T(8,128)(2,1)S(1)}, bf16[1024,384]{1,0:T(8,128)(2,1)S(1)}, bf16[2,1024,1024]{2,1,0:T(8,128)(2,1)S(1)}, bf16[1024,128]{1,0:T(8,128)(2,1)S(1)}) custom-call(bf16[4,320,512]{2,1,0:T(8,128)(2,1)S(1)} %get-tuple-element.133.vec_ref, s32[16,128]{1,0:T(8,128)S(1)} %copy-done.28, ...), custom_call_target="tpu_custom_call" | custom-call | tf_op jit(solution)/shard_map/word_forward/pallas_call | solution.py:1063
  95.6 21.7 %gather_mixed.1 = (bf16[4,1024,128]{2,1,0:T(8,128)(2,1)S(1)}, bf16[256,1024]{1,0:T(8,128)(2,1)S(1)}, bf16[512,512]{1,0:T(8,128)(2,1)S(1)}) custom-call(bf16[1024,128]{1,0:T(8,128)(2,1)S(1)} %get-tuple-element.138.refs_0_, f32[4,32,256]{2,1,0:T(8,128)S(1)} %copy-done.21, f32[1,64,512]{2,1,0:T(8,128)S(1)} %copy-done.22), custom_call_target="tpu_custom_call" | custom-call | tf_op jit(solution)/shard_map/gather_mixed/pallas_call | solution.py:873
  117.3 0.8 copy-done.12
  118.0 0.8 copy-done.13
  118.9 6.5 %feed.1 = (f32[1024,512]{1,0:T(8,128)S(1)}, bf16[1024,512]{1,0:T(8,128)(2,1)}, bf16[1024,512]{1,0:T(8,128)(2,1)S(1)}, bf16[512,512]{1,0:T(8,128)(2,1)S(1)}, bf16[512,512]{1,0:T(8,128)(2,1)S(1)}) custom-call(bf16[4,1024,128]{2,1,0:T(8,128)(2,1)S(1)} %get-tuple-element.139.mixed_ref.mix, bf16[512,512]{1,0:T(8,128)(2,1)S(1)} %bitcast.48, ...), custom_call_target="tpu_custom_call" | custom-call | tf_op jit(solution)/shard_map/feed/pallas_call | solution.py:1152
  125.4 28.8 %hidden_grads.1 = (f32[256,512]{1,0:T(8,128)S(1)}, bf16[4,256,128]{2,1,0:T(8,128)(2,1)S(1)}, bf16[512,512]{1,0:T(8,128)(2,1)S(1)}, f32[1,512]{1,0:T(1,128)S(1)},...) custom-call(bf16[4,256,512]{2,1,0:T(8,128)(2,1)S(1)} %bitcast.51, ...), custom_call_target="tpu_custom_call" | custom-call | tf_op jit(solution)/shard_map/hidden_grads/pallas_call | solution.py:1501
  154.3 8.0 %word_backward.1 = (bf16[1024,512]{1,0:T(8,128)(2,1)S(1)}, bf16[512,384]{1,0:T(8,128)(2,1)S(1)}) custom-call(bf16[2,1024,1024]{2,1,0:T(8,128)(2,1)S(1)} %get-tuple-element.136.probs_ref, bf16[1024,384]{1,0:T(8,128)(2,1)S(1)} %get-tuple-element.137.qkv_ref.all_ref, bf16[1024,384]{1,0:T(8,128)(2,1)S(1)} %get-tuple-element.137.qkv_ref.all_ref, ...), custom_call_target="tpu_custom_call" | custom-call | tf_op jit(solution)/shard_map/word_backward/pallas_call | solution.py:1282
  162.4 59.2 %stream_grads.1 = (bf16[4,256,512]{2,1,0:T(8,128)(2,1)S(1)}, f32[1,512]{1,0:T(1,128)S(1)}, bf16[8,96,512]{2,1,0:T(8,128)(2,1)S(1)}, bf16[512,512]{1,0:T(8,128)(2...) custom-call(bf16[4,256,512]{2,1,0:T(8,128)(2,1)S(1)} %bitcast.50, ...), custom_call_target="tpu_custom_call" | custom-call | tf_op jit(solution)/shard_map/stream_grads/pallas_call | solution.py:1501
  221.7 1.0 copy-done.33
  222.6 0.9 copy-done.34
  223.6 0.0 all-reduce.2.cloned.1.call-update
  223.6 28.1 %char_backward.1 = (bf16[20,512,256]{2,1,0:T(8,128)(2,1)}, bf16[256,1536]{1,0:T(8,128)(2,1)}, f32[1,256]{1,0:T(1,128)S(1)}, bf16[4,256,512]{2,1,0:T(8,128)(2,1)}) custom-call(s32[20]{0:T(128)S(1)} %copy-done.32, s32[20,32]{1,0:T(8,128)S(1)} %copy-done.35, bf16[20,512,256]{2,1,0:T(8,128)(2,1)} %bitcast.74, s32[20,32]{1,0:T(8,128)S(1)} %copy-done.35, ...), custom_call_target="tpu_custom_call" | custom-call | flops 18790481920 | bytes 62914560 | tf_op jit(solution)/shard_map/char_backward/pallas_call | solution.py:281
  251.8 1.1 copy-done.9
  252.9 34.9 %sum_char_grads.1 = (bf16[256,1536]{1,0:T(8,128)(2,1)S(1)}, f32[8,512]{1,0:T(8,128)S(1)}) custom-call(bf16[4,2,32,1536]{3,2,1,0:T(8,128)(2,1)S(1)} %bitcast.54, f32[1,256]{1,0:T(1,128)S(1)} %get-tuple-element.164.gain_char, f32[1,512]{1,0:T(1,128)S(1)} %get-tuple-element.165.gain_one, f32[1,512]{1,0:T(1,128)S(1)} %get-tuple-element.166.gain_two, ...), custom_call_target="tpu_custom_call" | custom-call | tf_op jit(solution)/shard_map/sum_char_grads/pallas_call | solution.py:967
  287.8 0.9 copy-done.7
  288.7 0.6 copy-done.26
  289.3 0.7 pad_add_fusion.position
  290.0 12.0 %shampoo.1 = (f32[1,1]{1,0:T(1,128)}, f32[1,256]{1,0:T(1,128)}, f32[2,512]{1,0:T(2,128)}, f32[1,256]{1,0:T(1,128)}, f32[2,512]{1,0:T(2,128)}, /*index=5*/bf16[10...) custom-call(s32[2]{0:T(128)} %pad_add_fusion.position, ...), custom_call_target="tpu_custom_call" | custom-call | tf_op jit(solution)/shard_map/shampoo/pallas_call | solution.py:1446
  (67 shorter events, 0.2 us)
Async XLA Ops:
  7.2 282.8 %all-reduce.2.cloned.1.call-start = ((), (), s32[]{:S(2)}) async-start(), calls=%async_computation | async-start | bytes 2097152 | tf_op jit(solution)/shard_map/psum | solution.py:2080
  24.5 61.2 %copy-start.6 = (bf16[1,1024,512]{2,1,0:T(8,128)(2,1)S(1)}, bf16[1,1024,512]{2,1,0:T(8,128)(2,1)}, u32[]{:S(2)}) copy-start(bf16[1,1024,512]{2,1,0:T(8,128)(2,1)} %param.39) | copy-start | bytes 3145732
  24.5 61.2 %copy-start.27 = (s32[1,1024]{1,0:T(1,128)S(1)}, s32[1,1024]{1,0:T(1,128)}, u32[]{:S(2)}) copy-start(s32[1,1024]{1,0:T(1,128)} %doc_row_ref.1) | copy-start | bytes 12292
  24.5 61.2 %copy-start.28 = (s32[16,128]{1,0:T(8,128)S(1)}, s32[16,128]{1,0:T(8,128)}, u32[]{:S(2)}) copy-start(s32[16,128]{1,0:T(8,128)} %get-tuple-element.134.place_ref) | copy-start | bytes 24580
  24.5 71.0 %copy-start.21 = (f32[4,32,256]{2,1,0:T(8,128)S(1)}, f32[4,32,256]{2,1,0:T(8,128)}, u32[]{:S(2)}) copy-start(f32[4,32,256]{2,1,0:T(8,128)} %refs_1_.5) | copy-start | bytes 393220
  24.6 71.0 %copy-start.22 = (f32[1,64,512]{2,1,0:T(8,128)S(1)}, f32[1,64,512]{2,1,0:T(8,128)}, u32[]{:S(2)}) copy-start(f32[1,64,512]{2,1,0:T(8,128)} %refs_2_.5) | copy-start | bytes 393220
  45.2 73.7 %copy-start.1 = (bf16[1,1024,512]{2,1,0:T(8,128)(2,1)S(1)}, bf16[1,1024,512]{2,1,0:T(8,128)(2,1)}, u32[]{:S(2)}) copy-start(bf16[1,1024,512]{2,1,0:T(8,128)(2,1)} %param.41) | copy-start | bytes 3145732
  85.7 39.7 %copy-start.18 = (f32[1,64,512]{2,1,0:T(8,128)S(1)}, f32[1,64,512]{2,1,0:T(8,128)}, u32[]{:S(2)}) copy-start(f32[1,64,512]{2,1,0:T(8,128)} %refs_1_.6) | copy-start | bytes 393220
  85.7 39.7 %copy-start.19 = (f32[1,64,512]{2,1,0:T(8,128)S(1)}, f32[1,64,512]{2,1,0:T(8,128)}, u32[]{:S(2)}) copy-start(f32[1,64,512]{2,1,0:T(8,128)} %refs_2_.6) | copy-start | bytes 393220
  85.7 39.7 %copy-start.20 = (f32[1,64,512]{2,1,0:T(8,128)S(1)}, f32[1,64,512]{2,1,0:T(8,128)}, u32[]{:S(2)}) copy-start(f32[1,64,512]{2,1,0:T(8,128)} %refs_3_.2) | copy-start | bytes 393220
  85.7 39.7 %copy-start.25 = (f32[3,1,16,128]{3,2,1,0:T(8,128)S(1)}, f32[3,1,16,128]{3,2,1,0:T(8,128)}, u32[]{:S(2)}) copy-start(f32[3,1,16,128]{3,2,1,0:T(8,128)} %param.62) | copy-start | bytes 73732
  125.4 36.9 %copy-start = (f32[1024,512]{1,0:T(8,128)}, f32[1024,512]{1,0:T(8,128)S(1)}, u32[]{:S(2)}) copy-start(f32[1024,512]{1,0:T(8,128)S(1)} %get-tuple-element.145.hidden_ref.hidden_in) | copy-start | bytes 6291460
  154.2 67.4 %copy-start.14 = (bf16[512,512]{1,0:T(8,128)(2,1)}, bf16[512,512]{1,0:T(8,128)(2,1)S(1)}, u32[]{:S(2)}) copy-start(bf16[512,512]{1,0:T(8,128)(2,1)S(1)} %get-tuple-element.177.refs_19_) | copy-start | bytes 1572868
  154.2 67.4 %copy-start.15 = (bf16[512,512]{1,0:T(8,128)(2,1)}, bf16[512,512]{1,0:T(8,128)(2,1)S(1)}, u32[]{:S(2)}) copy-start(bf16[512,512]{1,0:T(8,128)(2,1)S(1)} %get-tuple-element.178.refs_24_) | copy-start | bytes 1572868
  154.2 67.4 %copy-start.16 = (bf16[512,512]{1,0:T(8,128)(2,1)}, bf16[512,512]{1,0:T(8,128)(2,1)S(1)}, u32[]{:S(2)}) copy-start(bf16[512,512]{1,0:T(8,128)(2,1)S(1)} %get-tuple-element.179.refs_29_) | copy-start | bytes 1572868
  154.2 67.4 %copy-start.23 = (bf16[128,384]{1,0:T(8,128)(2,1)}, bf16[128,384]{1,0:T(8,128)(2,1)S(1)}, u32[]{:S(2)}) copy-start(bf16[128,384]{1,0:T(8,128)(2,1)S(1)} %get-tuple-element.176.refs_14_) | copy-start | bytes 294916
  162.3 61.3 %copy-start.31 = (f32[256]{0:T(256)S(1)}, f32[256]{0:T(256)}, u32[]{:S(2)}) copy-start(f32[256]{0:T(256)} %param.46) | copy-start | bytes 3076
  162.3 61.3 %copy-start.32 = (s32[20]{0:T(128)S(1)}, s32[20]{0:T(128)}, u32[]{:S(2)}) copy-start(s32[20]{0:T(128)} %home.3) | copy-start | bytes 244
  162.4 61.3 %copy-start.35 = (s32[20,32]{1,0:T(8,128)S(1)}, s32[20,32]{1,0:T(8,128)}, u32[]{:S(2)}) copy-start(s32[20,32]{1,0:T(8,128)} %counts_in.3) | copy-start | bytes 7684
  162.4 61.3 %copy-start.36 = (bf16[640,256]{1,0:T(8,128)(2,1)S(1)}, bf16[640,256]{1,0:T(8,128)(2,1)}, u32[]{:S(2)}) copy-start(bf16[640,256]{1,0:T(8,128)(2,1)} %get-tuple-element.160.pooled_ref) | copy-start | bytes 983044
  223.6 28.2 %copy-start.2 = (bf16[512,512]{1,0:T(8,128)(2,1)}, bf16[512,512]{1,0:T(8,128)(2,1)S(1)}, u32[]{:S(2)}) copy-start(bf16[512,512]{1,0:T(8,128)(2,1)S(1)} %get-tuple-element.169.refs_2_.upper) | copy-start | bytes 1572868
  223.6 28.2 %copy-start.3 = (bf16[512,512]{1,0:T(8,128)(2,1)}, bf16[512,512]{1,0:T(8,128)(2,1)S(1)}, u32[]{:S(2)}) copy-start(bf16[512,512]{1,0:T(8,128)(2,1)S(1)} %get-tuple-element.170.refs_3_.lower) | copy-start | bytes 1572868
  223.6 28.2 %copy-start.4 = (bf16[512,512]{1,0:T(8,128)(2,1)}, bf16[512,512]{1,0:T(8,128)(2,1)S(1)}, u32[]{:S(2)}) copy-start(bf16[512,512]{1,0:T(8,128)(2,1)S(1)} %get-tuple-element.168.refs_1_.output) | copy-start | bytes 1572868
  223.6 28.2 %copy-start.5 = (bf16[512,384]{1,0:T(8,128)(2,1)}, bf16[512,384]{1,0:T(8,128)(2,1)S(1)}, u32[]{:S(2)}) copy-start(bf16[512,384]{1,0:T(8,128)(2,1)S(1)} %get-tuple-element.167.refs_0_.project) | copy-start | bytes 1179652
  (14 other events, 119.1 us)
Sparse Core Ops, SparseCore 0:
  223.7 57.4 all-reduce.1

commit v3 on v2

--- a/solution.py
+++ b/solution.py
@@ -562,14 +562,22 @@
 MESH_ID = pl.DeviceIdType.MESH
 
 
-def greet(sizes, me):
+def greet_start(sizes, me):
     barrier = pltpu.get_barrier_semaphore()
     for axis, n in sizes.items():
         for d in range(1, n):
             pl.semaphore_signal(
                 barrier, inc=1, device_id={axis: lax.rem(me[axis] + d, n)}, device_id_type=MESH_ID
             )
-    pl.semaphore_wait(barrier, sum(n - 1 for n in sizes.values()))
+
+
+def greet_wait(sizes):
+    pl.semaphore_wait(pltpu.get_barrier_semaphore(), sum(n - 1 for n in sizes.values()))
+
+
+def greet(sizes, me):
+    greet_start(sizes, me)
+    greet_wait(sizes)
 
 
 def remote(source, target, sems, at, axis, peer):
@@ -1108,234 +1116,54 @@
 FEED_ROWS = 512
 
 
-def feed_kernel(
-    mixed_ref, output_ref, stream_ref, cot_ref, gain_ref, upper_ref, lower_ref,
-    hidden_ref, feed_ref, part_ref, grad_upper_ref, grad_lower_ref, upper_sum, lower_sum
-):
-    step = pl.program_id(0)
-
-    @pl.when(step == 0)
-    def _():
-        upper_sum[...] = jnp.zeros_like(upper_sum)
-        lower_sum[...] = jnp.zeros_like(lower_sum)
-
-    parts, _, width = mixed_ref.shape
-    hidden = stream_ref[...]
-    for j in range(parts):
-        hidden = hidden + nn(mixed_ref[j], output_ref[j * width : (j + 1) * width, :])
-    hidden_ref[...] = hidden
-    normed = (hidden * rms_scale(hidden) * gain_ref[...]).astype(BF)
-    raised = nn(normed, upper_ref[...])
+def feed_rows(mixed, output_ref, stream, grad_feed, gain, upper, lower):
+    hidden = stream
+    for j, part in enumerate(mixed):
+        width = part.shape[1]
+        hidden = hidden + nn(part, output_ref[j * width : (j + 1) * width, :])
+    normed = (hidden * rms_scale(hidden) * gain).astype(BF)
+    raised = nn(normed, upper)
     constant = math.sqrt(2.0 / math.pi)
     square = raised * raised
     curve = jnp.tanh(constant * raised * (1.0 + 0.044715 * square))
     half = 0.5 * (1.0 + curve)
     active = (raised * half).astype(BF)
     slope = half + 0.5 * raised * (1.0 - curve * curve) * constant * (1.0 + 3.0 * 0.044715 * square)
-    feed_ref[...] = nn(active, lower_ref[...]).astype(BF)
-    grad_feed = cot_ref[...]
-    grad_raised = (nt(grad_feed, lower_ref[...]) * slope).astype(BF)
-    part_ref[...] = nt(grad_raised, upper_ref[...]).astype(BF)
-    lower_sum[...] += tn(active, grad_feed)
-    upper_sum[...] += tn(normed, grad_raised)
-
-    @pl.when(step == pl.num_programs(0) - 1)
-    def _():
-        grad_upper_ref[...] = upper_sum[...].astype(BF)
-        grad_lower_ref[...] = lower_sum[...].astype(BF)
-
-
-def feed(mixed, output, stream, cotangent, gain, upper, lower):
-    length = stream.shape[0]
-    rows = pl.BlockSpec((FEED_ROWS, D), lambda i: (i, 0))
-    full = lambda shape: pl.BlockSpec(shape, lambda i: (0,) * len(shape))
-    return pl.pallas_call(
-        feed_kernel,
-        grid=(length // FEED_ROWS,),
-        in_specs=[
-            pl.BlockSpec((mixed.shape[0], FEED_ROWS, mixed.shape[2]), lambda i: (0, i, 0)),
-            full(output.shape),
-            rows,
-            rows,
-            full((1, D)),
-            full(upper.shape),
-            full(lower.shape),
-        ],
-        out_specs=[rows, rows, rows, full(upper.shape), full(lower.shape)],
-        out_shape=[
-            jax.ShapeDtypeStruct((length, D), F32),
-            jax.ShapeDtypeStruct((length, D), BF),
-            jax.ShapeDtypeStruct((length, D), BF),
-            jax.ShapeDtypeStruct(upper.shape, BF),
-            jax.ShapeDtypeStruct(lower.shape, BF),
-        ],
-        scratch_shapes=[pltpu.VMEM(upper.shape, F32), pltpu.VMEM(lower.shape, F32)],
-        compiler_params=pltpu.CompilerParams(vmem_limit_bytes=32 << 20),
-        name="feed",
-    )(mixed, output, stream, cotangent, gain.reshape(1, D), upper, lower)
-
-
-def hidden_back_kernel(
-    own, grad_ref, hidden_ref, cot_ref, mixed_ref, output_ref, gain_ref,
-    grad_hidden_ref, grad_mixed_ref, grad_output_ref, gain_grad_ref
-):
-    hidden = hidden_ref[...]
-    scale = rms_scale(hidden)
-    grad = grad_ref[...]
-    grad_hidden = cot_ref[...].astype(F32) + norm_back(hidden, scale, gain_ref[...], grad)
-    grad_hidden_ref[...] = grad_hidden
-    gain_grad_ref[...] = jnp.sum(hidden * scale * grad, axis=0, keepdims=True)
-    attend = grad_hidden.astype(BF)
-    parts, _, width = mixed_ref.shape
-    for j in range(parts):
-        at = slice(j * width, (j + 1) * width)
-        grad_mixed_ref[j] = nt(attend, output_ref[at, :]).astype(BF)
-        grad_output_ref[at, :] = tn(mixed_ref[j], attend).astype(BF)
-
-
-def hidden_back(own, grad, hidden, cotangent, mixed, output, gain):
-    share = grad.shape[0]
-    parts, _, width = mixed.shape
-    mine = pl.BlockSpec((share, D), lambda i, own: (own[0], 0))
-    full = lambda shape: pl.BlockSpec(shape, lambda i, own: (0,) * len(shape))
-    return pl.pallas_call(
-        hidden_back_kernel,
-        grid_spec=pltpu.PrefetchScalarGridSpec(
-            num_scalar_prefetch=1,
-            grid=(1,),
-            in_specs=[
-                full((share, D)),
-                mine,
-                mine,
-                pl.BlockSpec((parts, share, width), lambda i, own: (0, own[0], 0)),
-                full(output.shape),
-                full((1, D)),
-            ],
-            out_specs=[
-                full((share, D)),
-                full((parts, share, width)),
-                full(output.shape),
-                full((1, D)),
-            ],
-        ),
-        out_shape=[
-            jax.ShapeDtypeStruct((share, D), F32),
-            jax.ShapeDtypeStruct((parts, share, width), BF),
-            jax.ShapeDtypeStruct(output.shape, BF),
-            jax.ShapeDtypeStruct((1, D), F32),
-        ],
-        compiler_params=pltpu.CompilerParams(vmem_limit_bytes=32 << 20),
-        name="hidden_back",
-    )(own, grad, hidden, cotangent, mixed, output, gain.reshape(1, D))
-
-
-def word_backward_kernel(
-    width, probs_ref, qkv_ref, all_ref, grad_ref, normed_ref, project_ref,
-    part_ref, grad_project_ref, grads, key_sum, value_sum
-):
-    step = pl.program_id(0)
-    steps = all_ref.shape[0] // ROWS
-    first = pl.ds(pl.multiple_of(step * ROWS, ROWS), ROWS)
+    grad_raised = (nt(grad_feed, lower) * slope).astype(BF)
+    return (
+        hidden,
+        nn(active, lower).astype(BF),
+        nt(grad_raised, upper).astype(BF),
+        tn(normed, grad_raised),
+        tn(active, grad_feed),
+    )
+
+
+def attention_back(width, probs_ref, qkv_ref, grad_ref, grads, key_sum, value_sum):
     eighth = 1.0 / math.sqrt(HD)
-    queries = (qkv_ref[:, :width].astype(F32) * eighth).astype(BF)
-
-    @pl.when(step == 0)
-    def _():
-        key_sum[...] = jnp.zeros_like(key_sum)
-        value_sum[...] = jnp.zeros_like(value_sum)
-
-    def attend(number):
+    key_sum[...] = jnp.zeros_like(key_sum)
+    value_sum[...] = jnp.zeros_like(value_sum)
+    for number in range(qkv_ref.shape[0] // ROWS):
+        rows = slice(number * ROWS, (number + 1) * ROWS)
         count = (number + 1) * ROWS
+        queries = (qkv_ref[rows, :width].astype(F32) * eighth).astype(BF)
         parts = []
         for head in range(width // HD):
             at = slice(head * HD, (head + 1) * HD)
-            keys = all_ref[:count, width + head * HD : width + (head + 1) * HD]
-            values = all_ref[:count, 2 * width + head * HD : 2 * width + (head + 1) * HD]
-            grad = grad_ref[:, at]
-            probs = probs_ref[head, :count, :]
+            keys = qkv_ref[:count, width + head * HD : width + (head + 1) * HD]
+            values = qkv_ref[:count, 2 * width + head * HD : 2 * width + (head + 1) * HD]
+            grad = grad_ref[rows, at]
+            probs = probs_ref[head, :count, rows]
             wide = probs.astype(F32)
             product = wide * nt(values, grad)
             scores = (product - wide * jnp.sum(product, axis=0, keepdims=True)).astype(BF)
             key_sum[head, :count, :] += nn(scores, queries[:, at])
             value_sum[head, :count, :] += nn(probs, grad)
             parts.append(tn(keys, scores).T * eighth)
-        grads[first, :width] = jnp.concatenate(parts, axis=1).astype(BF)
-
-    for number in range(steps):
-        pl.when(step == number)(functools.partial(attend, number))
-
-    @pl.when(step == steps - 1)
-    def _():
-        for head in range(width // HD):
-            grads[:, width + head * HD : width + (head + 1) * HD] = key_sum[head].astype(BF)
-            grads[:, 2 * width + head * HD : 2 * width + (head + 1) * HD] = value_sum[head].astype(BF)
-        grad_project_ref[...] = tn(normed_ref[...], grads[...]).astype(BF)
-        part_ref[...] = nt(grads[...], project_ref[...]).astype(BF)
-
-
-def word_backward(probs, qkv, grad_mixed, normed, project):
-    length = qkv.shape[0]
-    width = project.shape[1] // 3
-    heads = width // HD
-    rows = lambda cols: pl.BlockSpec((ROWS, cols), lambda i: (i, 0))
-    full = lambda shape: pl.BlockSpec(shape, lambda i: (0,) * len(shape))
-    return pl.pallas_call(
-        functools.partial(word_backward_kernel, width),
-        grid=(length // ROWS,),
-        in_specs=[
-            pl.BlockSpec((heads, length, ROWS), lambda i: (0, 0, i)),
-            rows(3 * width),
-            full(qkv.shape),
-            rows(width),
-            full(normed.shape),
-            full(project.shape),
-        ],
-        out_specs=[full((length, D)), full(project.shape)],
-        out_shape=[
-            jax.ShapeDtypeStruct((length, D), BF),
-            jax.ShapeDtypeStruct(project.shape, BF),
-        ],
-        scratch_shapes=[
-            pltpu.VMEM(qkv.shape, BF),
-            pltpu.VMEM((heads, length, HD), F32),
-            pltpu.VMEM((heads, length, HD), F32),
-        ],
-        compiler_params=pltpu.CompilerParams(vmem_limit_bytes=32 << 20),
-        name="word_backward",
-    )(probs, qkv, qkv, grad_mixed, normed, project)
-
-
-def stream_back_kernel(own, grad_ref, stream_ref, hidden_grad_ref, gain_ref, out_ref, gain_grad_ref):
-    stream = stream_ref[...]
-    scale = rms_scale(stream)
-    grad = grad_ref[...]
-    total = hidden_grad_ref[...] + norm_back(stream, scale, gain_ref[...], grad)
-    out_ref[...] = total.astype(BF)
-    gain_grad_ref[...] = jnp.sum(stream * scale * grad, axis=0, keepdims=True)
-
-
-def stream_back(own, grad, stream, hidden_grad, gain):
-    share = grad.shape[0]
-    full = lambda shape: pl.BlockSpec(shape, lambda i, own: (0,) * len(shape))
-    return pl.pallas_call(
-        stream_back_kernel,
-        grid_spec=pltpu.PrefetchScalarGridSpec(
-            num_scalar_prefetch=1,
-            grid=(1,),
-            in_specs=[
-                full((share, D)),
-                pl.BlockSpec((share, D), lambda i, own: (own[0], 0)),
-                full((share, D)),
-                full((1, D)),
-            ],
-            out_specs=[full((share, D)), full((1, D))],
-        ),
-        out_shape=[
-            jax.ShapeDtypeStruct((share, D), BF),
-            jax.ShapeDtypeStruct((1, D), F32),
-        ],
-        name="stream_back",
-    )(own, grad, stream, hidden_grad, gain.reshape(1, D))
+        grads[rows, :width] = jnp.concatenate(parts, axis=1).astype(BF)
+    for head in range(width // HD):
+        grads[:, width + head * HD : width + (head + 1) * HD] = key_sum[head].astype(BF)
+        grads[:, 2 * width + head * HD : 2 * width + (head + 1) * HD] = value_sum[head].astype(BF)
 
 
 def shampoo_kernel(
@@ -1505,7 +1333,7 @@
         out_specs=[vmem] * len(outs),
         scratch_shapes=scratch,
         compiler_params=pltpu.CompilerParams(
-            collective_id=number, has_side_effects=True, vmem_limit_bytes=28 << 20
+            collective_id=number, has_side_effects=True, vmem_limit_bytes=36 << 20
         ),
         name=name,
     )(*inputs)
@@ -1700,22 +1528,47 @@
     )
 
 
-def hidden_grads(part_two, hidden, cotangent, mixed, output, gain, grad_upper, grad_lower, roots):
+def feed_step(mixed, stream, cotangent, output, gain, upper, lower, roots):
     n, m = lax.axis_size("dp"), lax.axis_size("mp")
-    share = part_two.shape[1]
-    width = mixed.shape[2]
+    length, width = mixed.shape
+    share = length // m
     made = [gather_shape([a], n) for a in roots]
-    parts = [by_chip(grad_upper), by_chip(grad_lower)]
-
-    def kernel(part, hidden_ref, cot, mix, out_mat, gain_ref, up, low, *refs):
+    chip_shape = lambda a: (n // 2, 2, a.shape[0] // n, a.shape[1])
+
+    def kernel(mixed_ref, stream_ref, cot, out_mat, gain_ref, upper_ref, lower_ref, *refs):
         roots_in, refs = refs[: len(roots)], refs[len(roots) :]
-        grad_hidden, grad_mixed, grad_output, gain_grad, up_sum, low_sum = refs[:6]
-        roots_out, refs = refs[6 : 6 + len(roots)], refs[6 + len(roots) :]
-        held, total, swapped, up_held, up_came, low_held, low_came, *sems = refs
-        pairs = [tuple(sems[2 * t : 2 * t + 2]) for t in range(5 + len(roots))]
+        hidden_ref, feed_ref, grad_hidden, grad_mixed, grad_output, gain_grad, up_sum, low_sum = refs[:8]
+        roots_out, refs = refs[8 : 8 + len(roots)], refs[8 + len(roots) :]
+        mix, part, up, low, held, total, swapped, up_held, up_came, low_held, low_came, *sems = refs
+        pairs = [tuple(sems[2 * t : 2 * t + 2]) for t in range(7 + len(roots))]
         i, j = lax.axis_index("dp"), lax.axis_index("mp")
         greet({"dp": n, "mp": m}, {"dp": i, "mp": j})
         stages = []
+        mix[j] = mixed_ref[...]
+        for h, cut in enumerate(halves(length)):
+            stages += line_gather_stages(
+                mix, pairs[5 + len(roots) + h], "mp", m, j, -50.0 + 0.05 * h, 6.0, cut
+            )
+
+        def run_feed():
+            grad_upper = jnp.zeros(upper_ref.shape, F32)
+            grad_lower = jnp.zeros(lower_ref.shape, F32)
+            for first in range(0, length, FEED_ROWS):
+                rows = slice(first, first + FEED_ROWS)
+                hidden, fed, part_rows, more_upper, more_lower = feed_rows(
+                    [mix[p, rows, :] for p in range(m)], out_mat, stream_ref[rows, :], cot[rows, :],
+                    gain_ref[...], upper_ref[...], lower_ref[...],
+                )
+                hidden_ref[rows, :] = hidden
+                feed_ref[rows, :] = fed
+                for p in range(FEED_ROWS // share):
+                    part[first // share + p] = part_rows[p * share : (p + 1) * share]
+                grad_upper = grad_upper + more_upper
+                grad_lower = grad_lower + more_lower
+            up[...] = grad_upper.astype(BF).reshape(up.shape)
+            low[...] = grad_lower.astype(BF).reshape(low.shape)
+
+        stages.append((-0.5, run_feed))
         for h, cut in enumerate(halves(share)):
             stages += line_part_stages(
                 part, held, total, pairs[(0, 4 + len(roots))[h]], "mp", m, j, 0.05 * h, 6.0, 70.0 + 0.1 * h, cut
@@ -1725,7 +1578,7 @@
         for t, (x, out) in enumerate(zip(roots_in, roots_out)):
             own_of, put = gather_setup([x], out)
             put(i)
-            stages += pair_gather_stages(own_of, pairs[4 + t], "dp", n, i, 2.0, 72.5)
+            stages += pair_gather_stages(own_of, pairs[4 + t], "dp", n, i, -49.8, 72.5)
 
         def back():
             mine = pl.ds(pl.multiple_of(j * share, share), share)
@@ -1752,52 +1605,69 @@
         )
         run_stages(stages)
 
-    block = lambda a: pltpu.VMEM(a.shape[:1] + a.shape[2:], BF)
+    chips = lambda a: pltpu.VMEM(chip_shape(a), BF)
+    block = lambda a: pltpu.VMEM(chip_shape(a)[:1] + chip_shape(a)[2:], BF)
     results = call_remote(
         kernel,
-        "hidden_grads",
+        "feed_step",
         4,
         [
+            jax.ShapeDtypeStruct((length, D), F32),
+            jax.ShapeDtypeStruct((length, D), BF),
             jax.ShapeDtypeStruct((share, D), F32),
             jax.ShapeDtypeStruct((m, share, width), BF),
             jax.ShapeDtypeStruct(output.shape, BF),
             jax.ShapeDtypeStruct((1, D), F32),
-            jax.ShapeDtypeStruct(parts[0].shape[2:], F32),
-            jax.ShapeDtypeStruct(parts[1].shape[2:], F32),
+            jax.ShapeDtypeStruct(chip_shape(upper)[2:], F32),
+            jax.ShapeDtypeStruct(chip_shape(lower)[2:], F32),
         ]
         + [shape for shape, _ in made],
         [
+            pltpu.VMEM((m, length, width), BF),
+            pltpu.VMEM((m, share, D), BF),
+            chips(upper),
+            chips(lower),
             pltpu.VMEM((2, m, share, D), BF),
             pltpu.VMEM((share, D), F32),
             pltpu.VMEM((m, share, width), BF),
-            block(parts[0]),
-            block(parts[0]),
-            block(parts[1]),
-            block(parts[1]),
+            block(upper),
+            block(upper),
+            block(lower),
+            block(lower),
         ]
-        + dma_sems(2 * max(n, m)) * (5 + len(roots)),
-        [part_two, hidden, cotangent, mixed, output, gain.reshape(1, D)] + parts + roots,
-    )
-    return list(results[:6]) + [shaper(a) for (_, shaper), a in zip(made, results[6:])]
-
-
-def stream_grads(part_one, stream, grad_hidden, gain, own_row, sums, grad_project, grad_output):
+        + dma_sems(2 * max(n, m)) * (7 + len(roots)),
+        [mixed, stream, cotangent, output, gain.reshape(1, D), upper, lower] + roots,
+    )
+    return list(results[:8]) + [shaper(a) for (_, shaper), a in zip(made, results[8:])]
+
+
+def stream_grads(probs, qkv, grad_mixed, normed, project_mat, stream, grad_hidden, gain, own_row, sums, grad_output):
     n, m = lax.axis_size("dp"), lax.axis_size("mp")
-    share = part_one.shape[1]
+    share = stream.shape[0] // m
+    width = project_mat.shape[1] // 3
+    heads = width // HD
     block = own_row.shape[2]
     total_words = n * block
     words = share * m
-    parts = [by_chip(grad_project), by_chip(grad_output)]
+    project_chips = (n // 2, 2, project_mat.shape[0] // n, project_mat.shape[1])
+    parts = [jax.ShapeDtypeStruct(project_chips, BF), by_chip(grad_output)]
     chunk = lambda a: jax.ShapeDtypeStruct((1,) + a.shape[-2:], F32)
     made = [gather_shape([chunk(a)], n) for a in (sums[0], sums[1], parts[0], parts[1])]
 
-    def kernel(part, stream_ref, hidden_ref, gain_ref, row_ref, up, low, project, output, *refs):
+    def kernel(
+        probs_ref, qkv_ref, mixed_grad, normed_ref, mat_ref, stream_ref, hidden_ref, gain_ref, row_ref, up, low, output, *refs
+    ):
         out, gain_grad, came, up_out, low_out, project_out, output_out = refs[:7]
-        (held, total, project_sum, output_sum, line_held, picked, hits,
+        (part, project, head_grads, key_sum, value_sum, held, total, project_sum, output_sum, line_held, picked, hits,
          p_held, p_came, o_held, o_came, *sems) = refs[7:]
         pairs = [tuple(sems[2 * t : 2 * t + 2]) for t in range(13)]
         i, j = lax.axis_index("dp"), lax.axis_index("mp")
-        greet({"dp": n, "mp": m}, {"dp": i, "mp": j})
+        greet_start({"dp": n, "mp": m}, {"dp": i, "mp": j})
+        attention_back(width, probs_ref, qkv_ref, mixed_grad, head_grads, key_sum, value_sum)
+        grads = head_grads[...]
+        part[...] = nt(grads, mat_ref[...]).astype(BF).reshape(part.shape)
+        project[...] = tn(normed_ref[...], grads).astype(BF).reshape(project.shape)
+        greet_wait({"dp": n, "mp": m})
         stages = []
         for h, cut in enumerate(halves(share)):
             stages += line_part_stages(
@@ -1934,6 +1804,11 @@
         ]
         + [shape for shape, _ in made],
         [
+            pltpu.VMEM((m, share, D), BF),
+            pltpu.VMEM(project_chips, BF),
+            pltpu.VMEM(qkv.shape, BF),
+            pltpu.VMEM((heads, words, HD), F32),
+            pltpu.VMEM((heads, words, HD), F32),
             pltpu.VMEM((2, m, share, D), BF),
             pltpu.VMEM((share, D), F32),
             pltpu.VMEM((1,) + parts[0].shape[2:], F32),
@@ -1948,15 +1823,19 @@
         ]
         + dma_sems(2 * max(n, m)) * 13,
         [
-            part_one,
+            probs,
+            qkv,
+            grad_mixed,
+            normed,
+            project_mat,
             stream,
             grad_hidden,
             gain.reshape(1, D),
             own_row,
             sums[0][None],
             sums[1][None],
-        ]
-        + parts,
+            parts[1],
+        ],
     )
     return list(results[:3]) + [shaper(a) for (_, shaper), a in zip(made, results[3:])]
 
@@ -2032,48 +1911,35 @@
         word_gains[0],
         project_mat,
     )
-    mixed_all, mixer_root, lift_root = exchange(
-        "gather_mixed",
-        3,
-        [
-            ("line_gather", "mp", [mixed]),
-            ("gather", "dp", [char_mixer_right_root]),
-            ("gather", "dp", [char_lift_right_root]),
-        ],
-    )
-    flat_cotangent = cotangent.reshape(words_dev, D)
-    hidden, feed_part, part_two, grad_upper, grad_lower = feed(
-        mixed_all, output_mat, stream, flat_cotangent, word_gains[1], upper_mat, lower_mat
-    )
-    shares = (part_count, words_dev // part_count, D)
-    grad_hidden, grad_mixed, grad_output_mat, gain_two, part_upper, part_lower, *word_roots = hidden_grads(
-        part_two.reshape(shares),
-        hidden,
-        flat_cotangent,
-        mixed_all,
+    hidden, feed_part, grad_hidden, grad_mixed, grad_output_mat, gain_two, part_upper, part_lower, *every_root = feed_step(
+        mixed,
+        stream,
+        cotangent.reshape(words_dev, D),
         output_mat,
         word_gains[1],
-        grad_upper,
-        grad_lower,
+        upper_mat,
+        lower_mat,
         [
+            char_mixer_right_root,
+            char_lift_right_root,
             word_project_right_root.reshape((3,) + word_project_right_root.shape[2:]),
             word_output_right_root,
             feed_upper_right_root,
             feed_lower_right_root,
         ],
     )
-    project_root, output_root, upper_root, lower_root = word_roots
-    part_one, grad_project = word_backward(
-        probs, qkv, grad_mixed.reshape(words_dev, -1), normed_one, project_mat
-    )
+    mixer_root, lift_root, project_root, output_root, upper_root, lower_root = every_root
     grad_words, gain_one, grad_vectors, sum_upper, sum_lower, sum_project, sum_output = stream_grads(
-        part_one.reshape(shares),
+        probs,
+        qkv,
+        grad_mixed.reshape(words_dev, -1),
+        normed_one,
+        project_mat,
         stream,
         grad_hidden,
         word_gains[0],
         own_row,
         (part_upper, part_lower),
-        grad_project,
         grad_output_mat,
     )
     grad_vectors, feed_part = lax.optimization_barrier((grad_vectors, feed_part))

time: 313 us -> 312 us (level)
  Pallas kernels: 285 us -> 280 us
    pallas_call x3 -> x0, Pallas kernels: 36.2 us -> none  [the longest x1 21.7 us: exchange(): pl.pallas_call(kernel, out_shape=outs, in_specs=[vmem] * total_ins, out_s...]
    pallas_call x3, Pallas kernels: 127 us -> 160 us  [call_remote(): pl.pallas_call(kernel, out_shape=outs, in_specs=[vmem] * len(inputs), out...]
    pallas_call x2, Pallas kernels: 48.7 us -> 39.6 us  [char_call(): pl.pallas_call(kernel, in_specs=[smem] * len(scalars) + [hbm if t in in_h...]
    pallas_call x1, Pallas kernels: 34.9 us -> 42 us  [sum_char_grads(): pl.pallas_call(kernel, out_shape=[jax.ShapeDtypeStruct((n * rows, cols) i...]
  transfers between devices with their start and end apart: 1 -> 1, of which waited for: 0 -> 0; matrix products, arithmetic and copies ran while one was open for 0% -> 0% of each run, Pallas kernels for 20% -> 21%
where the time goes in v3:
time: 312 us; the launch traced here: 307 us
  Pallas kernels  280 us (90%)
  between operations  14.8 us (5%)
  local copies, waits for them, and re-layouts  11 us (4%)
    pallas_call x3, Pallas kernels, call_remote(): pl.pallas_call(kernel, out_shape=outs, in_specs=[vmem] * len(inputs), out...  160 us
    pallas_call x1, Pallas kernels, sum_char_grads(): pl.pallas_call(kernel, out_shape=[jax.ShapeDtypeStruct((n * rows, cols) i...  42 us
    pallas_call x2, Pallas kernels, char_call(): pl.pallas_call(kernel, in_specs=[smem] * len(scalars) + [hbm if t in in_h...  39.6 us
    pallas_call x1, Pallas kernels, gather_char(): pl.pallas_call(kernel, out_shape=[shape, jax.ShapeDtypeStruct((m, rows, D...  16.4 us
    pallas_call x1, Pallas kernels, shampoo(): pl.pallas_call(functools.partial(shampoo_kernel, threshold), in_specs=[sm...  12 us
    unnamed x74, local copies, waits for them, and re-layouts  10.2 us
    pallas_call x1, Pallas kernels, word_forward(): pl.pallas_call(functools.partial(word_forward_kernel, width), grid=(lengt...  10 us
  transfers between devices with their start and end apart: 1, of which 0 were waited for; matrix products, arithmetic and copies ran while one was open for 0% of the time, Pallas kernels for 21%

profile of v3, /device:TPU:0, one launch (start us, length us, event | category | flops | bytes accessed | tf_op | source)
XLA Modules:
  0.0 306.7 jit_solution(4375275963251136936)
XLA Ops:
  7.2 0.0 all-reduce.2.cloned.1.call-start
  7.3 0.8 fusion
  8.0 16.4 %gather_char.1 = (bf16[256,1536]{1,0:T(8,128)(2,1)}, bf16[4,16,512]{2,1,0:T(8,128)(2,1)}, bf16[24,128]{1,0:T(8,128)(2,1)}, s32[16,128]{1,0:T(8,128)}, s32[8,1,96]{2,1,0:T(1,128)}) custom-call(f32[4,32,256]{2,1,0:T(8,128)} %refs_0_.3, f32[1,32,512]{2,1,0:T(8,128)} %refs_5_.3, f32[1,16,512]{2,1,0:T(8,128)} %refs_15_.1, s32[1,20]{1,0:T(1,128)} %bitcast.56, ...), custom_call_target="tpu_custom_call" | custom-call | tf_op jit(solution)/shard_map/gather_char/pallas_call | solution.py:1426
  24.6 16.6 %char_forward.1 = (bf16[24,32,512]{2,1,0:T(8,128)(2,1)}, bf16[20,512,1536]{2,1,0:T(8,128)(2,1)}, bf16[640,256]{1,0:T(8,128)(2,1)}, f32[640,256]{1,0:T(8,128)}) custom-call(s32[20]{0:T(128)} %home.3, s32[20,32]{1,0:T(8,128)} %counts_in.3, bf16[20,512,256]{2,1,0:T(8,128)(2,1)} %bitcast.61, s32[20,32]{1,0:T(8,128)} %counts_in.3, f32[1,256]{1,0:T(1,128)} %bitcast.53, ...), custom_call_target="tpu_custom_call" | custom-call | flops 10737418240 | bytes 62914560 | tf_op jit(solution)/shard_map/char_forward/pallas_call | solution.py:281
  41.3 1.2 copy-done.8
  42.5 44.5 %send_vectors.1 = (bf16[4,320,512]{2,1,0:T(8,128)(2,1)S(1)}, bf16[512,384]{1,0:T(8,128)(2,1)S(1)}, bf16[512,512]{1,0:T(8,128)(2,1)S(1)}, bf16[512,512]{1,0:T(8,128)(2,1)S(1)}, bf16[4,128,512]{2,1,0:T(8,128)(2,1)S(1)}) custom-call(bf16[8,96,512]{2,1,0:T(8,128)(2,1)S(1)} %bitcast.43, bf16[24,128]{1,0:T(8,128)(2,1)S(1)} %copy-done.29, ...), custom_call_target="tpu_custom_call" | custom-call | tf_op jit(solution)/shard_map/send_vectors/pallas_call | solution.py:1329
  87.0 10.0 %word_forward.1 = (f32[1024,512]{1,0:T(8,128)S(1)}, bf16[1024,512]{1,0:T(8,128)(2,1)S(1)}, bf16[1024,384]{1,0:T(8,128)(2,1)S(1)}, bf16[2,1024,1024]{2,1,0:T(8,128)(2,1)S(1)}, bf16[1024,128]{1,0:T(8,128)(2,1)S(1)}) custom-call(bf16[4,320,512]{2,1,0:T(8,128)(2,1)S(1)} %get-tuple-element.127.vec_ref, s32[16,128]{1,0:T(8,128)S(1)} %copy-done.28, ...), custom_call_target="tpu_custom_call" | custom-call | tf_op jit(solution)/shard_map/word_forward/pallas_call | solution.py:1071
  97.1 54.8 %feed_step.1 = (f32[1024,512]{1,0:T(8,128)S(1)}, bf16[1024,512]{1,0:T(8,128)(2,1)}, f32[256,512]{1,0:T(8,128)S(1)}, bf16[4,256,128]{2,1,0:T(8,128)(2,1)S(1)}, bf...) custom-call(bf16[1024,128]{1,0:T(8,128)(2,1)S(1)} %get-tuple-element, ...), custom_call_target="tpu_custom_call" | custom-call | tf_op jit(solution)/shard_map/feed_step/pallas_call | solution.py:1329
  152.0 1.3 copy-done
  153.3 0.8 copy-done.12
  154.1 0.8 copy-done.13
  154.9 0.8 copy-done.14
  155.7 0.6 copy-done.23
  156.4 61.0 %stream_grads.1 = (bf16[4,256,512]{2,1,0:T(8,128)(2,1)S(1)}, f32[1,512]{1,0:T(1,128)S(1)}, bf16[8,96,512]{2,1,0:T(8,128)(2,1)S(1)}, bf16[512,512]{1,0:T(8,128)(2...) custom-call(bf16[2,1024,1024]{2,1,0:T(8,128)(2,1)S(1)} %get-tuple-element.130.prob, ...), custom_call_target="tpu_custom_call" | custom-call | tf_op jit(solution)/shard_map/stream_grads/pallas_call | solution.py:1329
  217.4 1.0 copy-done.33
  218.4 0.9 copy-done.34
  219.3 0.0 all-reduce.2.cloned.1.call-update
  219.4 23.0 %char_backward.1 = (bf16[20,512,256]{2,1,0:T(8,128)(2,1)}, bf16[256,1536]{1,0:T(8,128)(2,1)}, f32[1,256]{1,0:T(1,128)S(1)}, bf16[4,256,512]{2,1,0:T(8,128)(2,1)}) custom-call(s32[20]{0:T(128)S(1)} %copy-done.32, s32[20,32]{1,0:T(8,128)S(1)} %copy-done.35, bf16[20,512,256]{2,1,0:T(8,128)(2,1)} %bitcast.62, s32[20,32]{1,0:T(8,128)S(1)} %copy-done.35, ...), custom_call_target="tpu_custom_call" | custom-call | flops 18790481920 | bytes 62914560 | tf_op jit(solution)/shard_map/char_backward/pallas_call | solution.py:281
  242.4 1.1 copy-done.9
  243.6 42.0 %sum_char_grads.1 = (bf16[256,1536]{1,0:T(8,128)(2,1)S(1)}, f32[8,512]{1,0:T(8,128)S(1)}) custom-call(bf16[4,2,32,1536]{3,2,1,0:T(8,128)(2,1)S(1)} %bitcast.44, f32[1,256]{1,0:T(1,128)S(1)} %get-tuple-element.151.gain_char, f32[1,512]{1,0:T(1,128)S(1)} %get-tuple-element.152.gain_one, f32[1,512]{1,0:T(1,128)S(1)} %get-tuple-element.153.gain_two, ...), custom_call_target="tpu_custom_call" | custom-call | tf_op jit(solution)/shard_map/sum_char_grads/pallas_call | solution.py:975
  285.6 0.9 copy-done.7
  286.5 0.6 copy-done.26
  287.1 0.6 pad_add_fusion.position
  287.6 12.0 %shampoo.1 = (f32[1,1]{1,0:T(1,128)}, f32[1,256]{1,0:T(1,128)}, f32[2,512]{1,0:T(2,128)}, f32[1,256]{1,0:T(1,128)}, f32[2,512]{1,0:T(2,128)}, /*index=5*/bf16[10...) custom-call(s32[2]{0:T(128)} %pad_add_fusion.position, ...), custom_call_target="tpu_custom_call" | custom-call | tf_op jit(solution)/shard_map/shampoo/pallas_call | solution.py:1274
  (64 shorter events, 0.2 us)
Async XLA Ops:
  7.2 280.4 %all-reduce.2.cloned.1.call-start = ((), (), s32[]{:S(2)}) async-start(), calls=%async_computation | async-start | bytes 2097152 | tf_op jit(solution)/shard_map/psum | solution.py:1946
  24.5 16.8 %copy-start.10 = (f32[1,64,512]{2,1,0:T(8,128)S(1)}, f32[1,64,512]{2,1,0:T(8,128)}, u32[]{:S(2)}) copy-start(f32[1,64,512]{2,1,0:T(8,128)} %refs_20_.1) | copy-start | bytes 393220
  24.5 16.8 %copy-start.11 = (f32[1,64,512]{2,1,0:T(8,128)S(1)}, f32[1,64,512]{2,1,0:T(8,128)}, u32[]{:S(2)}) copy-start(f32[1,64,512]{2,1,0:T(8,128)} %refs_25_.1) | copy-start | bytes 393220
  24.5 62.5 %copy-start.6 = (bf16[1,1024,512]{2,1,0:T(8,128)(2,1)S(1)}, bf16[1,1024,512]{2,1,0:T(8,128)(2,1)}, u32[]{:S(2)}) copy-start(bf16[1,1024,512]{2,1,0:T(8,128)(2,1)} %param.39) | copy-start | bytes 3145732
  24.5 62.4 %copy-start.27 = (s32[1,1024]{1,0:T(1,128)S(1)}, s32[1,1024]{1,0:T(1,128)}, u32[]{:S(2)}) copy-start(s32[1,1024]{1,0:T(1,128)} %doc_row_ref.1) | copy-start | bytes 12292
  24.6 62.4 %copy-start.28 = (s32[16,128]{1,0:T(8,128)S(1)}, s32[16,128]{1,0:T(8,128)}, u32[]{:S(2)}) copy-start(s32[16,128]{1,0:T(8,128)} %get-tuple-element.128.place_ref) | copy-start | bytes 24580
  24.6 72.5 %copy-start.18 = (f32[4,32,256]{2,1,0:T(8,128)S(1)}, f32[4,32,256]{2,1,0:T(8,128)}, u32[]{:S(2)}) copy-start(f32[4,32,256]{2,1,0:T(8,128)} %refs_0_.2) | copy-start | bytes 393220
  24.6 72.5 %copy-start.19 = (f32[1,64,512]{2,1,0:T(8,128)S(1)}, f32[1,64,512]{2,1,0:T(8,128)}, u32[]{:S(2)}) copy-start(f32[1,64,512]{2,1,0:T(8,128)} %refs_1_.4) | copy-start | bytes 393220
  24.6 72.5 %copy-start.20 = (f32[1,64,512]{2,1,0:T(8,128)S(1)}, f32[1,64,512]{2,1,0:T(8,128)}, u32[]{:S(2)}) copy-start(f32[1,64,512]{2,1,0:T(8,128)} %refs_3_.2) | copy-start | bytes 393220
  24.6 72.5 %copy-start.21 = (f32[1,64,512]{2,1,0:T(8,128)S(1)}, f32[1,64,512]{2,1,0:T(8,128)}, u32[]{:S(2)}) copy-start(f32[1,64,512]{2,1,0:T(8,128)} %refs_4_.1) | copy-start | bytes 393220
  24.6 72.5 %copy-start.22 = (f32[1,64,512]{2,1,0:T(8,128)S(1)}, f32[1,64,512]{2,1,0:T(8,128)}, u32[]{:S(2)}) copy-start(f32[1,64,512]{2,1,0:T(8,128)} %refs_5_.2) | copy-start | bytes 393220
  24.6 72.5 %copy-start.25 = (f32[3,1,16,128]{3,2,1,0:T(8,128)S(1)}, f32[3,1,16,128]{3,2,1,0:T(8,128)}, u32[]{:S(2)}) copy-start(f32[3,1,16,128]{3,2,1,0:T(8,128)} %param.62) | copy-start | bytes 73732
  41.2 55.9 %copy-start.5 = (bf16[1,1024,512]{2,1,0:T(8,128)(2,1)S(1)}, bf16[1,1024,512]{2,1,0:T(8,128)(2,1)}, u32[]{:S(2)}) copy-start(bf16[1,1024,512]{2,1,0:T(8,128)(2,1)} %param.41) | copy-start | bytes 3145732
  87.0 69.3 %copy-start.30 = (s32[8,1,96]{2,1,0:T(1,128)S(1)}, s32[8,1,96]{2,1,0:T(1,128)}, u32[]{:S(2)}) copy-start(s32[8,1,96]{2,1,0:T(1,128)} %get-tuple-element.140.row_ref) | copy-start | bytes 9220
  156.3 61.1 %copy-start.15 = (bf16[512,512]{1,0:T(8,128)(2,1)}, bf16[512,512]{1,0:T(8,128)(2,1)S(1)}, u32[]{:S(2)}) copy-start(bf16[512,512]{1,0:T(8,128)(2,1)S(1)} %get-tuple-element.166.refs_24_) | copy-start | bytes 1572868
  156.3 61.1 %copy-start.16 = (bf16[512,512]{1,0:T(8,128)(2,1)}, bf16[512,512]{1,0:T(8,128)(2,1)S(1)}, u32[]{:S(2)}) copy-start(bf16[512,512]{1,0:T(8,128)(2,1)S(1)} %get-tuple-element.167.refs_29_) | copy-start | bytes 1572868
  156.3 63.0 %copy-start.31 = (f32[256]{0:T(256)S(1)}, f32[256]{0:T(256)}, u32[]{:S(2)}) copy-start(f32[256]{0:T(256)} %param.46) | copy-start | bytes 3076
  156.3 63.0 %copy-start.32 = (s32[20]{0:T(128)S(1)}, s32[20]{0:T(128)}, u32[]{:S(2)}) copy-start(s32[20]{0:T(128)} %home.3) | copy-start | bytes 244
  156.3 63.0 %copy-start.35 = (s32[20,32]{1,0:T(8,128)S(1)}, s32[20,32]{1,0:T(8,128)}, u32[]{:S(2)}) copy-start(s32[20,32]{1,0:T(8,128)} %counts_in.3) | copy-start | bytes 7684
  156.4 63.0 %copy-start.36 = (bf16[640,256]{1,0:T(8,128)(2,1)S(1)}, bf16[640,256]{1,0:T(8,128)(2,1)}, u32[]{:S(2)}) copy-start(bf16[640,256]{1,0:T(8,128)(2,1)} %get-tuple-element.147.pooled_ref) | copy-start | bytes 983044
  219.3 23.1 %copy-start.1 = (bf16[512,512]{1,0:T(8,128)(2,1)}, bf16[512,512]{1,0:T(8,128)(2,1)S(1)}, u32[]{:S(2)}) copy-start(bf16[512,512]{1,0:T(8,128)(2,1)S(1)} %get-tuple-element.156.refs_2_.upper) | copy-start | bytes 1572868
  219.3 23.1 %copy-start.2 = (bf16[512,512]{1,0:T(8,128)(2,1)}, bf16[512,512]{1,0:T(8,128)(2,1)S(1)}, u32[]{:S(2)}) copy-start(bf16[512,512]{1,0:T(8,128)(2,1)S(1)} %get-tuple-element.157.refs_3_.lower) | copy-start | bytes 1572868
  219.3 23.1 %copy-start.3 = (bf16[512,512]{1,0:T(8,128)(2,1)}, bf16[512,512]{1,0:T(8,128)(2,1)S(1)}, u32[]{:S(2)}) copy-start(bf16[512,512]{1,0:T(8,128)(2,1)S(1)} %get-tuple-element.155.refs_1_.output) | copy-start | bytes 1572868
  219.3 23.1 %copy-start.4 = (bf16[512,384]{1,0:T(8,128)(2,1)}, bf16[512,384]{1,0:T(8,128)(2,1)S(1)}, u32[]{:S(2)}) copy-start(bf16[512,384]{1,0:T(8,128)(2,1)S(1)} %get-tuple-element.154.refs_0_.project) | copy-start | bytes 1179652
  (14 other events, 60.4 us)
Sparse Core Ops, SparseCore 0:
  219.4 56.5 all-reduce.1

commit v4 on v3

--- a/solution.py
+++ b/solution.py
@@ -896,23 +896,33 @@
     return array.reshape(lax.axis_size("dp") // 2, 2, -1, array.shape[-1])
 
 
-def sum_char_grads(grads, gains, word_sums, block_rows):
+def sum_char_grads(grads, gains, word_sums, block_rows, block_own):
     n, m = lax.axis_size("dp"), lax.axis_size("mp")
     grads = by_chip(grads)
     rows, cols = grads.shape[2:]
     slim = cols // m
     small = jax.ShapeDtypeStruct((8, D), F32)
 
-    def kernel(x, gain_char, gain_one, gain_two, *refs):
+    share = block_own.shape[0]
+
+    def kernel(x, gain_char, gain_one, gain_two, own_ref, *refs):
         words = refs[: len(word_sums)]
-        (out, small_out, held, came, total_dp, cut, cut_held, merged, small_dp, small_mp, *sems) = refs[len(word_sums) :]
-        pairs = [tuple(sems[2 * t : 2 * t + 2]) for t in range(6)]
+        (out, small_out, block_out, held, came, total_dp, cut, cut_held, merged, small_dp, small_mp, *sems) = refs[len(word_sums) :]
+        pairs = [tuple(sems[2 * t : 2 * t + 2]) for t in range(8)]
         i, j = lax.axis_index("dp"), lax.axis_index("mp")
-        greet({"dp": n, "mp": m}, {"dp": i, "mp": j})
+        greet_start({"dp": n, "mp": m}, {"dp": i, "mp": j})
+        block_out[j] = own_ref[...]
+        greet_wait({"dp": n, "mp": m})
+        line = []
+        for h, span in enumerate(halves(share)):
+            line += line_gather_stages(block_out, pairs[6 + h], "mp", m, j, 0.05 * h, 1.0, span)
+        line = [run for _, run in sorted(line, key=lambda stage: stage[0])]
         part = [
             run for _, run in pair_part_stages(x, held, came, total_dp, pairs[0], "dp", n, i, 0.0, 0.0)
         ]
         part[0]()
+        line.pop(0)()
+        line.pop(0)()
         squares = jnp.zeros((1, 1), F32)
         for t, word in enumerate(words):
             if t == 1:
@@ -951,6 +961,8 @@
         four = direct_stages(lambda p: merged.at[j], merged, pairs[4], "mp", m, j, 0, lambda: None, 0)
         one[0][1]()
         part[2]()
+        line.pop(0)()
+        line.pop(0)()
         for p in range(m):
             cut[p] = total_dp[:, p * slim : (p + 1) * slim]
         cut_held[j] = cut[j]
@@ -961,6 +973,8 @@
         four[0][1]()
         two[1][1]()
         four[1][1]()
+        line.pop(0)()
+        line.pop(0)()
         if rows % 16 == 0:
             own_of = lambda d: out.at[pl.ds(pl.multiple_of(d * rows, 16), rows), :]
         else:
@@ -970,16 +984,19 @@
             own[:, p * slim : (p + 1) * slim] = merged[p]
         for _, run in pair_gather_stages(own_of, pairs[5], "dp", n, i, 0, 0):
             run()
+        for run in line:
+            run()
 
     vmem = pl.BlockSpec(memory_space=pltpu.VMEM)
-    sums, smalls = pl.pallas_call(
+    sums, smalls, block = pl.pallas_call(
         kernel,
         out_shape=[
             jax.ShapeDtypeStruct((n * rows, cols) if rows % 16 == 0 else (n, rows, cols), BF),
             jax.ShapeDtypeStruct(small.shape, F32),
+            jax.ShapeDtypeStruct((m,) + block_own.shape, BF),
         ],
-        in_specs=[vmem] * (4 + len(word_sums)),
-        out_specs=[vmem] * 2,
+        in_specs=[vmem] * (5 + len(word_sums)),
+        out_specs=[vmem] * 3,
         scratch_shapes=[
             pltpu.VMEM((n // 2, rows, cols), BF),
             pltpu.VMEM((n // 2, rows, cols), BF),
@@ -990,13 +1007,13 @@
             pltpu.VMEM((n,) + small.shape, F32),
             pltpu.VMEM((m,) + small.shape, F32),
         ]
-        + [pltpu.SemaphoreType.DMA((2 * max(n, m),))] * 12,
+        + [pltpu.SemaphoreType.DMA((2 * max(n, m),))] * 16,
         compiler_params=pltpu.CompilerParams(
             collective_id=20, has_side_effects=True, vmem_limit_bytes=24 << 20
         ),
         name="sum_char_grads",
-    )(grads, *gains, *word_sums)
-    return sums.reshape(n * rows, cols), smalls
+    )(grads, *gains, block_own, *word_sums)
+    return sums.reshape(n * rows, cols), smalls, block
 
 
 ROWS = 256
@@ -1167,26 +1184,21 @@
 
 
 def shampoo_kernel(
-    threshold, position, char_ref, small_ref, gain_ref, gains_ref, project, output, upper, lower, hidden_in, feed_in, *refs
+    threshold, position, char_ref, small_ref, gain_ref, gains_ref, project, output, upper, lower, block_in, *refs
 ):
     given_in, refs = refs[:30], refs[30:]
     norm_ref, gain_grad_ref, gains_grad_ref, gain_new_ref, gains_new_ref, block_out = refs[:6]
     made_out, refs = refs[6:36], refs[36:]
     given, made = refs[:30], refs[30:60]
-    hidden, feed_sum, total, in_sems, out_sems = refs[60:]
+    in_sems, out_sems = refs[60:]
     loads = [pltpu.make_async_copy(a, b, in_sems.at[t]) for t, (a, b) in enumerate(zip(given_in, given))]
-    loads += [
-        pltpu.make_async_copy(hidden_in, hidden, in_sems.at[30]),
-        pltpu.make_async_copy(feed_in, feed_sum, in_sems.at[31]),
-    ]
     order = (4, 5, 2, 3, 0, 1)
     for number in order:
         for t in range(5):
             loads[5 * number + t].start()
-    loads[30].start()
-    loads[31].start()
     saves = [pltpu.make_async_copy(a, b, out_sems.at[t]) for t, (a, b) in enumerate(zip(made, made_out))]
-    saves.append(pltpu.make_async_copy(total, block_out, out_sems.at[30]))
+    saves.append(pltpu.make_async_copy(block_in, block_out, out_sems.at[30]))
+    saves[30].start()
     me = position[0]
     char = char_ref[...].astype(F32)
     small = small_ref[...]
@@ -1245,15 +1257,11 @@
             copy_out[t] = new.astype(BF)
         for t in range(5):
             saves[5 * number + t].start()
-    loads[30].wait()
-    loads[31].wait()
-    total[...] = (hidden[...] + feed_sum[...].astype(F32)).astype(BF)
-    saves[30].start()
     for save in saves:
         save.wait()
 
 
-def shampoo(threshold, position, char_sums, small, gain, gains, word_sums, hidden, feed_sum, given):
+def shampoo(threshold, position, char_sums, small, gain, gains, word_sums, block_out, given):
     flat = []
     shapes = []
     for master, left, right, left_root, right_root in given:
@@ -1273,21 +1281,18 @@
     hbm = pl.BlockSpec(memory_space=pltpu.HBM)
     return pl.pallas_call(
         functools.partial(shampoo_kernel, threshold),
-        in_specs=[smem] + [vmem] * 8 + [hbm] * 32,
+        in_specs=[smem] + [vmem] * 9 + [hbm] * 30,
         out_specs=[vmem] * 5 + [hbm] * 31,
-        out_shape=first + [jax.ShapeDtypeStruct(feed_sum.shape, BF)] + shapes,
+        out_shape=first + [jax.ShapeDtypeStruct(block_out.shape, BF)] + shapes,
         scratch_shapes=[pltpu.VMEM(a.shape, a.dtype) for a in flat]
         + [pltpu.VMEM(a.shape, a.dtype) for a in shapes]
         + [
-            pltpu.VMEM(hidden.shape, F32),
-            pltpu.VMEM(feed_sum.shape, BF),
-            pltpu.VMEM(feed_sum.shape, BF),
-            pltpu.SemaphoreType.DMA((32,)),
+            pltpu.SemaphoreType.DMA((30,)),
             pltpu.SemaphoreType.DMA((31,)),
         ],
         compiler_params=pltpu.CompilerParams(vmem_limit_bytes=60 << 20),
         name="shampoo",
-    )(position, char_sums, small, gain.reshape(1, CW), gains, *word_sums, hidden, feed_sum, *flat)
+    )(position, char_sums, small, gain.reshape(1, CW), gains, *word_sums, block_out, *flat)
 
 
 def run_stages(stages):
@@ -1641,7 +1646,7 @@
     return list(results[:8]) + [shaper(a) for (_, shaper), a in zip(made, results[8:])]
 
 
-def stream_grads(probs, qkv, grad_mixed, normed, project_mat, stream, grad_hidden, gain, own_row, sums, grad_output):
+def stream_grads(probs, qkv, grad_mixed, normed, project_mat, stream, grad_hidden, gain, own_row, sums, grad_output, fed, hidden):
     n, m = lax.axis_size("dp"), lax.axis_size("mp")
     share = stream.shape[0] // m
     width = project_mat.shape[1] // 3
@@ -1655,12 +1660,12 @@
     made = [gather_shape([chunk(a)], n) for a in (sums[0], sums[1], parts[0], parts[1])]
 
     def kernel(
-        probs_ref, qkv_ref, mixed_grad, normed_ref, mat_ref, stream_ref, hidden_ref, gain_ref, row_ref, up, low, output, *refs
+        probs_ref, qkv_ref, mixed_grad, normed_ref, mat_ref, stream_ref, hidden_ref, gain_ref, row_ref, up, low, output, fed_ref, hidden_in, *refs
     ):
-        out, gain_grad, came, up_out, low_out, project_out, output_out = refs[:7]
+        out, gain_grad, came, block_own, up_out, low_out, project_out, output_out = refs[:8]
         (part, project, head_grads, key_sum, value_sum, held, total, project_sum, output_sum, line_held, picked, hits,
-         p_held, p_came, o_held, o_came, *sems) = refs[7:]
-        pairs = [tuple(sems[2 * t : 2 * t + 2]) for t in range(13)]
+         p_held, p_came, o_held, o_came, fed_held, fed_sum, *sems) = refs[8:]
+        pairs = [tuple(sems[2 * t : 2 * t + 2]) for t in range(15)]
         i, j = lax.axis_index("dp"), lax.axis_index("mp")
         greet_start({"dp": n, "mp": m}, {"dp": i, "mp": j})
         attention_back(width, probs_ref, qkv_ref, mixed_grad, head_grads, key_sum, value_sum)
@@ -1790,6 +1795,16 @@
                     ).wait()
 
         stages.append((82.0, place))
+        for h, cut in enumerate(halves(share)):
+            stages += line_part_stages(
+                fed_ref, fed_held, fed_sum, pairs[13 + h], "mp", m, j, 73.5 + 0.005 * h, 0.1, 90.0 + h, cut
+            )
+
+        def add_hidden():
+            mine = pl.ds(pl.multiple_of(j * share, share), share)
+            block_own[...] = (hidden_in[mine, :] + fed_sum[...]).astype(BF)
+
+        stages.append((92.0, add_hidden))
         run_stages(stages)
 
     held_of = lambda a: pltpu.VMEM(a.shape[:1] + a.shape[2:], BF)
@@ -1801,6 +1816,7 @@
             jax.ShapeDtypeStruct((m, share, D), BF),
             jax.ShapeDtypeStruct((1, D), F32),
             jax.ShapeDtypeStruct((n, block, D), BF),
+            jax.ShapeDtypeStruct((share, D), BF),
         ]
         + [shape for shape, _ in made],
         [
@@ -1821,7 +1837,8 @@
             held_of(parts[1]),
             held_of(parts[1]),
         ]
-        + dma_sems(2 * max(n, m)) * 13,
+        + [pltpu.VMEM((2, m, share, D), BF), pltpu.VMEM((share, D), F32)]
+        + dma_sems(2 * max(n, m)) * 15,
         [
             probs,
             qkv,
@@ -1835,9 +1852,11 @@
             sums[0][None],
             sums[1][None],
             parts[1],
+            fed,
+            hidden,
         ],
     )
-    return list(results[:3]) + [shaper(a) for (_, shaper), a in zip(made, results[3:])]
+    return list(results[:4]) + [shaper(a) for (_, shaper), a in zip(made, results[4:])]
 
 
 def local(
@@ -1929,7 +1948,7 @@
         ],
     )
     mixer_root, lift_root, project_root, output_root, upper_root, lower_root = every_root
-    grad_words, gain_one, grad_vectors, sum_upper, sum_lower, sum_project, sum_output = stream_grads(
+    grad_words, gain_one, grad_vectors, block_own, sum_upper, sum_lower, sum_project, sum_output = stream_grads(
         probs,
         qkv,
         grad_mixed.reshape(words_dev, -1),
@@ -1941,9 +1960,9 @@
         own_row,
         (part_upper, part_lower),
         grad_output_mat,
-    )
-    grad_vectors, feed_part = lax.optimization_barrier((grad_vectors, feed_part))
-    feed_total = lax.psum(feed_part, "mp")
+        feed_part.reshape(part_count, words_dev // part_count, D),
+        hidden,
+    )
     char_embeds_gradient, char_grads, grad_char_gain, grad_stream = char_backward(
         character_embeddings, block_home, char_count, char_gain, char_whole, kept, pooled, msum,
         grad_vectors.reshape(-1, share_rows, D),
@@ -1951,8 +1970,9 @@
         peer_count,
     )
     word_sums = (sum_project, sum_output, sum_upper, sum_lower)
-    char_sums, small_sums = sum_char_grads(
-        char_grads, (grad_char_gain, gain_one, gain_two), word_sums, word_output.shape[1] * peer_count
+    char_sums, small_sums, block_out = sum_char_grads(
+        char_grads, (grad_char_gain, gain_one, gain_two), word_sums, word_output.shape[1] * peer_count,
+        block_own,
     )
     parameter_count = (
         sum(
@@ -1972,8 +1992,7 @@
         char_gain,
         word_gains,
         word_sums,
-        hidden,
-        feed_total,
+        block_out,
         [
             tuple(flat(a) for a in group[:4]) + (group[4],)
             for group in (

time: 312 us -> 304 us (0.974)
  between operations: 14.8 us -> 1.4 us
  Pallas kernels: 280 us -> 288 us
    pallas_call x3, Pallas kernels: 160 us -> 172 us  [call_remote(): pl.pallas_call(kernel, out_shape=outs, in_specs=[vmem] * len(inputs), out...]
    pallas_call x2, Pallas kernels: 39.6 us -> 30.3 us  [char_call(): pl.pallas_call(kernel, in_specs=[smem] * len(scalars) + [hbm if t in in_h...]
    pallas_call x1, Pallas kernels: 42 us -> 46.9 us  [sum_char_grads(): pl.pallas_call(kernel, out_shape=[jax.ShapeDtypeStruct((n * rows, cols) i...]
    unnamed x74 -> x76, local copies, waits for them, and re-layouts: 10.2 us -> 9.21 us
  transfers between devices with their start and end apart: 1 -> 0, of which waited for: 0 -> 0; matrix products, arithmetic and copies ran while one was open for 0% -> 0% of each run, Pallas kernels for 21% -> 0%
where the time goes in v4:
time: 304 us; the launch traced here: 300 us
  Pallas kernels  288 us (95%)
  local copies, waits for them, and re-layouts  9.22 us (3%)
    pallas_call x3, Pallas kernels, call_remote(): pl.pallas_call(kernel, out_shape=outs, in_specs=[vmem] * len(inputs), out...  172 us
    pallas_call x1, Pallas kernels, sum_char_grads(): pl.pallas_call(kernel, out_shape=[jax.ShapeDtypeStruct((n * rows, cols) i...  46.9 us
    pallas_call x2, Pallas kernels, char_call(): pl.pallas_call(kernel, in_specs=[smem] * len(scalars) + [hbm if t in in_h...  30.3 us
    pallas_call x1, Pallas kernels, gather_char(): pl.pallas_call(kernel, out_shape=[shape, jax.ShapeDtypeStruct((m, rows, D...  16.5 us
    pallas_call x1, Pallas kernels, shampoo(): pl.pallas_call(functools.partial(shampoo_kernel, threshold), in_specs=[sm...  12.2 us
    pallas_call x1, Pallas kernels, word_forward(): pl.pallas_call(functools.partial(word_forward_kernel, width), grid=(lengt...  10 us
    unnamed x76, local copies, waits for them, and re-layouts  9.21 us

profile of v4, /device:TPU:0, one launch (start us, length us, event | category | flops | bytes accessed | tf_op | source)
XLA Modules:
  0.0 299.5 jit_solution(13678674841804128813)
XLA Ops:
  0.7 16.5 %gather_char.1 = (bf16[256,1536]{1,0:T(8,128)(2,1)}, bf16[4,16,512]{2,1,0:T(8,128)(2,1)}, bf16[24,128]{1,0:T(8,128)(2,1)}, s32[16,128]{1,0:T(8,128)}, s32[8,1,96]{2,1,0:T(1,128)}) custom-call(f32[4,32,256]{2,1,0:T(8,128)} %refs_0_.3, f32[1,32,512]{2,1,0:T(8,128)} %refs_5_.3, f32[1,16,512]{2,1,0:T(8,128)} %refs_15_.1, s32[1,20]{1,0:T(1,128)} %bitcast.58, ...), custom_call_target="tpu_custom_call" | custom-call | tf_op jit(solution)/shard_map/gather_char/pallas_call | solution.py:1431
  17.2 0.0 copy-start.17
  17.2 0.0 copy-start.37
  17.3 0.0 copy-start.18
  17.3 0.0 copy-start.19
  17.3 12.5 %char_forward.1 = (bf16[24,32,512]{2,1,0:T(8,128)(2,1)}, bf16[20,512,1536]{2,1,0:T(8,128)(2,1)}, bf16[640,256]{1,0:T(8,128)(2,1)}, f32[640,256]{1,0:T(8,128)}) custom-call(s32[20]{0:T(128)} %home.3, s32[20,32]{1,0:T(8,128)} %counts_in.3, bf16[20,512,256]{2,1,0:T(8,128)(2,1)} %bitcast.63, s32[20,32]{1,0:T(8,128)} %counts_in.3, f32[1,256]{1,0:T(1,128)} %bitcast.55, ...), custom_call_target="tpu_custom_call" | custom-call | flops 10737418240 | bytes 62914560 | tf_op jit(solution)/shard_map/char_forward/pallas_call | solution.py:281
  29.9 1.2 copy-done.7
  31.1 45.9 %send_vectors.1 = (bf16[4,320,512]{2,1,0:T(8,128)(2,1)S(1)}, bf16[512,384]{1,0:T(8,128)(2,1)S(1)}, bf16[512,512]{1,0:T(8,128)(2,1)S(1)}, bf16[512,512]{1,0:T(8,128)(2,1)S(1)}, bf16[4,128,512]{2,1,0:T(8,128)(2,1)S(1)}) custom-call(bf16[8,96,512]{2,1,0:T(8,128)(2,1)S(1)} %bitcast.45, bf16[24,128]{1,0:T(8,128)(2,1)S(1)} %copy-done.29, ...), custom_call_target="tpu_custom_call" | custom-call | tf_op jit(solution)/shard_map/send_vectors/pallas_call | solution.py:1334
  77.1 10.0 %word_forward.1 = (f32[1024,512]{1,0:T(8,128)S(1)}, bf16[1024,512]{1,0:T(8,128)(2,1)S(1)}, bf16[1024,384]{1,0:T(8,128)(2,1)S(1)}, bf16[2,1024,1024]{2,1,0:T(8,128)(2,1)S(1)}, bf16[1024,128]{1,0:T(8,128)(2,1)S(1)}) custom-call(bf16[4,320,512]{2,1,0:T(8,128)(2,1)S(1)} %get-tuple-element.127.vec_ref, s32[16,128]{1,0:T(8,128)S(1)} %copy-done.28, ...), custom_call_target="tpu_custom_call" | custom-call | tf_op jit(solution)/shard_map/word_forward/pallas_call | solution.py:1088
  87.2 54.1 %feed_step.1 = (f32[1024,512]{1,0:T(8,128)S(1)}, bf16[1024,512]{1,0:T(8,128)(2,1)S(1)}, f32[256,512]{1,0:T(8,128)S(1)}, bf16[4,256,128]{2,1,0:T(8,128)(2,1)S(1)}...) custom-call(bf16[1024,128]{1,0:T(8,128)(2,1)S(1)} %get-tuple-element, ...), custom_call_target="tpu_custom_call" | custom-call | tf_op jit(solution)/shard_map/feed_step/pallas_call | solution.py:1334
  141.3 0.8 copy-done.14
  142.1 0.8 copy-done.15
  142.9 0.8 copy-done.16
  143.8 72.4 %stream_grads.1 = (bf16[4,256,512]{2,1,0:T(8,128)(2,1)S(1)}, f32[1,512]{1,0:T(1,128)S(1)}, bf16[8,96,512]{2,1,0:T(8,128)(2,1)S(1)}, bf16[256,512]{1,0:T(8,128)(2...) custom-call(bf16[2,1024,1024]{2,1,0:T(8,128)(2,1)S(1)} %get-tuple-el, ...), custom_call_target="tpu_custom_call" | custom-call | tf_op jit(solution)/shard_map/stream_grads/pallas_call | solution.py:1334
  216.2 1.0 copy-done.33
  217.1 0.9 copy-done.34
  218.1 17.8 %char_backward.1 = (bf16[20,512,256]{2,1,0:T(8,128)(2,1)}, bf16[256,1536]{1,0:T(8,128)(2,1)}, f32[1,256]{1,0:T(1,128)S(1)}, bf16[4,256,512]{2,1,0:T(8,128)(2,1)}) custom-call(s32[20]{0:T(128)S(1)} %copy-done.32, s32[20,32]{1,0:T(8,128)S(1)} %copy-done.35, bf16[20,512,256]{2,1,0:T(8,128)(2,1)} %bitcast.64, s32[20,32]{1,0:T(8,128)S(1)} %copy-done.35, ...), custom_call_target="tpu_custom_call" | custom-call | flops 18790481920 | bytes 62914560 | tf_op jit(solution)/shard_map/char_backward/pallas_call | solution.py:281
  236.0 1.1 copy-done.8
  237.1 46.9 %sum_char_grads.1 = (bf16[256,1536]{1,0:T(8,128)(2,1)S(1)}, f32[8,512]{1,0:T(8,128)S(1)}, bf16[4,256,512]{2,1,0:T(8,128)(2,1)S(1)}) custom-call(bf16[4,2,32,1536]{3,2,1,0:T(8,128)(2,1)S(1)} %bitcast.46, f32[1,256]{1,0:T(1,128)S(1)} %get-tuple-element.151.gain_char, f32[1,512]{1,0:T(1,128)S(1)} %get-tuple-element.152.gain_one, ...), custom_call_target="tpu_custom_call" | custom-call | tf_op jit(solution)/shard_map/sum_char_grads/pallas_call | solution.py:991
  284.0 1.0 copy-done.6
  285.0 0.9 copy-done.9
  285.9 0.6 copy-done.26
  286.5 0.7 pad_add_fusion.position
  287.1 12.2 %shampoo.1 = (f32[1,1]{1,0:T(1,128)}, f32[1,256]{1,0:T(1,128)}, f32[2,512]{1,0:T(2,128)}, f32[1,256]{1,0:T(1,128)}, f32[2,512]{1,0:T(2,128)}, /*index=5*/bf16[4,...) custom-call(s32[2]{0:T(128)} %pad_add_fusion.position, ...), custom_call_target="tpu_custom_call" | custom-call | tf_op jit(solution)/shard_map/shampoo/pallas_call | solution.py:1282
  (63 shorter events, 0.2 us)
Async XLA Ops:
  17.2 12.7 %copy-start.10 = (f32[1,64,512]{2,1,0:T(8,128)S(1)}, f32[1,64,512]{2,1,0:T(8,128)}, u32[]{:S(2)}) copy-start(f32[1,64,512]{2,1,0:T(8,128)} %refs_20_.1) | copy-start | bytes 393220
  17.2 59.8 %copy-start.37 = (f32[2,512]{1,0:T(2,128)S(1)}, f32[2,512]{1,0:T(2,128)}, u32[]{:S(2)}) copy-start(f32[2,512]{1,0:T(2,128)} %gains_ref.1) | copy-start | bytes 12292
  17.2 59.8 %copy-start.5 = (bf16[1,1024,512]{2,1,0:T(8,128)(2,1)S(1)}, bf16[1,1024,512]{2,1,0:T(8,128)(2,1)}, u32[]{:S(2)}) copy-start(bf16[1,1024,512]{2,1,0:T(8,128)(2,1)} %param.39) | copy-start | bytes 3145732
  17.3 59.8 %copy-start.27 = (s32[1,1024]{1,0:T(1,128)S(1)}, s32[1,1024]{1,0:T(1,128)}, u32[]{:S(2)}) copy-start(s32[1,1024]{1,0:T(1,128)} %doc_row_ref.1) | copy-start | bytes 12292
  17.3 59.8 %copy-start.28 = (s32[16,128]{1,0:T(8,128)S(1)}, s32[16,128]{1,0:T(8,128)}, u32[]{:S(2)}) copy-start(s32[16,128]{1,0:T(8,128)} %get-tuple-element.128.place_ref) | copy-start | bytes 24580
  17.3 69.9 %copy-start.18 = (f32[4,32,256]{2,1,0:T(8,128)S(1)}, f32[4,32,256]{2,1,0:T(8,128)}, u32[]{:S(2)}) copy-start(f32[4,32,256]{2,1,0:T(8,128)} %refs_0_.2) | copy-start | bytes 393220
  17.3 69.9 %copy-start.19 = (f32[1,64,512]{2,1,0:T(8,128)S(1)}, f32[1,64,512]{2,1,0:T(8,128)}, u32[]{:S(2)}) copy-start(f32[1,64,512]{2,1,0:T(8,128)} %refs_1_.4) | copy-start | bytes 393220
  17.3 69.9 %copy-start.20 = (f32[1,64,512]{2,1,0:T(8,128)S(1)}, f32[1,64,512]{2,1,0:T(8,128)}, u32[]{:S(2)}) copy-start(f32[1,64,512]{2,1,0:T(8,128)} %refs_3_.2) | copy-start | bytes 393220
  17.3 69.9 %copy-start.21 = (f32[1,64,512]{2,1,0:T(8,128)S(1)}, f32[1,64,512]{2,1,0:T(8,128)}, u32[]{:S(2)}) copy-start(f32[1,64,512]{2,1,0:T(8,128)} %refs_4_.1) | copy-start | bytes 393220
  17.3 69.9 %copy-start.22 = (f32[1,64,512]{2,1,0:T(8,128)S(1)}, f32[1,64,512]{2,1,0:T(8,128)}, u32[]{:S(2)}) copy-start(f32[1,64,512]{2,1,0:T(8,128)} %refs_5_.2) | copy-start | bytes 393220
  17.3 69.9 %copy-start.25 = (f32[3,1,16,128]{3,2,1,0:T(8,128)S(1)}, f32[3,1,16,128]{3,2,1,0:T(8,128)}, u32[]{:S(2)}) copy-start(f32[3,1,16,128]{3,2,1,0:T(8,128)} %param.62) | copy-start | bytes 73732
  29.8 57.4 %copy-start.4 = (bf16[1,1024,512]{2,1,0:T(8,128)(2,1)S(1)}, bf16[1,1024,512]{2,1,0:T(8,128)(2,1)}, u32[]{:S(2)}) copy-start(bf16[1,1024,512]{2,1,0:T(8,128)(2,1)} %param.41) | copy-start | bytes 3145732
  77.1 66.6 %copy-start.30 = (s32[8,1,96]{2,1,0:T(1,128)S(1)}, s32[8,1,96]{2,1,0:T(1,128)}, u32[]{:S(2)}) copy-start(s32[8,1,96]{2,1,0:T(1,128)} %get-tuple-element.140.row_ref) | copy-start | bytes 9220
  143.7 72.4 %copy-start.12 = (bf16[256,1024]{1,0:T(8,128)(2,1)}, bf16[256,1024]{1,0:T(8,128)(2,1)S(1)}, u32[]{:S(2)}) copy-start(bf16[256,1024]{1,0:T(8,128)(2,1)S(1)} %get-tuple-element.162.refs_4_) | copy-start | bytes 1572868
  143.7 72.4 %copy-start.13 = (bf16[512,512]{1,0:T(8,128)(2,1)}, bf16[512,512]{1,0:T(8,128)(2,1)S(1)}, u32[]{:S(2)}) copy-start(bf16[512,512]{1,0:T(8,128)(2,1)S(1)} %get-tuple-element.163.refs_9_) | copy-start | bytes 1572868
  143.7 72.5 %copy-start.23 = (bf16[128,384]{1,0:T(8,128)(2,1)}, bf16[128,384]{1,0:T(8,128)(2,1)S(1)}, u32[]{:S(2)}) copy-start(bf16[128,384]{1,0:T(8,128)(2,1)S(1)} %get-tuple-element.164.refs_14_) | copy-start | bytes 294916
  143.7 74.3 %copy-start.31 = (f32[256]{0:T(256)S(1)}, f32[256]{0:T(256)}, u32[]{:S(2)}) copy-start(f32[256]{0:T(256)} %param.46) | copy-start | bytes 3076
  143.7 74.3 %copy-start.32 = (s32[20]{0:T(128)S(1)}, s32[20]{0:T(128)}, u32[]{:S(2)}) copy-start(s32[20]{0:T(128)} %home.3) | copy-start | bytes 244
  143.7 74.3 %copy-start.35 = (s32[20,32]{1,0:T(8,128)S(1)}, s32[20,32]{1,0:T(8,128)}, u32[]{:S(2)}) copy-start(s32[20,32]{1,0:T(8,128)} %counts_in.3) | copy-start | bytes 7684
  143.8 74.3 %copy-start.36 = (bf16[640,256]{1,0:T(8,128)(2,1)S(1)}, bf16[640,256]{1,0:T(8,128)(2,1)}, u32[]{:S(2)}) copy-start(bf16[640,256]{1,0:T(8,128)(2,1)} %get-tuple-element.147.pooled_ref) | copy-start | bytes 983044
  218.0 17.9 %copy-start = (bf16[512,512]{1,0:T(8,128)(2,1)}, bf16[512,512]{1,0:T(8,128)(2,1)S(1)}, u32[]{:S(2)}) copy-start(bf16[512,512]{1,0:T(8,128)(2,1)S(1)} %get-tuple-element.157.refs_2_.upper) | copy-start | bytes 1572868
  218.0 17.9 %copy-start.1 = (bf16[512,512]{1,0:T(8,128)(2,1)}, bf16[512,512]{1,0:T(8,128)(2,1)S(1)}, u32[]{:S(2)}) copy-start(bf16[512,512]{1,0:T(8,128)(2,1)S(1)} %get-tuple-element.158.refs_3_.lower) | copy-start | bytes 1572868
  218.0 17.9 %copy-start.2 = (bf16[512,512]{1,0:T(8,128)(2,1)}, bf16[512,512]{1,0:T(8,128)(2,1)S(1)}, u32[]{:S(2)}) copy-start(bf16[512,512]{1,0:T(8,128)(2,1)S(1)} %get-tuple-element.156.refs_1_.output) | copy-start | bytes 1572868
  218.1 17.9 %copy-start.3 = (bf16[512,384]{1,0:T(8,128)(2,1)}, bf16[512,384]{1,0:T(8,128)(2,1)S(1)}, u32[]{:S(2)}) copy-start(bf16[512,384]{1,0:T(8,128)(2,1)S(1)} %get-tuple-element.155.refs_0_.project) | copy-start | bytes 1179652
  (14 other events, 59.8 us)
